TPU v7x, 128 devices: a whole 4x4x4 slice. The times are simulated.
128 devices in a mesh: seq: 8 (over x_lo, z), ch: 16 (over y, x_hi, core).
Axes of the slice: x: 4 (x_hi: 2, x_lo: 2; x = x_hi * 2 + x_lo), y: 4, z: 4, core: 2. Of those that a mesh axis runs over, the one named last changes fastest.
Arguments:
- query_stream: bfloat16 [256, 131072], P(None, ('seq', 'ch')), may hold values from -6 to 6
- key_stream: bfloat16 [256, 131072], P(None, ('seq', 'ch')), may hold values from -6 to 6
- value_stream: bfloat16 [256, 131072], P(None, ('seq', 'ch')), may hold values from -6 to 6
- short_taps: float32 [3, 3, 256], replicated, may hold values from -3.5 to 3.5
- long_filter: bfloat16 [16, 8, 2, 131072], P('ch', 'seq'), may hold values from -0.015625 to 0.015625
- skip_gain: float32 [256], replicated, may hold values from -4 to 4
Outputs:
- gated_output: bfloat16 [256, 131072], P(None, ('seq', 'ch'))
All inputs are finite; a program needn't handle non-finite values.
Results may differ from a plain program's by a relative error of at most 0.0085.
Values may be sent and summed in bfloat16 or wider, within the bound.
No kernel may reach another device: no remote copies, remote signals or barrier semaphores. Data moves between devices by JAX's collectives and lax.ppermute only.
A program may use at most 64 MiB of HBM per device.

v0:
```python
import functools
import math

import jax
import jax.numpy as jnp
import ml_dtypes
import numpy as np
from jax import lax
from jax.experimental import pallas as pl
from jax.experimental.pallas import tpu as pltpu
from jax.sharding import PartitionSpec as P

F32 = jnp.float32
BF16 = jnp.bfloat16
LANES = 128
OUTER = 1024
LENGTH = OUTER * LANES
CHANNELS = 256
TOKENS = 1024
TILES = TOKENS // LANES
SEQ = 8
CH = 16
ROWS = 32
CHUNK = 256
AXES = ("seq", "ch")
VMEM = pl.BlockSpec(memory_space=pltpu.VMEM)


def tables():
    step = 2.0 * math.pi
    a = np.arange(OUTER)[None, :]
    k1 = np.arange(OUTER)[:, None]
    outer_phase = ((4 * a + 1) * (4 * k1 + 1) % (16 * OUTER)) * (step / (16 * OUTER))
    outer = np.stack([np.cos(outer_phase), -np.sin(outer_phase)]).astype(ml_dtypes.bfloat16)
    lane = np.arange(LANES)[None, :]
    turn_phase = (k1 + 0.25) * (lane / LENGTH - 1.0 / (4 * OUTER)) * step
    turn = np.stack([np.cos(turn_phase), -np.sin(turn_phase)]).astype(np.float32)
    inner_phase = (lane * lane.T % LANES) * (step / LANES)
    cos, sin = np.cos(inner_phase), np.sin(inner_phase)
    forward = np.block([[cos, -sin], [sin, cos]]).astype(ml_dtypes.bfloat16)
    inverse = np.block([[cos, sin], [-sin, cos]]).astype(ml_dtypes.bfloat16)
    return outer, turn, forward, inverse


def dot(left, right):
    return jnp.dot(left, right, preferred_element_type=F32)


def call(body, out_shape, scratch, flops, nbytes, name, **kwargs):
    return pl.pallas_call(
        body,
        out_shape=out_shape,
        scratch_shapes=scratch,
        compiler_params=pltpu.CompilerParams(vmem_limit_bytes=48 * 1024 * 1024),
        cost_estimate=pl.CostEstimate(flops=flops, bytes_accessed=nbytes, transcendentals=0),
        name=name,
        **kwargs,
    )


def tails_body(q_ref, k_ref, v_ref, out_ref):
    row = lax.broadcasted_iota(jnp.int32, (16, LANES), 0)
    col = lax.broadcasted_iota(jnp.int32, (16, LANES), 1)
    total = jnp.zeros((16, CHANNELS), F32)
    for i, ref in enumerate((q_ref, k_ref, v_ref)):
        pick = (row - 2 * i == col - (LANES - 2)) & (col >= LANES - 2)
        total += lax.dot_general(
            pick.astype(BF16), ref[...], (((1,), (1,)), ((), ())), preferred_element_type=F32
        )
    out_ref[...] = total.astype(BF16)


def tails(q, k, v):
    last = pl.BlockSpec((CHANNELS, LANES), lambda i: (0, TILES - 1))
    return call(
        tails_body,
        jax.ShapeDtypeStruct((16, CHANNELS), BF16),
        [],
        4 * 10**6,
        200 * 1024,
        "tails",
        grid=(1,),
        in_specs=[last] * 3,
        out_specs=pl.BlockSpec((16, CHANNELS), lambda i: (0, 0)),
    )(q, k, v)


def rim_columns(rim):
    row = lax.broadcasted_iota(jnp.int32, (16, LANES), 0)
    col = lax.broadcasted_iota(jnp.int32, (16, LANES), 1)
    eye = (row == col).astype(BF16)
    return lax.dot_general(rim, eye, (((0,), (0,)), ((), ())), preferred_element_type=F32)


def short_conv(x, cols, rim, stream):
    lane = lax.broadcasted_iota(jnp.int32, x.shape, 1)
    older = rim[:, 2 * stream : 2 * stream + 1]
    newer = rim[:, 2 * stream + 1 : 2 * stream + 2]
    back1 = jnp.where(lane == 0, newer, pltpu.roll(x, 1, 1))
    back2 = jnp.where(lane == 0, older, jnp.where(lane == 1, newer, pltpu.roll(x, 2, 1)))
    tap = [cols[:, 3 * stream + i : 3 * stream + i + 1] for i in range(3)]
    return tap[0] * x + tap[1] * back1 + tap[2] * back2


def gate_body(k_ref, v_ref, rim_ref, cols_ref, gated_ref, out_ref, rim_cols, rows):
    rim_cols[...] = rim_columns(rim_ref[...])
    groups = ROWS // (2 * SEQ)
    for step in range(CHANNELS // ROWS):
        at = slice(step * ROWS, (step + 1) * ROWS)
        cols = cols_ref[at, :]
        rim = rim_cols[at, :]
        key = short_conv(k_ref[at, :].astype(F32), cols, rim, 1)
        value = short_conv(v_ref[at, :].astype(F32), cols, rim, 2)
        gated = (key * value).astype(BF16)
        gated_ref[at, :] = gated
        wide = gated.astype(F32)
        for c in range(TILES):
            rows[pl.ds(c, ROWS, stride=TILES), :] = wide[:, c * LANES : (c + 1) * LANES]
        message = rows[...].reshape(groups, SEQ, 2 * TILES, LANES).astype(BF16)
        for g in range(groups):
            out_ref[:, step * groups + g] = message[g]


def gate(k, v, rim, cols):
    return call(
        gate_body,
        (
            jax.ShapeDtypeStruct((CHANNELS, TOKENS), BF16),
            jax.ShapeDtypeStruct((SEQ, CH, 2 * TILES, LANES), BF16),
        ),
        [pltpu.VMEM((CHANNELS, LANES), F32), pltpu.VMEM((ROWS * TILES, LANES), F32)],
        10**7,
        2 * 1024 * 1024,
        "gate",
        in_specs=[VMEM] * 4,
        out_specs=(VMEM, VMEM),
    )(k, v, rim, cols)


def forward_chunk(at, signal, outer_ref, turn_ref, forward):
    section_real = dot(outer_ref[0, at, :], signal)
    section_imag = dot(outer_ref[1, at, :], signal)
    turn_real, turn_imag = turn_ref[0, at, :], turn_ref[1, at, :]
    spectra = []
    for j in range(2):
        half = slice(j * LANES, (j + 1) * LANES)
        real, imag = section_real[:, half], section_imag[:, half]
        turned = [real * turn_real - imag * turn_imag, imag * turn_real + real * turn_imag]
        spectra.append(dot(jnp.concatenate(turned, axis=1).astype(BF16), forward))
    return spectra


def filter_body(filt_ref, outer_ref, turn_ref, forward_ref, spec_ref):
    signal = jnp.concatenate([filt_ref[0], filt_ref[1]], axis=1)
    for step in range(OUTER // CHUNK):
        at = slice(step * CHUNK, (step + 1) * CHUNK)
        spectra = forward_chunk(at, signal, outer_ref, turn_ref, forward_ref[...])
        for j in range(2):
            spec_ref[j, at, :] = spectra[j] * (1.0 / LENGTH)


def filter_spectra(filt, outer, turn, forward):
    return call(
        filter_body,
        jax.ShapeDtypeStruct((2, OUTER, 2 * LANES), F32),
        [],
        14 * 10**8,
        8 * 1024 * 1024,
        "filter_spectra",
        in_specs=[VMEM] * 4,
        out_specs=VMEM,
    )(filt, outer, turn, forward)


def conv_body(
    arrived_ref, spec_ref, outer_ref, turn_ref, forward_ref, inverse_ref, out_ref, back_ref
):
    arrived = arrived_ref[...].astype(F32)
    halves = [arrived[:, j * TILES : (j + 1) * TILES, :].reshape(OUTER, LANES) for j in range(2)]
    signal = jnp.concatenate(halves, axis=1).astype(BF16)
    for step in range(OUTER // CHUNK):
        at = slice(step * CHUNK, (step + 1) * CHUNK)
        spectra = forward_chunk(at, signal, outer_ref, turn_ref, forward_ref[...])
        turn_real, turn_imag = turn_ref[0, at, :], turn_ref[1, at, :]
        for j in range(2):
            real, imag = spectra[j][:, :LANES], spectra[j][:, LANES:]
            filt_real, filt_imag = spec_ref[j, at, :LANES], spec_ref[j, at, LANES:]
            parts = [real * filt_real - imag * filt_imag, real * filt_imag + imag * filt_real]
            inner = dot(jnp.concatenate(parts, axis=1).astype(BF16), inverse_ref[...])
            real, imag = inner[:, :LANES], inner[:, LANES:]
            half = slice(j * LANES, (j + 1) * LANES)
            back_ref[0, at, half] = (real * turn_real + imag * turn_imag).astype(BF16)
            back_ref[1, at, half] = (imag * turn_real - real * turn_imag).astype(BF16)
    blocks = CHUNK // TILES
    for step in range(OUTER // CHUNK):
        at = slice(step * CHUNK, (step + 1) * CHUNK)
        result = dot(outer_ref[0, at, :], back_ref[0]) + dot(outer_ref[1, at, :], back_ref[1])
        halves = [
            result[:, j * LANES : (j + 1) * LANES].reshape(blocks, TILES, LANES) for j in range(2)
        ]
        out_ref[step * blocks : (step + 1) * blocks] = jnp.concatenate(halves, axis=1).astype(BF16)


def conv(arrived, spec, outer, turn, forward, inverse):
    return call(
        conv_body,
        jax.ShapeDtypeStruct((SEQ * CH, 2 * TILES, LANES), BF16),
        [pltpu.VMEM((2, OUTER, 2 * LANES), BF16)],
        28 * 10**8,
        8 * 1024 * 1024,
        "conv",
        in_specs=[VMEM] * 6,
        out_specs=VMEM,
    )(arrived, spec, outer, turn, forward, inverse)


def final_body(returned_ref, gated_ref, q_ref, rim_ref, cols_ref, out_ref, rim_cols, rows):
    rim_cols[...] = rim_columns(rim_ref[...])
    groups = ROWS // (2 * SEQ)
    per_group = ROWS * TILES // groups
    for step in range(CHANNELS // ROWS):
        at = slice(step * ROWS, (step + 1) * ROWS)
        cols = cols_ref[at, :]
        for g in range(groups):
            message = returned_ref[:, step * groups + g].astype(F32)
            rows[g * per_group : (g + 1) * per_group, :] = message.reshape(per_group, LANES)
        long_result = jnp.concatenate(
            [rows[pl.ds(c, ROWS, stride=TILES), :] for c in range(TILES)], axis=1
        )
        query = short_conv(q_ref[at, :].astype(F32), cols, rim_cols[at, :], 0)
        mixed = query * (long_result + cols[:, 9:10] * gated_ref[at, :].astype(F32))
        out_ref[at, :] = mixed.astype(BF16)


def final(returned, gated, q, rim, cols):
    return call(
        final_body,
        jax.ShapeDtypeStruct((CHANNELS, TOKENS), BF16),
        [pltpu.VMEM((CHANNELS, LANES), F32), pltpu.VMEM((ROWS * TILES, LANES), F32)],
        10**7,
        2 * 1024 * 1024,
        "final",
        in_specs=[VMEM] * 5,
        out_specs=VMEM,
    )(returned, gated, q, rim, cols)


def exchange(messages):
    flat = messages.reshape(SEQ * CH, 2 * TILES, LANES)
    return lax.all_to_all(flat, AXES, split_axis=0, concat_axis=0, tiled=True)


def shards(consts, query_stream, key_stream, value_stream, short_taps, long_filter, skip_gain):
    outer, turn, forward, inverse = (jnp.asarray(c) for c in consts)
    count = lax.axis_size("seq") * lax.axis_size("ch")
    ends = tails(query_stream, key_stream, value_stream)
    rim = lax.ppermute(ends, AXES, [(i, i + 1) for i in range(count - 1)])
    cols = jnp.concatenate([short_taps.reshape(9, CHANNELS), skip_gain[None]]).T
    gated, messages = gate(key_stream, value_stream, rim, cols)
    arrived = exchange(messages)
    spec = filter_spectra(long_filter.reshape(2, OUTER, LANES), outer, turn, forward)
    results = conv(arrived, spec, outer, turn, forward, inverse)
    returned = exchange(results).reshape(SEQ, CH, 2 * TILES, LANES)
    return final(returned, gated, query_stream, rim, cols)


def solution(mesh):
    tokens = P(None, AXES)
    placed = (tokens, tokens, tokens, P(), P("ch", "seq", None, None), P())
    return jax.shard_map(
        functools.partial(shards, tables()),
        mesh=mesh,
        in_specs=placed,
        out_specs=tokens,
        check_vma=False,
    )
```

profile of v0, /device:TPU:1, one launch (start us, length us, event | category | flops | bytes accessed | tf_op | source)
XLA Modules:
  0.0 66.3 jit_solution(5773179833627547760)
XLA Ops:
  0.0 1.0 %copy-done = bf16[256,1024]{1,0:T(8,128)(2,1)S(1)} copy-done((bf16[256,1024]{1,0:T(8,128)(2,1)S(1)}, bf16[256,1024]{1,0:T(8,128)(2,1)}, u32[]{:S(2)}) %copy-start) | copy-done | bytes 524312
  1.0 1.0 %copy-done.2 = bf16[256,1024]{1,0:T(8,128)(2,1)S(1)} copy-done((bf16[256,1024]{1,0:T(8,128)(2,1)S(1)}, bf16[256,1024]{1,0:T(8,128)(2,1)}, u32[]{:S(2)}) %copy-start.2) | copy-done | bytes 524312
  2.1 1.0 %copy-done.4 = bf16[256,1024]{1,0:T(8,128)(2,1)S(1)} copy-done((bf16[256,1024]{1,0:T(8,128)(2,1)S(1)}, bf16[256,1024]{1,0:T(8,128)(2,1)}, u32[]{:S(2)}) %copy-start.4) | copy-done | bytes 524312
  3.1 0.2 tails.1
  3.3 6.1 %collective-permute-start = (bf16[16,256]{1,0:T(8,128)(2,1)S(1)}, bf16[16,256]{1,0:T(8,128)(2,1)S(1)}, u32[]{:S(2)}, u32[]{:S(2)}) collective-permute-start(bf16[16,256]{1,0:T(8,128)(2,1)S(1)} %tails.1), channel_id=1, source_target_pairs={{0,1},{1,2},{2,3},{3,4},{4,5},{5,6},{6,7},{7,8},{8,9},{9,10},{10,1... | collective-permute-start | bytes 24584 | tf_op jit(solution)/shard_map/ppermute | solution.py:257
  9.4 0.7 %reshape.12 = f32[9,256]{1,0:T(8,128)S(1)} reshape(f32[3,3,256]{2,1,0:T(4,128)} %param.13) | data formatting | bytes 18432 | tf_op jit(solution)/shard_map/reshape | solution.py:258
  10.1 0.7 %pad_maximum_fusion = f32[10,256]{1,0:T(8,128)S(1)} fusion(f32[1,256]{1,0:T(1,128)} %bitcast.14, f32[9,256]{1,0:T(8,128)S(1)} %reshape.12), kind=kLoop, calls=%fused_computation.1 | loop fusion | flops 2560 | bytes 20480 | tf_op jit(solution)/shard_map/concatenate | solution.py:258
  10.8 0.1 copy.14
  10.9 0.0 collective-permute-done.rim_ref
  10.9 0.0 copy-start.1
  10.9 1.0 %copy-done.1 = bf16[256,1024]{1,0:T(8,128)(2,1)S(1)} copy-done((bf16[256,1024]{1,0:T(8,128)(2,1)S(1)}, bf16[256,1024]{1,0:T(8,128)(2,1)}, u32[]{:S(2)}) %copy-start.1) | copy-done | bytes 524312
  12.0 1.0 %copy-done.3 = bf16[256,1024]{1,0:T(8,128)(2,1)S(1)} copy-done((bf16[256,1024]{1,0:T(8,128)(2,1)S(1)}, bf16[256,1024]{1,0:T(8,128)(2,1)}, u32[]{:S(2)}) %copy-start.3) | copy-done | bytes 524312
  13.0 2.4 %gate.1 = (bf16[256,1024]{1,0:T(8,128)(2,1)S(1)}, bf16[8,16,16,128]{3,2,1,0:T(8,128)(2,1)}) custom-call(bf16[256,1024]{1,0:T(8,128)(2,1)S(1)} %copy-done.1, bf16[256,1024]{1,0:T(8,128)(2,1)S(1)} %copy-done.3, bf16[16,256]{1,0:T(8,128)(2,1)S(1)} %collective-permute-done.rim_ref, f32[256,10]{1,0:T(8,128)S(1)} %bitcast.11), custom_call_target="tpu_custom_call" | custom-call | flops 10000000 | bytes 2097152 | tf_op jit(solution)/shard_map/gate/pallas_call | solution.py:125
  15.4 10.8 %all-to-all-start = ((bf16[128,16,128]{2,1,0:T(8,128)(2,1)}), bf16[128,16,128]{2,1,0:T(8,128)(2,1)}, u32[]{:S(2)}, u32[]{:S(2)}) async-start(bf16[128,16,128]{2,1,0:T(8,128)(2,1)} %bitcast.2), calls=%async_computation | async-start | bytes 1048576 | tf_op jit(solution)/shard_map/all_to_all | solution.py:250
  26.3 0.1 copy.17
  26.4 0.0 copy-start.6
  26.4 1.2 %copy-done.6 = f32[2,1024,128]{2,1,0:T(8,128)S(1)} copy-done((f32[2,1024,128]{2,1,0:T(8,128)S(1)}, f32[2,1024,128]{2,1,0:T(8,128)}, u32[]{:S(2)}) %copy-start.6) | copy-done | bytes 1048600
  27.6 4.1 %filter_spectra.1.spec_ref = f32[2,1024,256]{2,1,0:T(8,128)S(1)} custom-call(bf16[2,1024,128]{2,1,0:T(8,128)(2,1)S(1)} %bitcast.10, bf16[2,1024,1024]{2,1,0:T(8,128)(2,1)} %constant.8.clone.outer_ref, f32[2,1024,128]{2,1,0:T(8,128)S(1)} %copy-done.6, bf16[256,256]{1,0:T(8,128)(2,1)S(1)} %copy-done.8), custom_call_target="tpu_custom_call" | custom-call | flops 1400000000 | bytes 8388608 | tf_op jit(solution)/shard_map/filter_spectra/pallas_call | solution.py:163
  31.7 0.0 copy-start.5
  31.7 8.1 %all-to-all-done.arrived_ref = bf16[128,16,128]{2,1,0:T(8,128)(2,1)} async-done(((bf16[128,16,128]{2,1,0:T(8,128)(2,1)}), bf16[128,16,128]{2,1,0:T(8,128)(2,1)}, u32[]{:S(2)}, u32[]{:S(2)}) %all-to-all-start) | async-done | bytes 524320 | tf_op jit(solution)/shard_map/all_to_all | solution.py:250
  39.8 1.2 %copy-done.7 = f32[2,1024,128]{2,1,0:T(8,128)S(1)} copy-done((f32[2,1024,128]{2,1,0:T(8,128)S(1)}, f32[2,1024,128]{2,1,0:T(8,128)}, u32[]{:S(2)}) %copy-start.7) | copy-done | bytes 1048600
  41.0 5.9 %conv.1 = bf16[128,16,128]{2,1,0:T(8,128)(2,1)S(1)} custom-call(bf16[128,16,128]{2,1,0:T(8,128)(2,1)} %all-to-all-done.arrived_ref, f32[2,1024,256]{2,1,0:T(8,128)S(1)} %filter_spectra.1.spec_ref, bf16[2,1024,1024]{2,1,0:T(8,128)(2,1)} %constant.8.clone.outer_ref, f32[2,1024,128]{2,1,0:T(8,128)S(1)} %copy-done.7, bf16[256,256]{1,0:T(8,128)(2,1)S(1)} %copy-done.8, ...), custom_call_target="tpu_custom_call" | custom-call | flops 2800000000 | bytes 8388608 | tf_op jit(solution)/shard_map/conv/pallas_call | solution.py:205
  46.9 17.6 %all_to_all.10 = bf16[128,16,128]{2,1,0:T(8,128)(2,1)S(1)} all-to-all(bf16[128,16,128]{2,1,0:T(8,128)(2,1)S(1)} %conv.1), channel_id=1, replica_groups=mesh['seq'=8,'ch'=16] {'seq','ch'}, dimensions={0} | all-to-all | bytes 1048576 | tf_op jit(solution)/shard_map/all_to_all | solution.py:250
  64.5 1.8 %final.1 = bf16[256,1024]{1,0:T(8,128)(2,1)} custom-call(bf16[8,16,16,128]{3,2,1,0:T(8,128)(2,1)S(1)} %bitcast.9, bf16[256,1024]{1,0:T(8,128)(2,1)S(1)} %get-tuple-element.8.gated_ref, bf16[256,1024]{1,0:T(8,128)(2,1)S(1)} %copy-done.5, bf16[16,256]{1,0:T(8,128)(2,1)S(1)} %collective-permute-done.rim_ref, f32[256,10]{1,0:T(8,128)S(1)} %bitcast.12), custom_call_target="tpu_custom_call" | custom-call | flops 10000000 | bytes 2097152 | tf_op jit(solution)/shard_map/final/pallas_call | solution.py:236
  (12 shorter events, 0.0 us)
Async XLA Ops:
  0.0 1.0 %copy-start = (bf16[256,1024]{1,0:T(8,128)(2,1)S(1)}, bf16[256,1024]{1,0:T(8,128)(2,1)}, u32[]{:S(2)}) copy-start(bf16[256,1024]{1,0:T(8,128)(2,1)} %k_ref.3) | copy-start | bytes 1572868
  1.0 1.0 %copy-start.2 = (bf16[256,1024]{1,0:T(8,128)(2,1)S(1)}, bf16[256,1024]{1,0:T(8,128)(2,1)}, u32[]{:S(2)}) copy-start(bf16[256,1024]{1,0:T(8,128)(2,1)} %v_ref.3) | copy-start | bytes 1572868
  2.1 1.0 %copy-start.4 = (bf16[256,1024]{1,0:T(8,128)(2,1)S(1)}, bf16[256,1024]{1,0:T(8,128)(2,1)}, u32[]{:S(2)}) copy-start(bf16[256,1024]{1,0:T(8,128)(2,1)} %q_ref.3) | copy-start | bytes 1572868
  3.1 23.2 %copy-start.10 = (bf16[1,1,2,131072]{3,2,1,0:T(2,128)(2,1)S(1)}, bf16[1,1,2,131072]{3,2,1,0:T(2,128)(2,1)}, u32[]{:S(2)}) copy-start(bf16[1,1,2,131072]{3,2,1,0:T(2,128)(2,1)} %param.14) | copy-start | bytes 1572868
  3.1 23.2 %copy-start.8 = (bf16[256,256]{1,0:T(8,128)(2,1)S(1)}, bf16[256,256]{1,0:T(8,128)(2,1)}, u32[]{:S(2)}) copy-start(bf16[256,256]{1,0:T(8,128)(2,1)} %constant.10.clone.forward_ref) | copy-start | bytes 393220
  3.3 7.6 %collective-permute-start = (bf16[16,256]{1,0:T(8,128)(2,1)S(1)}, bf16[16,256]{1,0:T(8,128)(2,1)S(1)}, u32[]{:S(2)}, u32[]{:S(2)}) collective-permute-start(bf16[16,256]{1,0:T(8,128)(2,1)S(1)} %tails.1), channel_id=1, source_target_pairs={{0,1},{1,2},{2,3},{3,4},{4,5},{5,6},{6,7},{7,8},{8,9},{9,10},{10,1... | collective-permute-start | bytes 24584 | tf_op jit(solution)/shard_map/ppermute | solution.py:257
  10.9 1.0 %copy-start.1 = (bf16[256,1024]{1,0:T(8,128)(2,1)S(1)}, bf16[256,1024]{1,0:T(8,128)(2,1)}, u32[]{:S(2)}) copy-start(bf16[256,1024]{1,0:T(8,128)(2,1)} %k_ref.3) | copy-start | bytes 1572868
  12.0 1.0 %copy-start.3 = (bf16[256,1024]{1,0:T(8,128)(2,1)S(1)}, bf16[256,1024]{1,0:T(8,128)(2,1)}, u32[]{:S(2)}) copy-start(bf16[256,1024]{1,0:T(8,128)(2,1)} %v_ref.3) | copy-start | bytes 1572868
  15.4 24.4 %all-to-all-start = ((bf16[128,16,128]{2,1,0:T(8,128)(2,1)}), bf16[128,16,128]{2,1,0:T(8,128)(2,1)}, u32[]{:S(2)}, u32[]{:S(2)}) async-start(bf16[128,16,128]{2,1,0:T(8,128)(2,1)} %bitcast.2), calls=%async_computation | async-start | bytes 1048576 | tf_op jit(solution)/shard_map/all_to_all | solution.py:250
  26.4 1.2 %copy-start.6 = (f32[2,1024,128]{2,1,0:T(8,128)S(1)}, f32[2,1024,128]{2,1,0:T(8,128)}, u32[]{:S(2)}) copy-start(f32[2,1024,128]{2,1,0:T(8,128)} %constant.9.clone.turn_ref) | copy-start | bytes 3145732
  27.6 12.2 %copy-start.9 = (bf16[256,256]{1,0:T(8,128)(2,1)S(1)}, bf16[256,256]{1,0:T(8,128)(2,1)}, u32[]{:S(2)}) copy-start(bf16[256,256]{1,0:T(8,128)(2,1)} %constant.11.clone.inverse_ref) | copy-start | bytes 393220
  31.7 32.8 %copy-start.5 = (bf16[256,1024]{1,0:T(8,128)(2,1)S(1)}, bf16[256,1024]{1,0:T(8,128)(2,1)}, u32[]{:S(2)}) copy-start(bf16[256,1024]{1,0:T(8,128)(2,1)} %q_ref.3) | copy-start | bytes 1572868
  39.8 1.2 %copy-start.7 = (f32[2,1024,128]{2,1,0:T(8,128)S(1)}, f32[2,1024,128]{2,1,0:T(8,128)}, u32[]{:S(2)}) copy-start(f32[2,1024,128]{2,1,0:T(8,128)} %constant.9.clone.turn_ref) | copy-start | bytes 3145732
where the time goes:
time: 66.9 us; the launch traced here: 66.3 us
  blocking collectives  17.6 us (26%)
  starting transfers between devices  16.9 us (25%)
  Pallas kernels  14.3 us (21%)
  local copies, waits for them, and re-layouts  8.57 us (13%)
  waiting for transfers between devices  8.1 us (12%)
  other arithmetic  0.69 us (1%)
    all_to_all x1, blocking collectives, exchange(): return lax.all_to_all(flat, AXES, split_axis=0, concat_axis=0, tiled=True)  17.6 us
    all_to_all x1, starting transfers between devices, exchange(): return lax.all_to_all(flat, AXES, split_axis=0, concat_axis=0, tiled=True)  10.8 us
    all_to_all x1, waiting for transfers between devices, exchange(): return lax.all_to_all(flat, AXES, split_axis=0, concat_axis=0, tiled=True)  8.1 us
    unnamed x23, local copies, waits for them, and re-layouts  7.73 us
    ppermute x1, starting transfers between devices, shards(): rim = lax.ppermute(ends, AXES, [(i, i + 1) for i in range(count - 1)])  6.07 us
    pallas_call x1, Pallas kernels, conv(): call(conv_body, jax.ShapeDtypeStruct((SEQ * CH, 2 * TILES, LANES), BF16),...  5.87 us
    pallas_call x1, Pallas kernels, filter_spectra(): call(filter_body, jax.ShapeDtypeStruct((2, OUTER, 2 * LANES), F32), [], 1...  4.05 us
    pallas_call x1, Pallas kernels, gate(): call(gate_body, (jax.ShapeDtypeStruct((CHANNELS, TOKENS), BF16), jax.Shap...  2.41 us
  transfers between devices with their start and end apart: 2, of which 1 were waited for; matrix products, arithmetic and copies ran while one was open for 2% of the time, Pallas kernels for 6%

commit v1 on v0

v1 whole, which is shorter than its diff:
```python
import functools
import math

import jax
import jax.numpy as jnp
import ml_dtypes
import numpy as np
from jax import lax
from jax.experimental import pallas as pl
from jax.experimental.pallas import tpu as pltpu
from jax.sharding import PartitionSpec as P

F32 = jnp.float32
BF16 = jnp.bfloat16
LANES = 128
TOKENS = 1024
TILES = TOKENS // LANES
BLOCKS = 128
LENGTH = BLOCKS * TOKENS
CHANNELS = 256
SEQ = 8
CH = 16
BODY = 2 * TILES
EDGE = 8
MESSAGE = BODY + EDGE
ROWS = 32
GROUPS = ROWS // (2 * SEQ)
STEPS = CHANNELS // ROWS
AXES = ("seq", "ch")
VMEM = pl.BlockSpec(memory_space=pltpu.VMEM)
HBM = pl.BlockSpec(memory_space=pltpu.HBM)


def tables():
    step = 2.0 * math.pi
    tile = np.arange(TILES)[:, None, None]
    k1 = np.arange(BLOCKS)[None, :, None]
    block = np.arange(BLOCKS)[None, None, :]
    phase = ((TILES * block + tile) * (4 * k1 + 1) % (4 * TOKENS)) * (step / (4 * TOKENS))
    outer = np.concatenate([np.cos(phase), -np.sin(phase)], axis=1)
    lane = np.arange(LANES)[None, :]
    phase = lane * (np.arange(BLOCKS)[:, None] + 0.25) * (step / LENGTH)
    turn = np.stack([np.cos(phase), -np.sin(phase)])
    lane = np.arange(LANES)[None, :, None]
    k2 = np.arange(LANES)[None, None, :]
    phase = (lane * (TILES * k2 + tile) % TOKENS) * (step / TOKENS)
    cos, sin = np.cos(phase), np.sin(phase)
    inner = np.concatenate(
        [np.concatenate([cos, -sin], axis=2), np.concatenate([sin, cos], axis=2)], axis=1
    )
    narrow = ml_dtypes.bfloat16
    return dict(
        outer=outer.astype(narrow),
        outer_back=outer.swapaxes(1, 2).astype(narrow),
        turn=turn.astype(np.float32),
        inner=inner.astype(narrow),
        inner_back=inner.swapaxes(1, 2).astype(narrow),
    )


def dot(left, right):
    return jnp.dot(left, right, preferred_element_type=F32)


def call(body, name, out_shape, scratch, in_specs, out_specs, flops, nbytes):
    return pl.pallas_call(
        body,
        out_shape=out_shape,
        in_specs=in_specs,
        out_specs=out_specs,
        scratch_shapes=scratch,
        compiler_params=pltpu.CompilerParams(vmem_limit_bytes=24 * 1024 * 1024),
        cost_estimate=pl.CostEstimate(flops=flops, bytes_accessed=nbytes, transcendentals=0),
        name=name,
    )


def shape(dims, dtype):
    return jax.ShapeDtypeStruct(dims, dtype)


def lanes_of(x):
    return lax.broadcasted_iota(jnp.int32, x.shape, 1)


def columns(rows, tap_rows):
    tap_rows[...] = jnp.zeros(tap_rows.shape, F32)
    at = 0
    for row in rows:
        tap_rows[at : at + row.shape[0], :] = row
        at += row.shape[0]
    return tap_rows[...].T


def split_conv(x, cols, first):
    taps = [cols[:, first + i : first + i + 1] for i in range(3)]
    back1 = pltpu.roll(x, 1, 1)
    back2 = pltpu.roll(x, 2, 1)
    whole = taps[0] * x + taps[1] * back1 + taps[2] * back2
    x, back1, back2 = (part[:, :LANES] for part in (x, back1, back2))
    lane = lanes_of(x)
    own = taps[0] * x + jnp.where(lane < 1, 0.0, taps[1] * back1)
    own = own + jnp.where(lane < 2, 0.0, taps[2] * back2)
    onward = jnp.where(lane < 1, taps[1] * back1, 0.0) + jnp.where(lane < 2, taps[2] * back2, 0.0)
    return jnp.concatenate([own, whole[:, LANES:]], axis=1), own, onward


def in_two(x):
    rest = x - x.astype(BF16).astype(F32)
    return jnp.where(lanes_of(x) < 2, x, pltpu.roll(rest, 2, 1))


def gate_body(
    k_ref, v_ref, taps_ref, gated_ref, first_ref, out_ref, k_buf, v_buf, tap_rows, cols_buf, rows, edge, sems
):
    copies = []
    for step in range(STEPS):
        at = pl.ds(step * ROWS, ROWS)
        copies.append(
            [
                pltpu.make_async_copy(ref.at[at], buf.at[at], sems.at[i, step])
                for i, (ref, buf) in enumerate(((k_ref, k_buf), (v_ref, v_buf)))
            ]
        )
    for pair in copies:
        for copy in pair:
            copy.start()
    cols_buf[...] = columns([taps_ref[1], taps_ref[2]], tap_rows)
    for step in range(STEPS):
        for copy in copies[step]:
            copy.wait()
        at = slice(step * ROWS, (step + 1) * ROWS)
        cols = cols_buf[at, :]
        key, key_own, key_onward = split_conv(k_buf[at, :].astype(F32), cols, 0)
        value, value_own, value_onward = split_conv(v_buf[at, :].astype(F32), cols, 3)
        gated = (key * value).astype(BF16)
        gated_ref[at, :] = gated
        first_ref[0, at, :] = key_own
        first_ref[1, at, :] = value_own
        wide = gated.astype(F32)
        for c in range(TILES):
            rows[pl.ds(c, ROWS, stride=TILES), :] = wide[:, c * LANES : (c + 1) * LANES]
        for m, part in enumerate((key_own, value_own, key_onward, value_onward)):
            edge[pl.ds(m, ROWS, stride=4), :] = in_two(part)
        body = rows[...].reshape(ROWS // 2, BODY, LANES)
        message = jnp.concatenate([body, edge[...].reshape(ROWS // 2, EDGE, LANES)], axis=1)
        message = message.astype(BF16)
        for g in range(GROUPS):
            out_ref[:, step * GROUPS + g] = message[g * SEQ : (g + 1) * SEQ]


def gate(k, v, taps):
    return call(
        gate_body,
        "gate",
        (
            shape((CHANNELS, TOKENS), BF16),
            shape((2, CHANNELS, LANES), F32),
            shape((SEQ, CH, MESSAGE, LANES), BF16),
        ),
        [
            pltpu.VMEM((CHANNELS, TOKENS), BF16),
            pltpu.VMEM((CHANNELS, TOKENS), BF16),
            pltpu.VMEM((LANES, CHANNELS), F32),
            pltpu.VMEM((CHANNELS, LANES), F32),
            pltpu.VMEM((ROWS * TILES, LANES), F32),
            pltpu.VMEM((ROWS * 4, LANES), F32),
            pltpu.SemaphoreType.DMA((2, STEPS)),
        ],
        [HBM, HBM, VMEM],
        (VMEM, VMEM, VMEM),
        10**7,
        2 * 1024 * 1024,
    )(k, v, taps)


def eight_points(re, im):
    half = math.sqrt(0.5)
    out_re, out_im = [None] * 8, [None] * 8

    def four_points(re, im, first):
        sum_re = [re[i] + re[i + 2] for i in range(2)]
        sum_im = [im[i] + im[i + 2] for i in range(2)]
        dif_re = [re[i] - re[i + 2] for i in range(2)]
        dif_im = [im[i] - im[i + 2] for i in range(2)]
        out_re[first], out_im[first] = sum_re[0] + sum_re[1], sum_im[0] + sum_im[1]
        out_re[first + 4], out_im[first + 4] = sum_re[0] - sum_re[1], sum_im[0] - sum_im[1]
        out_re[first + 2], out_im[first + 2] = dif_re[0] + dif_im[1], dif_im[0] - dif_re[1]
        out_re[first + 6], out_im[first + 6] = dif_re[0] - dif_im[1], dif_im[0] + dif_re[1]

    four_points([re[i] + re[i + 4] for i in range(4)], [im[i] + im[i + 4] for i in range(4)], 0)
    re = [re[i] - re[i + 4] for i in range(4)]
    im = [im[i] - im[i + 4] for i in range(4)]
    turned_re = [re[0], (re[1] + im[1]) * half, im[2], (im[3] - re[3]) * half]
    turned_im = [im[0], (im[1] - re[1]) * half, -re[2], (re[3] + im[3]) * -half]
    four_points(turned_re, turned_im, 1)
    return out_re, out_im


def forward(signals, outer_ref, turn_ref, section, turned):
    for c in range(TILES):
        section[c] = dot(outer_ref[c], signals[c])
    for row in range(0, BLOCKS, 16):
        turn_re, turn_im = turn_ref[0, row : row + 16, :], turn_ref[1, row : row + 16, :]
        for j in range(2):
            half = slice(j * LANES, (j + 1) * LANES)
            re = [section[c, row : row + 16, half] for c in range(TILES)]
            im = [section[c, BLOCKS + row : BLOCKS + row + 16, half] for c in range(TILES)]
            re, im = eight_points(re, im)
            at = slice(j * BLOCKS + row, j * BLOCKS + row + 16)
            for kc in range(TILES):
                turned[kc, at, :LANES] = (re[kc] * turn_re - im[kc] * turn_im).astype(BF16)
                turned[kc, at, LANES:] = (re[kc] * turn_im + im[kc] * turn_re).astype(BF16)


def filter_body(
    filt_ref, outer_ref, turn_ref, inner_ref, q_ref, k_ref, v_ref, gated_ref, spec_ref, ends_ref,
    rows, section, turned, last, sems
):
    del gated_ref
    copies = [
        pltpu.make_async_copy(
            ref.at[:, pl.ds(TOKENS - LANES, LANES)], last.at[i], sems.at[i]
        )
        for i, ref in enumerate((q_ref, k_ref, v_ref))
    ]
    for copy in copies:
        copy.start()
    rows[...] = filt_ref[...].astype(F32).reshape(2 * BLOCKS * TILES, LANES)
    signals = []
    for c in range(TILES):
        halves = [rows[pl.ds(j * TOKENS + c, BLOCKS, stride=TILES), :] for j in range(2)]
        signals.append(jnp.concatenate(halves, axis=1).astype(BF16))
    forward(signals, outer_ref, turn_ref, section, turned)
    for kc in range(TILES):
        spec_ref[kc] = dot(turned[kc], inner_ref[kc]) * (1.0 / LENGTH)
    row = lax.broadcasted_iota(jnp.int32, (16, LANES), 0)
    lane = lax.broadcasted_iota(jnp.int32, (16, LANES), 1)
    total = jnp.zeros((16, CHANNELS), F32)
    for i in range(3):
        copies[i].wait()
        pick = (row - 2 * i == lane - (LANES - 2)) & (lane >= LANES - 2)
        total += lax.dot_general(
            pick.astype(BF16), last[i], (((1,), (1,)), ((), ())), preferred_element_type=F32
        )
    ends_ref[...] = total.astype(BF16)


def filter_spectra(filt, consts, q, k, v, gated):
    return call(
        filter_body,
        "filter_spectra",
        (shape((TILES, 2 * BLOCKS, 2 * LANES), F32), shape((16, CHANNELS), BF16)),
        [
            pltpu.VMEM((2 * BLOCKS * TILES, LANES), F32),
            pltpu.VMEM((TILES, 2 * BLOCKS, 2 * LANES), F32),
            pltpu.VMEM((TILES, 2 * BLOCKS, 2 * LANES), BF16),
            pltpu.VMEM((3, CHANNELS, LANES), BF16),
            pltpu.SemaphoreType.DMA((3,)),
        ],
        [VMEM, VMEM, VMEM, VMEM, HBM, HBM, HBM, pl.BlockSpec(memory_space=pl.ANY)],
        (VMEM, VMEM),
        10**9,
        8 * 1024 * 1024,
    )(filt, consts["outer"], consts["turn"], consts["inner"], q, k, v, gated)


def conv_body(
    arrived_ref, spec_ref, outer_ref, outer_back_ref, turn_ref, inner_ref, inner_back_ref, out_ref,
    rows, section, turned, back
):
    rows[:MESSAGE, :] = jnp.zeros((MESSAGE, LANES), F32)
    rows[MESSAGE:, :] = arrived_ref[...].astype(F32).reshape(BLOCKS * MESSAGE, LANES)

    def picked(row, before=0):
        return rows[pl.ds((1 - before) * MESSAGE + row, BLOCKS, stride=MESSAGE), :]

    def edge(j, m, before):
        part = picked(BODY + 4 * j + m, before)
        return part + pltpu.roll(part, LANES - 2, 1)

    signals = []
    for c in range(TILES):
        halves = [picked(j * TILES + c) for j in range(2)]
        if c == 0:
            for j in range(2):
                key = edge(j, 0, 0) + edge(j, 2, 1)
                value = edge(j, 1, 0) + edge(j, 3, 1)
                halves[j] = jnp.where(lanes_of(key) < 2, key * value, halves[j])
        signals.append(jnp.concatenate(halves, axis=1).astype(BF16))
    forward(signals, outer_ref, turn_ref, section, turned)
    for kc in range(TILES):
        spectrum = dot(turned[kc], inner_ref[kc])
        re, im = spectrum[:, :LANES], spectrum[:, LANES:]
        filt_re, filt_im = spec_ref[kc, :, :LANES], spec_ref[kc, :, LANES:]
        parts = [re * filt_re - im * filt_im, re * filt_im + im * filt_re]
        section[kc] = dot(jnp.concatenate(parts, axis=1).astype(BF16), inner_back_ref[kc])
    for row in range(0, BLOCKS, 16):
        turn_re, turn_im = turn_ref[0, row : row + 16, :], turn_ref[1, row : row + 16, :]
        for j in range(2):
            at = slice(j * BLOCKS + row, j * BLOCKS + row + 16)
            re, im = [], []
            for kc in range(TILES):
                part_re, part_im = section[kc, at, :LANES], section[kc, at, LANES:]
                re.append(part_re * turn_re + part_im * turn_im)
                im.append(part_im * turn_re - part_re * turn_im)
            im, re = eight_points(im, re)
            half = slice(j * LANES, (j + 1) * LANES)
            for c in range(TILES):
                back[c, row : row + 16, half] = re[c].astype(BF16)
                back[c, BLOCKS + row : BLOCKS + row + 16, half] = im[c].astype(BF16)
    for c in range(TILES):
        result = dot(outer_back_ref[c], back[c])
        for j in range(2):
            rows[pl.ds(j * TILES + c, BLOCKS, stride=BODY), :] = result[:, j * LANES : (j + 1) * LANES]
    out_ref[...] = rows[: BLOCKS * BODY, :].reshape(BLOCKS, BODY, LANES).astype(BF16)


def conv(arrived, spec, consts):
    names = ("outer", "outer_back", "turn", "inner", "inner_back")
    return call(
        conv_body,
        "conv",
        shape((BLOCKS, BODY, LANES), BF16),
        [
            pltpu.VMEM(((BLOCKS + 1) * MESSAGE, LANES), F32),
            pltpu.VMEM((TILES, 2 * BLOCKS, 2 * LANES), F32),
            pltpu.VMEM((TILES, 2 * BLOCKS, 2 * LANES), BF16),
            pltpu.VMEM((TILES, 2 * BLOCKS, 2 * LANES), BF16),
        ],
        [VMEM] * 7,
        VMEM,
        10**9,
        8 * 1024 * 1024,
    )(arrived, spec, *(consts[name] for name in names))


def direct_body(
    q_ref, gated_ref, first_ref, rim_ref, taps_ref, skip_ref, query_ref, direct_ref, tap_rows, cols_buf, rim_buf
):
    cols_buf[...] = columns([taps_ref[0], taps_ref[1], taps_ref[2], skip_ref[...]], tap_rows)
    tap_rows[:16, :] = rim_ref[...].astype(F32)
    rim_buf[...] = tap_rows[...].T
    for step in range(STEPS):
        at = slice(step * ROWS, (step + 1) * ROWS)
        cols, rim = cols_buf[at, :], rim_buf[at, :]
        lane = lax.broadcasted_iota(jnp.int32, (ROWS, LANES), 1)

        def before(stream):
            older, newer = rim[:, 2 * stream : 2 * stream + 1], rim[:, 2 * stream + 1 : 2 * stream + 2]
            one, two = cols[:, 3 * stream + 1 : 3 * stream + 2], cols[:, 3 * stream + 2 : 3 * stream + 3]
            return jnp.where(
                lane == 0, one * newer + two * older, jnp.where(lane == 1, two * newer, 0.0)
            )

        query, query_own, _ = split_conv(q_ref[at, :].astype(F32), cols, 0)
        query_ref[at, :] = query
        query_ref[at, :LANES] = query_own + before(0)
        skip = cols[:, 9:10]
        direct_ref[at, :] = skip * gated_ref[at, :].astype(F32)
        start = (first_ref[0, at, :] + before(1)) * (first_ref[1, at, :] + before(2))
        direct_ref[at, :LANES] = skip * start.astype(BF16).astype(F32)


def direct(q, gated, first, rim, taps, skip):
    return call(
        direct_body,
        "direct",
        (shape((CHANNELS, TOKENS), F32), shape((CHANNELS, TOKENS), F32)),
        [
            pltpu.VMEM((LANES, CHANNELS), F32),
            pltpu.VMEM((CHANNELS, LANES), F32),
            pltpu.VMEM((CHANNELS, LANES), F32),
        ],
        [VMEM] * 6,
        (VMEM, VMEM),
        10**7,
        4 * 1024 * 1024,
    )(q, gated, first, rim, taps, skip)


def final_body(returned_ref, query_ref, direct_ref, out_ref, rows, out_buf, sems):
    per_group = ROWS * TILES // GROUPS
    copies = []
    for step in range(STEPS):
        at = slice(step * ROWS, (step + 1) * ROWS)
        for g in range(GROUPS):
            message = returned_ref[:, step * GROUPS + g].astype(F32)
            rows[g * per_group : (g + 1) * per_group, :] = message.reshape(per_group, LANES)
        for c in range(TILES):
            lanes = slice(c * LANES, (c + 1) * LANES)
            long_result = rows[pl.ds(c, ROWS, stride=TILES), :]
            mixed = query_ref[at, lanes] * (long_result + direct_ref[at, lanes])
            out_buf[at, lanes] = mixed.astype(BF16)
        place = pl.ds(step * ROWS, ROWS)
        copies.append(pltpu.make_async_copy(out_buf.at[place], out_ref.at[place], sems.at[step]))
        copies[-1].start()
    for copy in copies:
        copy.wait()


def final(returned, query, direct_term):
    return call(
        final_body,
        "final",
        shape((CHANNELS, TOKENS), BF16),
        [
            pltpu.VMEM((ROWS * TILES, LANES), F32),
            pltpu.VMEM((CHANNELS, TOKENS), BF16),
            pltpu.SemaphoreType.DMA((STEPS,)),
        ],
        [VMEM] * 3,
        HBM,
        10**6,
        2 * 1024 * 1024,
    )(returned, query, direct_term)


def exchange(messages):
    return lax.all_to_all(messages, AXES, split_axis=0, concat_axis=0, tiled=True)


def shards(consts, q, k, v, short_taps, long_filter, skip_gain):
    consts = {name: jnp.asarray(table) for name, table in consts.items()}
    count = lax.axis_size("seq") * lax.axis_size("ch")
    gated, first, messages = gate(k, v, short_taps)
    arrived = exchange(messages.reshape(BLOCKS, MESSAGE, LANES))
    filt = long_filter.reshape(2, BLOCKS * TILES, LANES)
    spec, ends = filter_spectra(filt, consts, q, k, v, gated)
    rim = lax.ppermute(ends, AXES, [(i, i + 1) for i in range(count - 1)])
    query, direct_term = direct(q, gated, first, rim, short_taps, skip_gain[None])
    results = conv(arrived, spec, consts)
    returned = exchange(results).reshape(SEQ, CH, BODY, LANES)
    return final(returned, query, direct_term)


def solution(mesh):
    tokens = P(None, AXES)
    placed = (tokens, tokens, tokens, P(), P("ch", "seq", None, None), P())
    return jax.shard_map(
        functools.partial(shards, tables()),
        mesh=mesh,
        in_specs=placed,
        out_specs=tokens,
        check_vma=False,
    )
```

time: 66.9 us -> 67.7 us (1.012)
  the two profiles are of different devices: /device:TPU:1 before, /device:TPU:2 now
where the time goes in v1:
time: 67.7 us; the launch traced here: 67.1 us
  local copies, waits for them, and re-layouts  18.2 us (27%)
  starting transfers between devices  17.8 us (26%)
  waiting for transfers between devices  17.8 us (26%)
  Pallas kernels  13 us (19%)
    unnamed x53, local copies, waits for them, and re-layouts  18.2 us
    all_to_all x2, starting transfers between devices, exchange(): lax.all_to_all(messages, AXES, split_axis=0, concat_axis=0, tiled=True)  15.7 us
    ppermute x1, waiting for transfers between devices, shards(): rim = lax.ppermute(ends, AXES, [(i, i + 1) for i in range(count - 1)])  9.35 us
    all_to_all x2, waiting for transfers between devices, exchange(): lax.all_to_all(messages, AXES, split_axis=0, concat_axis=0, tiled=True)  8.49 us
    pallas_call x1, Pallas kernels, gate(): call(gate_body, 'gate', (shape((CHANNELS, TOKENS), BF16), shape((2, CHANN...  3.9 us
    pallas_call x1, Pallas kernels, direct(): call(direct_body, 'direct', (shape((CHANNELS, TOKENS), F32), shape((CHANN...  3.65 us
    pallas_call x1, Pallas kernels, conv(): call(conv_body, 'conv', shape((BLOCKS, BODY, LANES), BF16), [pltpu.VMEM((...  2.77 us
    ppermute x1, starting transfers between devices, shards(): rim = lax.ppermute(ends, AXES, [(i, i + 1) for i in range(count - 1)])  2.06 us
  transfers between devices with their start and end apart: 3, of which 2 were waited for; matrix products, arithmetic and copies ran while one was open for 2% of the time, Pallas kernels for 8%

profile of v1, /device:TPU:2, one launch (start us, length us, event | category | flops | bytes accessed | tf_op | source)
XLA Modules:
  0.0 67.1 jit_solution(16436964230546739725)
XLA Ops:
  0.0 1.2 %copy-done.4 = bf16[256,1024]{1,0:T(8,128)(2,1)S(1)} copy-done((bf16[256,1024]{1,0:T(8,128)(2,1)S(1)}, bf16[256,1024]{1,0:T(8,128)(2,1)}, u32[]{:S(2)}) %copy-start.4) | copy-done | bytes 524312
  1.2 1.0 %copy-done.6 = bf16[256,1024]{1,0:T(8,128)(2,1)S(1)} copy-done((bf16[256,1024]{1,0:T(8,128)(2,1)S(1)}, bf16[256,1024]{1,0:T(8,128)(2,1)}, u32[]{:S(2)}) %copy-start.6) | copy-done | bytes 524312
  2.9 3.9 %gate.1 = (bf16[256,1024]{1,0:T(8,128)(2,1)S(1)}, f32[2,256,128]{2,1,0:T(8,128)S(1)}, bf16[8,16,24,128]{3,2,1,0:T(8,128)(2,1)S(1)}) custom-call(bf16[256,1024]{1,0:T(8,128)(2,1)S(1)} %copy-done.4, bf16[256,1024]{1,0:T(8,128)(2,1)S(1)} %copy-done.6, f32[3,3,256]{2,1,0:T(4,128)S(1)} %copy-done.22), custom_call_target="tpu_custom_call" | custom-call | flops 10000000 | bytes 2097152 | tf_op jit(solution)/shard_map/gate/pallas_call | solution.py:153
  7.6 0.9 %copy-done.17 = bf16[8,16,24,128]{3,2,1,0:T(8,128)(2,1)} copy-done((bf16[8,16,24,128]{3,2,1,0:T(8,128)(2,1)}, bf16[8,16,24,128]{3,2,1,0:T(8,128)(2,1)S(1)}, u32[]{:S(2)}) %copy-start.17) | copy-done | bytes 786456
  9.2 10.5 %all-to-all-start = ((bf16[128,24,128]{2,1,0:T(8,128)(2,1)}), bf16[128,24,128]{2,1,0:T(8,128)(2,1)S(1)}, u32[]{:S(2)}, u32[]{:S(2)}) async-start(bf16[128,24,128]{2,1,0:T(8,128)(2,1)} %bitcast.10), calls=%async_computation | async-start | bytes 1572864 | tf_op jit(solution)/shard_map/all_to_all | solution.py:420
  19.7 1.1 %copy.14 = bf16[1,2,1024,128]{3,2,1,0:T(8,128)(2,1)S(1)} copy(bf16[1,2,1024,128]{3,1,2,0:T(2,128)(2,1)} %bitcast.12) | data formatting | bytes 1048576
  20.9 1.0 %copy-done.8 = bf16[256,1024]{1,0:T(8,128)(2,1)S(1)} copy-done((bf16[256,1024]{1,0:T(8,128)(2,1)S(1)}, bf16[256,1024]{1,0:T(8,128)(2,1)}, u32[]{:S(2)}) %copy-start.8) | copy-done | bytes 524312
  22.0 1.0 %copy-done.11 = bf16[256,1024]{1,0:T(8,128)(2,1)S(1)} copy-done((bf16[256,1024]{1,0:T(8,128)(2,1)S(1)}, bf16[256,1024]{1,0:T(8,128)(2,1)}, u32[]{:S(2)}) %copy-start.11) | copy-done | bytes 524312
  23.0 1.7 %filter_spectra.1 = (f32[8,256,256]{2,1,0:T(8,128)S(1)}, bf16[16,256]{1,0:T(8,128)(2,1)S(1)}) custom-call(bf16[2,1024,128]{2,1,0:T(8,128)(2,1)S(1)} %bitcast.8, bf16[8,256,128]{2,1,0:T(8,128)(2,1)S(1)} %copy-done.3, f32[2,128,128]{2,1,0:T(8,128)S(1)} %copy-done.19, bf16[8,256,256]{2,1,0:T(8,128)(2,1)S(1)} %copy-done, bf16[256,1024]{1,0:T(8,128)(2,1)S(1)} %copy-done.8, ...), custom_call_target="tpu_custom_call" | custom-call | flops 1000000000 | bytes 8388608 | tf_op jit(solution)/shard_map/filter_spectra/pallas_call | solution.py:250
  24.7 1.3 %copy-done.1 = f32[8,256,256]{2,1,0:T(8,128)} copy-done((f32[8,256,256]{2,1,0:T(8,128)}, f32[8,256,256]{2,1,0:T(8,128)S(1)}, u32[]{:S(2)}) %copy-start.1) | copy-done | bytes 2097176
  26.6 8.5 %all-to-all-done.arrived_ref = bf16[128,24,128]{2,1,0:T(8,128)(2,1)S(1)} async-done(((bf16[128,24,128]{2,1,0:T(8,128)(2,1)}), bf16[128,24,128]{2,1,0:T(8,128)(2,1)S(1)}, u32[]{:S(2)}, u32[]{:S(2)}) %all-to-all-start) | async-done | bytes 786464 | tf_op jit(solution)/shard_map/all_to_all | solution.py:420
  35.1 1.6 %copy-done.2 = f32[8,256,256]{2,1,0:T(8,128)S(1)} copy-done((f32[8,256,256]{2,1,0:T(8,128)S(1)}, f32[8,256,256]{2,1,0:T(8,128)}, u32[]{:S(2)}) %copy-start.2) | copy-done | bytes 2097176
  36.7 1.2 %copy-done.14 = bf16[8,256,256]{2,1,0:T(8,128)(2,1)S(1)} copy-done((bf16[8,256,256]{2,1,0:T(8,128)(2,1)S(1)}, bf16[8,256,256]{2,1,0:T(8,128)(2,1)}, u32[]{:S(2)}) %copy-start.14) | copy-done | bytes 1048600
  37.9 1.0 %copy-done.18 = bf16[8,128,256]{2,1,0:T(8,128)(2,1)S(1)} copy-done((bf16[8,128,256]{2,1,0:T(8,128)(2,1)S(1)}, bf16[8,128,256]{2,1,0:T(8,128)(2,1)}, u32[]{:S(2)}) %copy-start.18) | copy-done | bytes 524312
  39.0 2.8 %conv.1 = bf16[128,16,128]{2,1,0:T(8,128)(2,1)S(1)} custom-call(bf16[128,24,128]{2,1,0:T(8,128)(2,1)S(1)} %all-to-all-done.arrived_ref, f32[8,256,256]{2,1,0:T(8,128)S(1)} %copy-done.2, bf16[8,256,128]{2,1,0:T(8,128)(2,1)S(1)} %copy-done.3, bf16[8,128,256]{2,1,0:T(8,128)(2,1)S(1)} %copy-done.18, f32[2,128,128]{2,1,0:T(8,128)S(1)} %copy-done.19, ...), custom_call_target="tpu_custom_call" | custom-call | flops 1000000000 | bytes 8388608 | tf_op jit(solution)/shard_map/conv/pallas_call | solution.py:321
  41.8 0.8 %copy-done.13 = bf16[128,16,128]{2,1,0:T(8,128)(2,1)} copy-done((bf16[128,16,128]{2,1,0:T(8,128)(2,1)}, bf16[128,16,128]{2,1,0:T(8,128)(2,1)S(1)}, u32[]{:S(2)}) %copy-start.13) | copy-done | bytes 524312
  42.6 5.2 %all-to-all-start.1 = ((bf16[128,16,128]{2,1,0:T(8,128)(2,1)}), bf16[128,16,128]{2,1,0:T(8,128)(2,1)S(1)}, u32[]{:S(2)}, u32[]{:S(2)}) async-start(bf16[128,16,128]{2,1,0:T(8,128)(2,1)} %copy-done.13), calls=%async_computation.1 | async-start | bytes 1048576 | tf_op jit(solution)/shard_map/all_to_all | solution.py:420
  47.8 2.1 %collective-permute-start = (bf16[16,256]{1,0:T(8,128)(2,1)}, bf16[16,256]{1,0:T(8,128)(2,1)S(1)}, u32[]{:S(2)}, u32[]{:S(2)}) collective-permute-start(bf16[16,256]{1,0:T(8,128)(2,1)} %copy-done.25), channel_id=1, source_target_pairs={{0,1},{1,2},{2,3},{3,4},{4,5},{5,6},{6,7},{7,8},{8,9},{9,10},{10,1... | collective-permute-start | bytes 24584 | tf_op jit(solution)/shard_map/ppermute | solution.py:430
  49.9 9.4 %collective-permute-done.rim_ref = bf16[16,256]{1,0:T(8,128)(2,1)S(1)} collective-permute-done((bf16[16,256]{1,0:T(8,128)(2,1)}, bf16[16,256]{1,0:T(8,128)(2,1)S(1)}, u32[]{:S(2)}, u32[]{:S(2)}) %collective-permute-start) | collective-permute-done | bytes 8224 | tf_op jit(solution)/shard_map/ppermute | solution.py:430
  59.2 0.9 %copy-done.21 = f32[2,256,128]{2,1,0:T(8,128)S(1)} copy-done((f32[2,256,128]{2,1,0:T(8,128)S(1)}, f32[2,256,128]{2,1,0:T(8,128)}, u32[]{:S(2)}) %copy-start.21) | copy-done | bytes 262168
  60.2 3.6 %direct.1 = (f32[256,1024]{1,0:T(8,128)S(1)}, f32[256,1024]{1,0:T(8,128)S(1)}) custom-call(bf16[256,1024]{1,0:T(8,128)(2,1)S(1)} %copy-done.9, bf16[256,1024]{1,0:T(8,128)(2,1)S(1)} %copy-done.12, f32[2,256,128]{2,1,0:T(8,128)S(1)} %copy-done.21, bf16[16,256]{1,0:T(8,128)(2,1)S(1)} %collective-permute-done.rim_ref, f32[3,3,256]{2,1,0:T(4,128)S(1)} %copy-done.23, ...), custom_call_target="tpu_custom_call" | custom-call | flops 10000000 | bytes 4194304 | tf_op jit(solution)/shard_map/direct/pallas_call | solution.py:366
  63.9 1.0 %copy-done.15 = f32[256,1024]{1,0:T(8,128)} copy-done((f32[256,1024]{1,0:T(8,128)}, f32[256,1024]{1,0:T(8,128)S(1)}, u32[]{:S(2)}) %copy-start.15) | copy-done | bytes 1048600
  64.8 1.2 %copy-done.16 = f32[256,1024]{1,0:T(8,128)S(1)} copy-done((f32[256,1024]{1,0:T(8,128)S(1)}, f32[256,1024]{1,0:T(8,128)}, u32[]{:S(2)}) %copy-start.16) | copy-done | bytes 1048600
  66.0 1.1 %final.1 = bf16[256,1024]{1,0:T(8,128)(2,1)} custom-call(bf16[8,16,16,128]{3,2,1,0:T(8,128)(2,1)S(1)} %bitcast.9, f32[256,1024]{1,0:T(8,128)S(1)} %get-tuple-element.17.query_ref, f32[256,1024]{1,0:T(8,128)S(1)} %copy-done.16), custom_call_target="tpu_custom_call" | custom-call | flops 1000000 | bytes 2097152 | tf_op jit(solution)/shard_map/final/pallas_call | solution.py:403
  (40 shorter events, 2.9 us)
Async XLA Ops:
  0.0 20.9 %copy-start = (bf16[8,256,256]{2,1,0:T(8,128)(2,1)S(1)}, bf16[8,256,256]{2,1,0:T(8,128)(2,1)}, u32[]{:S(2)}) copy-start(bf16[8,256,256]{2,1,0:T(8,128)(2,1)} %constant.13.clone.inner_ref) | copy-start | bytes 3145732
  0.0 20.9 %copy-start.3 = (bf16[8,256,128]{2,1,0:T(8,128)(2,1)S(1)}, bf16[8,256,128]{2,1,0:T(8,128)(2,1)}, u32[]{:S(2)}) copy-start(bf16[8,256,128]{2,1,0:T(8,128)(2,1)} %constant.10.clone.outer_ref) | copy-start | bytes 1572868
  0.0 1.2 %copy-start.4 = (bf16[256,1024]{1,0:T(8,128)(2,1)S(1)}, bf16[256,1024]{1,0:T(8,128)(2,1)}, u32[]{:S(2)}) copy-start(bf16[256,1024]{1,0:T(8,128)(2,1)} %k_ref.3) | copy-start | bytes 1572868
  1.2 1.0 %copy-start.6 = (bf16[256,1024]{1,0:T(8,128)(2,1)S(1)}, bf16[256,1024]{1,0:T(8,128)(2,1)}, u32[]{:S(2)}) copy-start(bf16[256,1024]{1,0:T(8,128)(2,1)} %v_ref.3) | copy-start | bytes 1572868
  2.9 18.0 %copy-start.5 = (bf16[256,1024]{1,0:T(8,128)(2,1)S(1)}, bf16[256,1024]{1,0:T(8,128)(2,1)}, u32[]{:S(2)}) copy-start(bf16[256,1024]{1,0:T(8,128)(2,1)} %k_ref.3) | copy-start | bytes 1572868
  2.9 18.0 %copy-start.7 = (bf16[256,1024]{1,0:T(8,128)(2,1)S(1)}, bf16[256,1024]{1,0:T(8,128)(2,1)}, u32[]{:S(2)}) copy-start(bf16[256,1024]{1,0:T(8,128)(2,1)} %v_ref.3) | copy-start | bytes 1572868
  2.9 18.0 %copy-start.19 = (f32[2,128,128]{2,1,0:T(8,128)S(1)}, f32[2,128,128]{2,1,0:T(8,128)}, u32[]{:S(2)}) copy-start(f32[2,128,128]{2,1,0:T(8,128)} %constant.12.clone.turn_ref) | copy-start | bytes 393220
  7.6 0.9 %copy-start.17 = (bf16[8,16,24,128]{3,2,1,0:T(8,128)(2,1)}, bf16[8,16,24,128]{3,2,1,0:T(8,128)(2,1)S(1)}, u32[]{:S(2)}) copy-start(bf16[8,16,24,128]{3,2,1,0:T(8,128)(2,1)S(1)} %get-tuple-element.12) | copy-start | bytes 2359300
  9.2 25.9 %all-to-all-start = ((bf16[128,24,128]{2,1,0:T(8,128)(2,1)}), bf16[128,24,128]{2,1,0:T(8,128)(2,1)S(1)}, u32[]{:S(2)}, u32[]{:S(2)}) async-start(bf16[128,24,128]{2,1,0:T(8,128)(2,1)} %bitcast.10), calls=%async_computation | async-start | bytes 1572864 | tf_op jit(solution)/shard_map/all_to_all | solution.py:420
  20.9 1.0 %copy-start.8 = (bf16[256,1024]{1,0:T(8,128)(2,1)S(1)}, bf16[256,1024]{1,0:T(8,128)(2,1)}, u32[]{:S(2)}) copy-start(bf16[256,1024]{1,0:T(8,128)(2,1)} %q_ref.3) | copy-start | bytes 1572868
  22.0 1.0 %copy-start.11 = (bf16[256,1024]{1,0:T(8,128)(2,1)S(1)}, bf16[256,1024]{1,0:T(8,128)(2,1)}, u32[]{:S(2)}) copy-start(bf16[256,1024]{1,0:T(8,128)(2,1)} %copy-done.10) | copy-start | bytes 1572868
  24.7 1.4 %copy-start.1 = (f32[8,256,256]{2,1,0:T(8,128)}, f32[8,256,256]{2,1,0:T(8,128)S(1)}, u32[]{:S(2)}) copy-start(f32[8,256,256]{2,1,0:T(8,128)S(1)} %get-tuple-element.14.spec_ref) | copy-start | bytes 6291460
  35.1 1.6 %copy-start.2 = (f32[8,256,256]{2,1,0:T(8,128)S(1)}, f32[8,256,256]{2,1,0:T(8,128)}, u32[]{:S(2)}) copy-start(f32[8,256,256]{2,1,0:T(8,128)} %copy-done.1) | copy-start | bytes 6291460
  36.7 1.2 %copy-start.14 = (bf16[8,256,256]{2,1,0:T(8,128)(2,1)S(1)}, bf16[8,256,256]{2,1,0:T(8,128)(2,1)}, u32[]{:S(2)}) copy-start(bf16[8,256,256]{2,1,0:T(8,128)(2,1)} %constant.14.clone.inner_back_ref) | copy-start | bytes 3145732
  37.9 1.0 %copy-start.18 = (bf16[8,128,256]{2,1,0:T(8,128)(2,1)S(1)}, bf16[8,128,256]{2,1,0:T(8,128)(2,1)}, u32[]{:S(2)}) copy-start(bf16[8,128,256]{2,1,0:T(8,128)(2,1)} %constant.11.clone.outer_back_ref) | copy-start | bytes 1572868
  39.0 20.2 %copy-start.9 = (bf16[256,1024]{1,0:T(8,128)(2,1)S(1)}, bf16[256,1024]{1,0:T(8,128)(2,1)}, u32[]{:S(2)}) copy-start(bf16[256,1024]{1,0:T(8,128)(2,1)} %q_ref.3) | copy-start | bytes 1572868
  39.0 20.2 %copy-start.12 = (bf16[256,1024]{1,0:T(8,128)(2,1)S(1)}, bf16[256,1024]{1,0:T(8,128)(2,1)}, u32[]{:S(2)}) copy-start(bf16[256,1024]{1,0:T(8,128)(2,1)} %copy-done.10) | copy-start | bytes 1572868
  39.0 20.2 %copy-start.23 = (f32[3,3,256]{2,1,0:T(4,128)S(1)}, f32[3,3,256]{2,1,0:T(4,128)}, u32[]{:S(2)}) copy-start(f32[3,3,256]{2,1,0:T(4,128)} %taps_ref.3) | copy-start | bytes 27652
  39.0 20.2 %copy-start.24 = (f32[256]{0:T(256)S(1)}, f32[256]{0:T(256)}, u32[]{:S(2)}) copy-start(f32[256]{0:T(256)} %param.16) | copy-start | bytes 3076
  42.6 22.2 %all-to-all-start.1 = ((bf16[128,16,128]{2,1,0:T(8,128)(2,1)}), bf16[128,16,128]{2,1,0:T(8,128)(2,1)S(1)}, u32[]{:S(2)}, u32[]{:S(2)}) async-start(bf16[128,16,128]{2,1,0:T(8,128)(2,1)} %copy-done.13), calls=%async_computation.1 | async-start | bytes 1048576 | tf_op jit(solution)/shard_map/all_to_all | solution.py:420
  47.8 11.4 %collective-permute-start = (bf16[16,256]{1,0:T(8,128)(2,1)}, bf16[16,256]{1,0:T(8,128)(2,1)S(1)}, u32[]{:S(2)}, u32[]{:S(2)}) collective-permute-start(bf16[16,256]{1,0:T(8,128)(2,1)} %copy-done.25), channel_id=1, source_target_pairs={{0,1},{1,2},{2,3},{3,4},{4,5},{5,6},{6,7},{7,8},{8,9},{9,10},{10,1... | collective-permute-start | bytes 24584 | tf_op jit(solution)/shard_map/ppermute | solution.py:430
  59.2 1.0 %copy-start.21 = (f32[2,256,128]{2,1,0:T(8,128)S(1)}, f32[2,256,128]{2,1,0:T(8,128)}, u32[]{:S(2)}) copy-start(f32[2,256,128]{2,1,0:T(8,128)} %copy-done.20) | copy-start | bytes 786436
  63.8 1.0 %copy-start.15 = (f32[256,1024]{1,0:T(8,128)}, f32[256,1024]{1,0:T(8,128)S(1)}, u32[]{:S(2)}) copy-start(f32[256,1024]{1,0:T(8,128)S(1)} %get-tuple-element.18.direct_ref) | copy-start | bytes 3145732
  64.8 1.2 %copy-start.16 = (f32[256,1024]{1,0:T(8,128)S(1)}, f32[256,1024]{1,0:T(8,128)}, u32[]{:S(2)}) copy-start(f32[256,1024]{1,0:T(8,128)} %copy-done.15) | copy-start | bytes 3145732
  (5 other events, 3.6 us)

commit v2 on v1

v2 whole, which is shorter than its diff:
```python
import functools
import math

import jax
import jax.numpy as jnp
import ml_dtypes
import numpy as np
from jax import lax
from jax.experimental import pallas as pl
from jax.experimental.pallas import tpu as pltpu
from jax.sharding import PartitionSpec as P

F32 = jnp.float32
BF16 = jnp.bfloat16
LANES = 128
TOKENS = 1024
TILES = TOKENS // LANES
BLOCKS = 128
LENGTH = BLOCKS * TOKENS
CHANNELS = 256
SEQ = 8
CH = 16
BODY = 2 * TILES
EDGE = 8
GATE_LIMIT, BESIDE_LIMIT, CONV_LIMIT, FINAL_LIMIT = 60, 16, 16, 16
MESSAGE = BODY + EDGE
ROWS = 64
GROUPS = ROWS // (2 * SEQ)
STEPS = CHANNELS // ROWS
AXES = ("seq", "ch")
VMEM = pl.BlockSpec(memory_space=pltpu.VMEM)
HBM = pl.BlockSpec(memory_space=pltpu.HBM)


def tables():
    step = 2.0 * math.pi
    tile = np.arange(TILES)[:, None, None]
    k1 = np.arange(BLOCKS)[None, :, None]
    block = np.arange(BLOCKS)[None, None, :]
    phase = ((TILES * block + tile) * (4 * k1 + 1) % (4 * TOKENS)) * (step / (4 * TOKENS))
    outer = np.concatenate([np.cos(phase), -np.sin(phase)], axis=1)
    lane = np.arange(LANES)[None, :]
    phase = lane * (np.arange(BLOCKS)[:, None] + 0.25) * (step / LENGTH)
    turn = np.stack([np.cos(phase), -np.sin(phase)])
    lane = np.arange(LANES)[None, :, None]
    k2 = np.arange(LANES)[None, None, :]
    phase = (lane * (TILES * k2 + tile) % TOKENS) * (step / TOKENS)
    cos, sin = np.cos(phase), np.sin(phase)
    inner = np.concatenate(
        [np.concatenate([cos, -sin], axis=2), np.concatenate([sin, cos], axis=2)], axis=1
    )
    narrow = ml_dtypes.bfloat16
    return dict(
        outer=outer.astype(narrow),
        outer_back=outer.swapaxes(1, 2).astype(narrow),
        turn=turn.astype(np.float32),
        inner=inner.astype(narrow),
    )


def dot(left, right):
    return jnp.dot(left, right, preferred_element_type=F32)


def dot_back(left, right):
    dims = (((1,), (1,)), ((), ()))
    return lax.dot_general(left, right, dims, preferred_element_type=F32)


def call(body, name, out_shape, scratch, in_specs, out_specs, flops, nbytes, limit=16):
    return pl.pallas_call(
        body,
        out_shape=out_shape,
        in_specs=in_specs,
        out_specs=out_specs,
        scratch_shapes=scratch,
        compiler_params=pltpu.CompilerParams(vmem_limit_bytes=limit * 1024 * 1024),
        cost_estimate=pl.CostEstimate(flops=flops, bytes_accessed=nbytes, transcendentals=0),
        name=name,
    )


def shape(dims, dtype):
    return jax.ShapeDtypeStruct(dims, dtype)


def lanes_of(x):
    return lax.broadcasted_iota(jnp.int32, x.shape, 1)


def columns(rows, tap_rows):
    tap_rows[...] = jnp.zeros(tap_rows.shape, F32)
    at = 0
    for row in rows:
        tap_rows[at : at + row.shape[0], :] = row
        at += row.shape[0]
    return tap_rows[...].T


def taps_of(cols, stream):
    return [cols[:, 3 * stream + i : 3 * stream + i + 1] for i in range(3)]


def causal(x, taps):
    return taps[0] * x + taps[1] * pltpu.roll(x, 1, 1) + taps[2] * pltpu.roll(x, 2, 1)


def with_edges(x, taps):
    back1, back2 = pltpu.roll(x, 1, 1), pltpu.roll(x, 2, 1)
    sums = taps[0] * x + taps[1] * back1 + taps[2] * back2
    lane = lax.broadcasted_iota(jnp.int32, (x.shape[0], LANES), 1)
    near = jnp.where(lane < 1, back1[:, :LANES], 0.0)
    far = jnp.where(lane < 2, back2[:, :LANES], 0.0)
    onward = taps[1] * near + taps[2] * far
    return sums, sums[:, :LANES] - onward, onward


def gate_body(
    q_ref, k_ref, v_ref, taps_ref, skip_ref, out_ref,
    taps_buf, skip_buf, q_buf, k_buf, v_buf, out_buf, tap_rows, cols_buf, rows, edge, small, sems, out_sems
):
    def small_copies():
        pairs = [(taps_ref, taps_buf), (skip_ref, skip_buf)]
        pairs += [
            (q_ref.at[:, pl.ds(i * (TOKENS - LANES), LANES)], q_buf.at[i]) for i in range(2)
        ]
        return [pltpu.make_async_copy(a, b, small.at[i]) for i, (a, b) in enumerate(pairs)]

    copies = []
    for step in range(STEPS):
        at = pl.ds(step * ROWS, ROWS)
        copies.append(
            [
                pltpu.make_async_copy(ref.at[at], buf.at[at], sems.at[i, step])
                for i, (ref, buf) in enumerate(((k_ref, k_buf), (v_ref, v_buf)))
            ]
        )
    first = small_copies()
    for copy in first:
        copy.start()
    for pair in copies:
        for copy in pair:
            copy.start()
    for copy in first:
        copy.wait()
    cols_buf[...] = columns([taps_buf[0], taps_buf[1], taps_buf[2], skip_buf[...]], tap_rows)
    out_copies = []
    for step in range(STEPS):
        for copy in copies[step]:
            copy.wait()
        at = slice(step * ROWS, (step + 1) * ROWS)
        cols = cols_buf[at, :]
        query_taps, key_taps, value_taps = (taps_of(cols, stream) for stream in range(3))
        key, key_own, key_onward = with_edges(k_buf[at, :].astype(F32), key_taps)
        value, value_own, value_onward = with_edges(v_buf[at, :].astype(F32), value_taps)
        query = jnp.concatenate([q_buf[0, at, :], q_buf[1, at, :]], axis=1).astype(F32)
        _, query_own, query_onward = with_edges(query, query_taps)
        gated = key * value
        for c in range(TILES):
            rows[pl.ds(c, ROWS, stride=TILES), :] = gated[:, c * LANES : (c + 1) * LANES]
        lane = lanes_of(key_own)
        parts = (
            jnp.where(lane < 2, key_own, pltpu.roll(query_own, 2, 1)),
            jnp.where(lane < 2, value_own, cols[:, 9:10]),
            jnp.where(lane < 2, key_onward, pltpu.roll(query_onward, 2, 1)),
            value_onward,
        )
        for m, part in enumerate(parts):
            edge[pl.ds(m, ROWS, stride=4), :] = part
        body = rows[...].reshape(ROWS // 2, BODY, LANES)
        message = jnp.concatenate([body, edge[...].reshape(ROWS // 2, EDGE, LANES)], axis=1)
        message = message.astype(BF16)
        for g in range(GROUPS):
            out_buf[:, step * GROUPS + g] = message[g * SEQ : (g + 1) * SEQ]
        place = pl.ds(step * GROUPS, GROUPS)
        out_copies.append(
            pltpu.make_async_copy(out_buf.at[:, place], out_ref.at[:, place], out_sems.at[step])
        )
        out_copies[-1].start()
    for copy in out_copies:
        copy.wait()


def gate(q, k, v, taps, skip):
    return call(
        gate_body,
        "gate",
        shape((SEQ, CH, MESSAGE, LANES), BF16),
        [
            pltpu.VMEM((3, 3, CHANNELS), F32),
            pltpu.VMEM((1, CHANNELS), F32),
            pltpu.VMEM((2, CHANNELS, LANES), BF16),
            pltpu.VMEM((CHANNELS, TOKENS), BF16),
            pltpu.VMEM((CHANNELS, TOKENS), BF16),
            pltpu.VMEM((SEQ, CH, MESSAGE, LANES), BF16),
            pltpu.VMEM((LANES, CHANNELS), F32),
            pltpu.VMEM((CHANNELS, LANES), F32),
            pltpu.VMEM((ROWS * TILES, LANES), F32),
            pltpu.VMEM((ROWS * 4, LANES), F32),
            pltpu.SemaphoreType.DMA((4,)),
            pltpu.SemaphoreType.DMA((2, STEPS)),
            pltpu.SemaphoreType.DMA((STEPS,)),
        ],
        [HBM] * 5,
        HBM,
        10**7,
        2 * 1024 * 1024,
        GATE_LIMIT,
    )(q, k, v, taps, skip)


def eight_points(re, im):
    half = math.sqrt(0.5)
    out_re, out_im = [None] * 8, [None] * 8

    def four_points(re, im, first):
        sum_re = [re[i] + re[i + 2] for i in range(2)]
        sum_im = [im[i] + im[i + 2] for i in range(2)]
        dif_re = [re[i] - re[i + 2] for i in range(2)]
        dif_im = [im[i] - im[i + 2] for i in range(2)]
        out_re[first], out_im[first] = sum_re[0] + sum_re[1], sum_im[0] + sum_im[1]
        out_re[first + 4], out_im[first + 4] = sum_re[0] - sum_re[1], sum_im[0] - sum_im[1]
        out_re[first + 2], out_im[first + 2] = dif_re[0] + dif_im[1], dif_im[0] - dif_re[1]
        out_re[first + 6], out_im[first + 6] = dif_re[0] - dif_im[1], dif_im[0] + dif_re[1]

    four_points([re[i] + re[i + 4] for i in range(4)], [im[i] + im[i + 4] for i in range(4)], 0)
    re = [re[i] - re[i + 4] for i in range(4)]
    im = [im[i] - im[i + 4] for i in range(4)]
    turned_re = [re[0], (re[1] + im[1]) * half, im[2], (im[3] - re[3]) * half]
    turned_im = [im[0], (im[1] - re[1]) * half, -re[2], (re[3] + im[3]) * -half]
    four_points(turned_re, turned_im, 1)
    return out_re, out_im


def forward(signals, outer_ref, turn_ref, section, turned):
    for c in range(TILES):
        section[c] = dot(outer_ref[c], signals[c])
    for row in range(0, BLOCKS, 16):
        turn_re, turn_im = turn_ref[0, row : row + 16, :], turn_ref[1, row : row + 16, :]
        for j in range(2):
            half = slice(j * LANES, (j + 1) * LANES)
            re = [section[c, row : row + 16, half] for c in range(TILES)]
            im = [section[c, BLOCKS + row : BLOCKS + row + 16, half] for c in range(TILES)]
            re, im = eight_points(re, im)
            at = slice(j * BLOCKS + row, j * BLOCKS + row + 16)
            for kc in range(TILES):
                turned[kc, at, :LANES] = (re[kc] * turn_re - im[kc] * turn_im).astype(BF16)
                turned[kc, at, LANES:] = (re[kc] * turn_im + im[kc] * turn_re).astype(BF16)


def beside_body(
    filt_ref, outer_ref, turn_ref, inner_ref, outer_back_ref, q_ref, k_ref, v_ref, taps_ref, skip_ref,
    spec_ref, query_ref, direct_ref, rows, section, turned, tap_rows, cols_buf
):
    del outer_back_ref
    rows[...] = filt_ref[...].astype(F32).reshape(2 * BLOCKS * TILES, LANES)
    signals = []
    for c in range(TILES):
        halves = [rows[pl.ds(j * TOKENS + c, BLOCKS, stride=TILES), :] for j in range(2)]
        signals.append(jnp.concatenate(halves, axis=1).astype(BF16))
    forward(signals, outer_ref, turn_ref, section, turned)
    for kc in range(TILES):
        spec_ref[kc] = (dot(turned[kc], inner_ref[kc]) * (1.0 / LENGTH)).astype(BF16)
    cols_buf[...] = columns([taps_ref[0], taps_ref[1], taps_ref[2], skip_ref[...]], tap_rows)
    for step in range(STEPS):
        at = slice(step * ROWS, (step + 1) * ROWS)
        cols = cols_buf[at, :]
        query, key, value = (
            causal(ref[at, :].astype(F32), taps_of(cols, stream))
            for stream, ref in enumerate((q_ref, k_ref, v_ref))
        )
        query_ref[at, :] = query
        direct_ref[at, :] = cols[:, 9:10] * (key * value).astype(BF16).astype(F32)


def beside(filt, consts, q, k, v, taps, skip):
    names = ("outer", "turn", "inner", "outer_back")
    return call(
        beside_body,
        "beside",
        (
            shape((TILES, 2 * BLOCKS, 2 * LANES), BF16),
            shape((CHANNELS, TOKENS), F32),
            shape((CHANNELS, TOKENS), F32),
        ),
        [
            pltpu.VMEM((2 * BLOCKS * TILES, LANES), F32),
            pltpu.VMEM((TILES, 2 * BLOCKS, 2 * LANES), F32),
            pltpu.VMEM((TILES, 2 * BLOCKS, 2 * LANES), BF16),
            pltpu.VMEM((LANES, CHANNELS), F32),
            pltpu.VMEM((CHANNELS, LANES), F32),
        ],
        [VMEM] * 10,
        (VMEM,) * 3,
        10**9,
        8 * 1024 * 1024,
        BESIDE_LIMIT,
    )(filt, *(consts[name] for name in names), q, k, v, taps, skip)


def conv_body(
    arrived_ref, spec_ref, outer_ref, outer_back_ref, turn_ref, inner_ref, out_ref,
    rows, section, turned, back, edges
):
    rows[:MESSAGE, :] = jnp.zeros((MESSAGE, LANES), F32)
    rows[MESSAGE:, :] = arrived_ref[...].astype(F32).reshape(BLOCKS * MESSAGE, LANES)

    def picked(row, before=0):
        return rows[pl.ds((1 - before) * MESSAGE + row, BLOCKS, stride=MESSAGE), :]

    signals = []
    for c in range(TILES):
        halves = [picked(j * TILES + c) for j in range(2)]
        if c == 0:
            for j in range(2):
                edge = BODY + 4 * j
                key_query = picked(edge) + picked(edge + 2, 1)
                value_skip = picked(edge + 1) + picked(edge + 3, 1)
                gated = (key_query * value_skip).astype(BF16).astype(F32)
                edges[0, j] = pltpu.roll(key_query, LANES - 2, 1)
                edges[1, j] = pltpu.roll(value_skip, LANES - 2, 1) * gated
                halves[j] = jnp.where(lanes_of(gated) < 2, gated, halves[j])
        signals.append(jnp.concatenate(halves, axis=1).astype(BF16))
    forward(signals, outer_ref, turn_ref, section, turned)
    for kc in range(TILES):
        spectrum = dot(turned[kc], inner_ref[kc])
        re, im = spectrum[:, :LANES], spectrum[:, LANES:]
        spec = spec_ref[kc].astype(F32)
        filt_re, filt_im = spec[:, :LANES], spec[:, LANES:]
        parts = [re * filt_re - im * filt_im, re * filt_im + im * filt_re]
        section[kc] = dot_back(jnp.concatenate(parts, axis=1).astype(BF16), inner_ref[kc])
    for row in range(0, BLOCKS, 16):
        turn_re, turn_im = turn_ref[0, row : row + 16, :], turn_ref[1, row : row + 16, :]
        for j in range(2):
            at = slice(j * BLOCKS + row, j * BLOCKS + row + 16)
            re, im = [], []
            for kc in range(TILES):
                part_re, part_im = section[kc, at, :LANES], section[kc, at, LANES:]
                re.append(part_re * turn_re + part_im * turn_im)
                im.append(part_im * turn_re - part_re * turn_im)
            im, re = eight_points(im, re)
            half = slice(j * LANES, (j + 1) * LANES)
            for c in range(TILES):
                back[c, row : row + 16, half] = re[c].astype(BF16)
                back[c, BLOCKS + row : BLOCKS + row + 16, half] = im[c].astype(BF16)
    for c in range(TILES):
        result = dot(outer_back_ref[c], back[c])
        for j in range(2):
            half = result[:, j * LANES : (j + 1) * LANES]
            if c == 0:
                start = edges[0, j] * (half.astype(BF16).astype(F32) + edges[1, j])
                half = jnp.where(lanes_of(half) < 2, start, half)
            rows[pl.ds(j * TILES + c, BLOCKS, stride=BODY), :] = half
    out_ref[...] = rows[: BLOCKS * BODY, :].reshape(BLOCKS, BODY, LANES).astype(BF16)


def conv(arrived, spec, consts):
    names = ("outer", "outer_back", "turn", "inner")
    return call(
        conv_body,
        "conv",
        shape((BLOCKS, BODY, LANES), BF16),
        [
            pltpu.VMEM(((BLOCKS + 1) * MESSAGE, LANES), F32),
            pltpu.VMEM((TILES, 2 * BLOCKS, 2 * LANES), F32),
            pltpu.VMEM((TILES, 2 * BLOCKS, 2 * LANES), BF16),
            pltpu.VMEM((TILES, 2 * BLOCKS, 2 * LANES), BF16),
            pltpu.VMEM((2, 2, BLOCKS, LANES), F32),
        ],
        [VMEM] * 6,
        VMEM,
        10**9,
        8 * 1024 * 1024,
        CONV_LIMIT,
    )(arrived, spec, *(consts[name] for name in names))


def final_body(returned_ref, query_ref, direct_ref, out_ref, rows, out_buf, sems):
    per_group = ROWS * TILES // GROUPS
    copies = []
    for step in range(STEPS):
        at = slice(step * ROWS, (step + 1) * ROWS)
        for g in range(GROUPS):
            message = returned_ref[:, step * GROUPS + g].astype(F32)
            rows[g * per_group : (g + 1) * per_group, :] = message.reshape(per_group, LANES)
        for c in range(TILES):
            lanes = slice(c * LANES, (c + 1) * LANES)
            long_result = rows[pl.ds(c, ROWS, stride=TILES), :]
            mixed = query_ref[at, lanes] * (long_result + direct_ref[at, lanes])
            if c == 0:
                mixed = jnp.where(lanes_of(mixed) < 2, long_result, mixed)
            out_buf[at, lanes] = mixed.astype(BF16)
        place = pl.ds(step * ROWS, ROWS)
        copies.append(pltpu.make_async_copy(out_buf.at[place], out_ref.at[place], sems.at[step]))
        copies[-1].start()
    for copy in copies:
        copy.wait()


def final(returned, query, direct_term):
    return call(
        final_body,
        "final",
        shape((CHANNELS, TOKENS), BF16),
        [
            pltpu.VMEM((ROWS * TILES, LANES), F32),
            pltpu.VMEM((CHANNELS, TOKENS), BF16),
            pltpu.SemaphoreType.DMA((STEPS,)),
        ],
        [VMEM] * 3,
        HBM,
        10**6,
        2 * 1024 * 1024,
        FINAL_LIMIT,
    )(returned, query, direct_term)


def exchange(messages):
    return lax.all_to_all(messages, AXES, split_axis=0, concat_axis=0, tiled=True)


def shards(consts, q, k, v, short_taps, long_filter, skip_gain):
    consts = {name: jnp.asarray(table) for name, table in consts.items()}
    skip = skip_gain[None]
    messages = gate(q, k, v, short_taps, skip)
    messages, q, k, v, long_filter = lax.optimization_barrier((messages, q, k, v, long_filter))
    arrived = exchange(messages.reshape(BLOCKS, MESSAGE, LANES))
    filt = long_filter.reshape(2, BLOCKS * TILES, LANES)
    spec, query, direct_term = beside(filt, consts, q, k, v, short_taps, skip)
    results = conv(arrived, spec, consts)
    returned = exchange(results).reshape(SEQ, CH, BODY, LANES)
    return final(returned, query, direct_term)


def solution(mesh):
    tokens = P(None, AXES)
    placed = (tokens, tokens, tokens, P(), P("ch", "seq", None, None), P())
    return jax.shard_map(
        functools.partial(shards, tables()),
        mesh=mesh,
        in_specs=placed,
        out_specs=tokens,
        check_vma=False,
    )
```

time: 67.7 us -> 55.4 us (0.82)
  the two profiles are of different devices: /device:TPU:2 before, /device:TPU:1 now
where the time goes in v2:
time: 55.4 us; the launch traced here: 55 us
  blocking collectives  17.7 us (32%)
  starting transfers between devices  11.5 us (21%)
  Pallas kernels  10.9 us (20%)
  local copies, waits for them, and re-layouts  8.14 us (15%)
  waiting for transfers between devices  6.62 us (12%)
    all_to_all x1, blocking collectives, exchange(): lax.all_to_all(messages, AXES, split_axis=0, concat_axis=0, tiled=True)  17.7 us
    all_to_all x1, starting transfers between devices, exchange(): lax.all_to_all(messages, AXES, split_axis=0, concat_axis=0, tiled=True)  11.5 us
    unnamed x31, local copies, waits for them, and re-layouts  8.14 us
    all_to_all x1, waiting for transfers between devices, exchange(): lax.all_to_all(messages, AXES, split_axis=0, concat_axis=0, tiled=True)  6.62 us
    pallas_call x1, Pallas kernels, gate(): call(gate_body, 'gate', shape((SEQ, CH, MESSAGE, LANES), BF16), [pltpu.VM...  4.15 us
    pallas_call x1, Pallas kernels, beside(): call(beside_body, 'beside', (shape((TILES, 2 * BLOCKS, 2 * LANES), BF16),...  2.93 us
    pallas_call x1, Pallas kernels, conv(): call(conv_body, 'conv', shape((BLOCKS, BODY, LANES), BF16), [pltpu.VMEM((...  2.77 us
  transfers between devices with their start and end apart: 1, of which 1 were waited for; matrix products, arithmetic and copies ran while one was open for 2% of the time, Pallas kernels for 5%

profile of v2, /device:TPU:1, one launch (start us, length us, event | category | flops | bytes accessed | tf_op | source)
XLA Modules:
  0.0 55.0 jit_solution(15462474723025356307)
XLA Ops:
  0.0 4.1 %gate.1 = bf16[8,16,24,128]{3,2,1,0:T(8,128)(2,1)} custom-call(bf16[256,1024]{1,0:T(8,128)(2,1)} %q_ref.2, bf16[256,1024]{1,0:T(8,128)(2,1)} %k_ref.2, bf16[256,1024]{1,0:T(8,128)(2,1)} %v_ref.2, f32[3,3,256]{2,1,0:T(4,128)} %taps_ref.3, f32[1,256]{1,0:T(1,128)} %bitcast.10), custom_call_target="tpu_custom_call" | custom-call | flops 10000000 | bytes 2097152 | tf_op jit(solution)/shard_map/gate/pallas_call | solution.py:185
  4.2 0.0 copy-start
  4.2 0.0 copy-start.3
  4.2 11.5 %all-to-all-start = ((bf16[128,24,128]{2,1,0:T(8,128)(2,1)}), bf16[128,24,128]{2,1,0:T(8,128)(2,1)S(1)}, u32[]{:S(2)}, u32[]{:S(2)}) async-start(bf16[128,24,128]{2,1,0:T(8,128)(2,1)} %bitcast.12), calls=%async_computation | async-start | bytes 1572864 | tf_op jit(solution)/shard_map/all_to_all | solution.py:419
  15.7 0.0 copy-start.1
  15.7 0.0 copy-start.2
  15.7 1.2 %copy.13 = bf16[1,2,1024,128]{3,2,1,0:T(8,128)(2,1)S(1)} copy(bf16[1,2,1024,128]{3,1,2,0:T(2,128)(2,1)} %bitcast.13) | data formatting | bytes 1048576
  16.9 0.0 copy-start.14
  16.9 0.0 copy-done.12
  16.9 0.0 copy-done.13
  17.0 0.0 copy-done
  17.0 0.1 copy-done.2
  17.1 0.6 %copy-done.14 = f32[256]{0:T(256)S(1)} copy-done((f32[256]{0:T(256)S(1)}, f32[256]{0:T(256)}, u32[]{:S(2)}) %copy-start.14) | copy-done | bytes 1048
  17.6 1.0 %copy-done.4 = bf16[256,1024]{1,0:T(8,128)(2,1)S(1)} copy-done((bf16[256,1024]{1,0:T(8,128)(2,1)S(1)}, bf16[256,1024]{1,0:T(8,128)(2,1)}, u32[]{:S(2)}) %copy-start.4) | copy-done | bytes 524312
  18.7 1.0 %copy-done.5 = bf16[256,1024]{1,0:T(8,128)(2,1)S(1)} copy-done((bf16[256,1024]{1,0:T(8,128)(2,1)S(1)}, bf16[256,1024]{1,0:T(8,128)(2,1)}, u32[]{:S(2)}) %copy-start.5) | copy-done | bytes 524312
  19.7 2.9 %beside.1 = (bf16[8,256,256]{2,1,0:T(8,128)(2,1)S(1)}, f32[256,1024]{1,0:T(8,128)S(1)}, f32[256,1024]{1,0:T(8,128)S(1)}) custom-call(bf16[2,1024,128]{2,1,0:T(8,128)(2,1)S(1)} %bitcast.9, bf16[8,256,128]{2,1,0:T(8,128)(2,1)S(1)} %copy-done.2, f32[2,128,128]{2,1,0:T(8,128)S(1)} %copy-done.12, bf16[8,256,256]{2,1,0:T(8,128)(2,1)S(1)} %copy-done, ...), custom_call_target="tpu_custom_call" | custom-call | flops 1000000000 | bytes 8388608 | tf_op jit(solution)/shard_map/beside/pallas_call | solution.py:278
  22.7 1.0 %copy-done.6 = f32[256,1024]{1,0:T(8,128)} copy-done((f32[256,1024]{1,0:T(8,128)}, f32[256,1024]{1,0:T(8,128)S(1)}, u32[]{:S(2)}) %copy-start.6) | copy-done | bytes 1048600
  23.6 1.0 %copy-done.8 = f32[256,1024]{1,0:T(8,128)} copy-done((f32[256,1024]{1,0:T(8,128)}, f32[256,1024]{1,0:T(8,128)S(1)}, u32[]{:S(2)}) %copy-start.8) | copy-done | bytes 1048600
  24.6 1.0 %copy-done.10 = bf16[8,256,256]{2,1,0:T(8,128)(2,1)} copy-done((bf16[8,256,256]{2,1,0:T(8,128)(2,1)}, bf16[8,256,256]{2,1,0:T(8,128)(2,1)S(1)}, u32[]{:S(2)}) %copy-start.10) | copy-done | bytes 1048600
  25.6 6.6 %all-to-all-done.arrived_ref = bf16[128,24,128]{2,1,0:T(8,128)(2,1)S(1)} async-done(((bf16[128,24,128]{2,1,0:T(8,128)(2,1)}), bf16[128,24,128]{2,1,0:T(8,128)(2,1)S(1)}, u32[]{:S(2)}, u32[]{:S(2)}) %all-to-all-start) | async-done | bytes 786464 | tf_op jit(solution)/shard_map/all_to_all | solution.py:419
  32.2 1.2 %copy-done.11 = bf16[8,256,256]{2,1,0:T(8,128)(2,1)S(1)} copy-done((bf16[8,256,256]{2,1,0:T(8,128)(2,1)S(1)}, bf16[8,256,256]{2,1,0:T(8,128)(2,1)}, u32[]{:S(2)}) %copy-start.11) | copy-done | bytes 1048600
  33.5 2.8 %conv.1 = bf16[128,16,128]{2,1,0:T(8,128)(2,1)S(1)} custom-call(bf16[128,24,128]{2,1,0:T(8,128)(2,1)S(1)} %all-to-all-done.arrived_ref, bf16[8,256,256]{2,1,0:T(8,128)(2,1)S(1)} %copy-done.11, bf16[8,256,128]{2,1,0:T(8,128)(2,1)S(1)} %copy-done.2, bf16[8,128,256]{2,1,0:T(8,128)(2,1)S(1)} %copy-done.1, f32[2,128,128]{2,1,0:T(8,128)S(1)} %copy-done.12, ...), custom_call_target="tpu_custom_call" | custom-call | flops 1000000000 | bytes 8388608 | tf_op jit(solution)/shard_map/conv/pallas_call | solution.py:359
  36.2 17.7 %all_to_all.10 = bf16[128,16,128]{2,1,0:T(8,128)(2,1)S(1)} all-to-all(bf16[128,16,128]{2,1,0:T(8,128)(2,1)S(1)} %conv.1), channel_id=1, replica_groups=mesh['seq'=8,'ch'=16] {'seq','ch'}, dimensions={0} | all-to-all | bytes 1048576 | tf_op jit(solution)/shard_map/all_to_all | solution.py:419
  54.0 1.1 %final.1 = bf16[256,1024]{1,0:T(8,128)(2,1)} custom-call(bf16[8,16,16,128]{3,2,1,0:T(8,128)(2,1)S(1)} %bitcast.8, f32[256,1024]{1,0:T(8,128)S(1)} %copy-done.7, f32[256,1024]{1,0:T(8,128)S(1)} %copy-done.9), custom_call_target="tpu_custom_call" | custom-call | flops 1000000 | bytes 2097152 | tf_op jit(solution)/shard_map/final/pallas_call | solution.py:401
  (14 shorter events, 0.0 us)
Async XLA Ops:
  0.0 16.9 %copy-start.12 = (f32[2,128,128]{2,1,0:T(8,128)S(1)}, f32[2,128,128]{2,1,0:T(8,128)}, u32[]{:S(2)}) copy-start(f32[2,128,128]{2,1,0:T(8,128)} %constant.10.clone.turn_ref) | copy-start | bytes 393220
  0.0 16.9 %copy-start.13 = (f32[3,3,256]{2,1,0:T(4,128)S(1)}, f32[3,3,256]{2,1,0:T(4,128)}, u32[]{:S(2)}) copy-start(f32[3,3,256]{2,1,0:T(4,128)} %taps_ref.3) | copy-start | bytes 27652
  4.2 12.8 %copy-start = (bf16[8,256,256]{2,1,0:T(8,128)(2,1)S(1)}, bf16[8,256,256]{2,1,0:T(8,128)(2,1)}, u32[]{:S(2)}) copy-start(bf16[8,256,256]{2,1,0:T(8,128)(2,1)} %constant.11.clone.inner_ref) | copy-start | bytes 3145732
  4.2 12.8 %copy-start.3 = (bf16[256,1024]{1,0:T(8,128)(2,1)S(1)}, bf16[256,1024]{1,0:T(8,128)(2,1)}, u32[]{:S(2)}) copy-start(bf16[256,1024]{1,0:T(8,128)(2,1)} %q_ref.2) | copy-start | bytes 1572868
  4.2 28.0 %all-to-all-start = ((bf16[128,24,128]{2,1,0:T(8,128)(2,1)}), bf16[128,24,128]{2,1,0:T(8,128)(2,1)S(1)}, u32[]{:S(2)}, u32[]{:S(2)}) async-start(bf16[128,24,128]{2,1,0:T(8,128)(2,1)} %bitcast.12), calls=%async_computation | async-start | bytes 1572864 | tf_op jit(solution)/shard_map/all_to_all | solution.py:419
  15.7 1.3 %copy-start.1 = (bf16[8,128,256]{2,1,0:T(8,128)(2,1)S(1)}, bf16[8,128,256]{2,1,0:T(8,128)(2,1)}, u32[]{:S(2)}) copy-start(bf16[8,128,256]{2,1,0:T(8,128)(2,1)} %constant.9.clone.outer_back_ref) | copy-start | bytes 1572868
  15.7 1.4 %copy-start.2 = (bf16[8,256,128]{2,1,0:T(8,128)(2,1)S(1)}, bf16[8,256,128]{2,1,0:T(8,128)(2,1)}, u32[]{:S(2)}) copy-start(bf16[8,256,128]{2,1,0:T(8,128)(2,1)} %constant.8.clone.outer_ref) | copy-start | bytes 1572868
  16.9 0.7 %copy-start.14 = (f32[256]{0:T(256)S(1)}, f32[256]{0:T(256)}, u32[]{:S(2)}) copy-start(f32[256]{0:T(256)} %param.15) | copy-start | bytes 3076
  17.6 1.0 %copy-start.4 = (bf16[256,1024]{1,0:T(8,128)(2,1)S(1)}, bf16[256,1024]{1,0:T(8,128)(2,1)}, u32[]{:S(2)}) copy-start(bf16[256,1024]{1,0:T(8,128)(2,1)} %k_ref.2) | copy-start | bytes 1572868
  18.7 1.0 %copy-start.5 = (bf16[256,1024]{1,0:T(8,128)(2,1)S(1)}, bf16[256,1024]{1,0:T(8,128)(2,1)}, u32[]{:S(2)}) copy-start(bf16[256,1024]{1,0:T(8,128)(2,1)} %v_ref.2) | copy-start | bytes 1572868
  22.7 1.0 %copy-start.6 = (f32[256,1024]{1,0:T(8,128)}, f32[256,1024]{1,0:T(8,128)S(1)}, u32[]{:S(2)}) copy-start(f32[256,1024]{1,0:T(8,128)S(1)} %get-tuple-element.19.query_ref) | copy-start | bytes 3145732
  23.6 1.0 %copy-start.8 = (f32[256,1024]{1,0:T(8,128)}, f32[256,1024]{1,0:T(8,128)S(1)}, u32[]{:S(2)}) copy-start(f32[256,1024]{1,0:T(8,128)S(1)} %get-tuple-element.20.direct_ref) | copy-start | bytes 3145732
  24.6 1.0 %copy-start.10 = (bf16[8,256,256]{2,1,0:T(8,128)(2,1)}, bf16[8,256,256]{2,1,0:T(8,128)(2,1)S(1)}, u32[]{:S(2)}) copy-start(bf16[8,256,256]{2,1,0:T(8,128)(2,1)S(1)} %get-tuple-element.18.spec_ref) | copy-start | bytes 3145732
  32.2 1.2 %copy-start.11 = (bf16[8,256,256]{2,1,0:T(8,128)(2,1)S(1)}, bf16[8,256,256]{2,1,0:T(8,128)(2,1)}, u32[]{:S(2)}) copy-start(bf16[8,256,256]{2,1,0:T(8,128)(2,1)} %copy-done.10) | copy-start | bytes 3145732
  33.5 20.5 %copy-start.9 = (f32[256,1024]{1,0:T(8,128)S(1)}, f32[256,1024]{1,0:T(8,128)}, u32[]{:S(2)}) copy-start(f32[256,1024]{1,0:T(8,128)} %copy-done.8) | copy-start | bytes 3145732
  36.2 17.7 %copy-start.7 = (f32[256,1024]{1,0:T(8,128)S(1)}, f32[256,1024]{1,0:T(8,128)}, u32[]{:S(2)}) copy-start(f32[256,1024]{1,0:T(8,128)} %copy-done.6) | copy-start | bytes 3145732

commit v3 on v2

--- a/solution.py
+++ b/solution.py
@@ -21,13 +21,12 @@
 SEQ = 8
 CH = 16
 BODY = 2 * TILES
-EDGE = 8
-GATE_LIMIT, BESIDE_LIMIT, CONV_LIMIT, FINAL_LIMIT = 60, 16, 16, 16
-MESSAGE = BODY + EDGE
+WIDTH = TILES + 1
+GATE_LIMIT, BESIDE_LIMIT, CONV_LIMIT, FINAL_LIMIT = 60, 60, 51, 16
 ROWS = 64
-GROUPS = ROWS // (2 * SEQ)
 STEPS = CHANNELS // ROWS
 AXES = ("seq", "ch")
+OWNERS = ("ch", "seq")
 VMEM = pl.BlockSpec(memory_space=pltpu.VMEM)
 HBM = pl.BlockSpec(memory_space=pltpu.HBM)
 
@@ -36,7 +35,7 @@
     step = 2.0 * math.pi
     tile = np.arange(TILES)[:, None, None]
     k1 = np.arange(BLOCKS)[None, :, None]
-    block = np.arange(BLOCKS)[None, None, :]
+    block = np.arange(BLOCKS).reshape(SEQ, CH).T.reshape(1, 1, BLOCKS)
     phase = ((TILES * block + tile) * (4 * k1 + 1) % (4 * TOKENS)) * (step / (4 * TOKENS))
     outer = np.concatenate([np.cos(phase), -np.sin(phase)], axis=1)
     lane = np.arange(LANES)[None, :]
@@ -117,7 +116,7 @@
 
 def gate_body(
     q_ref, k_ref, v_ref, taps_ref, skip_ref, out_ref,
-    taps_buf, skip_buf, q_buf, k_buf, v_buf, out_buf, tap_rows, cols_buf, rows, edge, small, sems, out_sems
+    taps_buf, skip_buf, q_buf, k_buf, v_buf, tap_rows, cols_buf, rows, small, sems
 ):
     def small_copies():
         pairs = [(taps_ref, taps_buf), (skip_ref, skip_buf)]
@@ -144,7 +143,6 @@
     for copy in first:
         copy.wait()
     cols_buf[...] = columns([taps_buf[0], taps_buf[1], taps_buf[2], skip_buf[...]], tap_rows)
-    out_copies = []
     for step in range(STEPS):
         for copy in copies[step]:
             copy.wait()
@@ -157,52 +155,35 @@
         _, query_own, query_onward = with_edges(query, query_taps)
         gated = key * value
         for c in range(TILES):
-            rows[pl.ds(c, ROWS, stride=TILES), :] = gated[:, c * LANES : (c + 1) * LANES]
+            rows[pl.ds(c, ROWS, stride=WIDTH), :] = gated[:, c * LANES : (c + 1) * LANES]
         lane = lanes_of(key_own)
-        parts = (
-            jnp.where(lane < 2, key_own, pltpu.roll(query_own, 2, 1)),
-            jnp.where(lane < 2, value_own, cols[:, 9:10]),
-            jnp.where(lane < 2, key_onward, pltpu.roll(query_onward, 2, 1)),
-            value_onward,
-        )
-        for m, part in enumerate(parts):
-            edge[pl.ds(m, ROWS, stride=4), :] = part
-        body = rows[...].reshape(ROWS // 2, BODY, LANES)
-        message = jnp.concatenate([body, edge[...].reshape(ROWS // 2, EDGE, LANES)], axis=1)
-        message = message.astype(BF16)
-        for g in range(GROUPS):
-            out_buf[:, step * GROUPS + g] = message[g * SEQ : (g + 1) * SEQ]
-        place = pl.ds(step * GROUPS, GROUPS)
-        out_copies.append(
-            pltpu.make_async_copy(out_buf.at[:, place], out_ref.at[:, place], out_sems.at[step])
-        )
-        out_copies[-1].start()
-    for copy in out_copies:
-        copy.wait()
+        own = jnp.where(lane < 2, key_own, pltpu.roll(query_own, 2, 1))
+        own_value = pltpu.roll(jnp.where(lane < 2, value_own, cols[:, 9:10]), 4, 1)
+        onward = key_onward + pltpu.roll(query_onward, 2, 1) + pltpu.roll(value_onward, 4, 1)
+        edge = jnp.where(lane < 8, own_value, pltpu.roll(onward, 8, 1))
+        rows[pl.ds(TILES, ROWS, stride=WIDTH), :] = jnp.where(lane < 4, own, edge)
+        out_ref[step * ROWS * WIDTH : (step + 1) * ROWS * WIDTH, :] = rows[...].astype(BF16)
 
 
 def gate(q, k, v, taps, skip):
     return call(
         gate_body,
         "gate",
-        shape((SEQ, CH, MESSAGE, LANES), BF16),
+        shape((CHANNELS * WIDTH, LANES), BF16),
         [
             pltpu.VMEM((3, 3, CHANNELS), F32),
             pltpu.VMEM((1, CHANNELS), F32),
             pltpu.VMEM((2, CHANNELS, LANES), BF16),
             pltpu.VMEM((CHANNELS, TOKENS), BF16),
             pltpu.VMEM((CHANNELS, TOKENS), BF16),
-            pltpu.VMEM((SEQ, CH, MESSAGE, LANES), BF16),
             pltpu.VMEM((LANES, CHANNELS), F32),
             pltpu.VMEM((CHANNELS, LANES), F32),
-            pltpu.VMEM((ROWS * TILES, LANES), F32),
-            pltpu.VMEM((ROWS * 4, LANES), F32),
+            pltpu.VMEM((ROWS * WIDTH, LANES), F32),
             pltpu.SemaphoreType.DMA((4,)),
             pltpu.SemaphoreType.DMA((2, STEPS)),
-            pltpu.SemaphoreType.DMA((STEPS,)),
         ],
         [HBM] * 5,
-        HBM,
+        VMEM,
         10**7,
         2 * 1024 * 1024,
         GATE_LIMIT,
@@ -249,49 +230,101 @@
 
 
 def beside_body(
-    filt_ref, outer_ref, turn_ref, inner_ref, outer_back_ref, q_ref, k_ref, v_ref, taps_ref, skip_ref,
-    spec_ref, query_ref, direct_ref, rows, section, turned, tap_rows, cols_buf
+    filt_ref, outer_ref, turn_ref, inner_ref, q_ref, k_ref, v_ref, taps_ref, skip_ref,
+    spec_ref, query_ref, direct_ref,
+    filt_buf, outer_buf, turn_buf, inner_buf, streams, taps_buf, skip_buf, spec_buf, query_buf, direct_buf,
+    rows, section, turned, tap_rows, cols_buf, small, in_sems, table_sems, out_sems, spec_sems
 ):
-    del outer_back_ref
-    rows[...] = filt_ref[...].astype(F32).reshape(2 * BLOCKS * TILES, LANES)
-    signals = []
-    for c in range(TILES):
-        halves = [rows[pl.ds(j * TOKENS + c, BLOCKS, stride=TILES), :] for j in range(2)]
-        signals.append(jnp.concatenate(halves, axis=1).astype(BF16))
-    forward(signals, outer_ref, turn_ref, section, turned)
-    for kc in range(TILES):
-        spec_ref[kc] = (dot(turned[kc], inner_ref[kc]) * (1.0 / LENGTH)).astype(BF16)
-    cols_buf[...] = columns([taps_ref[0], taps_ref[1], taps_ref[2], skip_ref[...]], tap_rows)
+    first = [
+        pltpu.make_async_copy(taps_ref, taps_buf, small.at[0]),
+        pltpu.make_async_copy(skip_ref, skip_buf, small.at[1]),
+    ]
+    places = [pl.ds(step * ROWS, ROWS) for step in range(STEPS)]
+    copies = [
+        [
+            pltpu.make_async_copy(ref.at[place], streams.at[i, place], in_sems.at[i, step])
+            for i, ref in enumerate((q_ref, k_ref, v_ref))
+        ]
+        for step, place in enumerate(places)
+    ]
+    pairs = ((filt_ref, filt_buf), (outer_ref, outer_buf), (turn_ref, turn_buf), (inner_ref, inner_buf))
+    tables_in = [
+        pltpu.make_async_copy(a, b, table_sems.at[i]) for i, (a, b) in enumerate(pairs)
+    ]
+    for copy in first + [copy for group in copies for copy in group] + tables_in:
+        copy.start()
+    for copy in first:
+        copy.wait()
+    out_copies = []
+    cols_buf[...] = columns([taps_buf[0], taps_buf[1], taps_buf[2], skip_buf[...]], tap_rows)
     for step in range(STEPS):
+        for copy in copies[step]:
+            copy.wait()
         at = slice(step * ROWS, (step + 1) * ROWS)
         cols = cols_buf[at, :]
         query, key, value = (
-            causal(ref[at, :].astype(F32), taps_of(cols, stream))
-            for stream, ref in enumerate((q_ref, k_ref, v_ref))
+            causal(streams[i, at, :].astype(F32), taps_of(cols, i)) for i in range(3)
         )
-        query_ref[at, :] = query
-        direct_ref[at, :] = cols[:, 9:10] * (key * value).astype(BF16).astype(F32)
+        query_buf[at, :] = query
+        direct_buf[at, :] = cols[:, 9:10] * (key * value).astype(BF16).astype(F32)
+        for i, (buf, ref) in enumerate(((query_buf, query_ref), (direct_buf, direct_ref))):
+            out_copies.append(
+                pltpu.make_async_copy(buf.at[places[step]], ref.at[places[step]], out_sems.at[i, step])
+            )
+            out_copies[-1].start()
+    for copy in tables_in:
+        copy.wait()
+    rows[...] = filt_buf[...].astype(F32)
+    signals = []
+    for c in range(TILES):
+        halves = []
+        for j in range(2):
+            parts = [
+                rows[pl.ds(2 * (g * TILES + c) + j, SEQ, stride=2 * TILES * CH), :]
+                for g in range(CH)
+            ]
+            halves.append(jnp.concatenate(parts, axis=0))
+        signals.append(jnp.concatenate(halves, axis=1).astype(BF16))
+    forward(signals, outer_buf, turn_buf, section, turned)
+    for kc in range(TILES):
+        spec_buf[kc] = (dot(turned[kc], inner_buf[kc]) * (1.0 / LENGTH)).astype(BF16)
+        out_copies.append(pltpu.make_async_copy(spec_buf.at[kc], spec_ref.at[kc], spec_sems.at[kc]))
+        out_copies[-1].start()
+    for copy in out_copies:
+        copy.wait()
 
 
 def beside(filt, consts, q, k, v, taps, skip):
-    names = ("outer", "turn", "inner", "outer_back")
+    names = ("outer", "turn", "inner")
+    spec = (TILES, 2 * BLOCKS, 2 * LANES)
     return call(
         beside_body,
         "beside",
-        (
-            shape((TILES, 2 * BLOCKS, 2 * LANES), BF16),
-            shape((CHANNELS, TOKENS), F32),
-            shape((CHANNELS, TOKENS), F32),
-        ),
-        [
+        (shape(spec, BF16), shape((CHANNELS, TOKENS), F32), shape((CHANNELS, TOKENS), F32)),
+        [
+            pltpu.VMEM((2 * BLOCKS * TILES, LANES), BF16),
+            pltpu.VMEM((TILES, 2 * BLOCKS, LANES), BF16),
+            pltpu.VMEM((2, BLOCKS, LANES), F32),
+            pltpu.VMEM((TILES, 2 * LANES, 2 * LANES), BF16),
+            pltpu.VMEM((3, CHANNELS, TOKENS), BF16),
+            pltpu.VMEM((3, 3, CHANNELS), F32),
+            pltpu.VMEM((1, CHANNELS), F32),
+            pltpu.VMEM(spec, BF16),
+            pltpu.VMEM((CHANNELS, TOKENS), F32),
+            pltpu.VMEM((CHANNELS, TOKENS), F32),
             pltpu.VMEM((2 * BLOCKS * TILES, LANES), F32),
-            pltpu.VMEM((TILES, 2 * BLOCKS, 2 * LANES), F32),
-            pltpu.VMEM((TILES, 2 * BLOCKS, 2 * LANES), BF16),
+            pltpu.VMEM(spec, F32),
+            pltpu.VMEM(spec, BF16),
             pltpu.VMEM((LANES, CHANNELS), F32),
             pltpu.VMEM((CHANNELS, LANES), F32),
+            pltpu.SemaphoreType.DMA((2,)),
+            pltpu.SemaphoreType.DMA((3, STEPS)),
+            pltpu.SemaphoreType.DMA((4,)),
+            pltpu.SemaphoreType.DMA((2, STEPS)),
+            pltpu.SemaphoreType.DMA((TILES,)),
         ],
-        [VMEM] * 10,
-        (VMEM,) * 3,
+        [HBM] * 9,
+        (HBM,) * 3,
         10**9,
         8 * 1024 * 1024,
         BESIDE_LIMIT,
@@ -300,35 +333,49 @@
 
 def conv_body(
     arrived_ref, spec_ref, outer_ref, outer_back_ref, turn_ref, inner_ref, out_ref,
-    rows, section, turned, back, edges
+    rows, section, turned, back, edges, inner_buf, spec_buf, sems
 ):
-    rows[:MESSAGE, :] = jnp.zeros((MESSAGE, LANES), F32)
-    rows[MESSAGE:, :] = arrived_ref[...].astype(F32).reshape(BLOCKS * MESSAGE, LANES)
-
-    def picked(row, before=0):
-        return rows[pl.ds((1 - before) * MESSAGE + row, BLOCKS, stride=MESSAGE), :]
+    copies = [
+        [
+            pltpu.make_async_copy(ref.at[kc], buf.at[kc], sems.at[i, kc])
+            for i, (ref, buf) in enumerate(((inner_ref, inner_buf), (spec_ref, spec_buf)))
+        ]
+        for kc in range(TILES)
+    ]
+    for pair in copies:
+        for copy in pair:
+            copy.start()
+    rows[...] = arrived_ref[...].astype(F32)
+
+    def arrived(j, c):
+        return rows[pl.ds(j * WIDTH + c, BLOCKS, stride=2 * WIDTH), :]
 
     signals = []
     for c in range(TILES):
-        halves = [picked(j * TILES + c) for j in range(2)]
+        halves = [arrived(j, c) for j in range(2)]
         if c == 0:
             for j in range(2):
-                edge = BODY + 4 * j
-                key_query = picked(edge) + picked(edge + 2, 1)
-                value_skip = picked(edge + 1) + picked(edge + 3, 1)
-                gated = (key_query * value_skip).astype(BF16).astype(F32)
-                edges[0, j] = pltpu.roll(key_query, LANES - 2, 1)
-                edges[1, j] = pltpu.roll(value_skip, LANES - 2, 1) * gated
+                edge = arrived(j, TILES)
+                last = edge[BLOCKS - SEQ :]
+                step = lax.broadcasted_iota(jnp.int32, last.shape, 0)
+                last = jnp.where(step == 0, 0.0, pltpu.roll(last, 1, 0))
+                before = jnp.concatenate([last, edge[: BLOCKS - SEQ]], axis=0)
+                total = edge + pltpu.roll(before, LANES - 8, 1)
+                gated = (total * pltpu.roll(total, LANES - 4, 1)).astype(BF16).astype(F32)
+                edges[0, j] = pltpu.roll(total, LANES - 2, 1)
+                edges[1, j] = pltpu.roll(total, LANES - 6, 1) * gated
                 halves[j] = jnp.where(lanes_of(gated) < 2, gated, halves[j])
         signals.append(jnp.concatenate(halves, axis=1).astype(BF16))
     forward(signals, outer_ref, turn_ref, section, turned)
     for kc in range(TILES):
-        spectrum = dot(turned[kc], inner_ref[kc])
+        for copy in copies[kc]:
+            copy.wait()
+        spectrum = dot(turned[kc], inner_buf[kc])
         re, im = spectrum[:, :LANES], spectrum[:, LANES:]
-        spec = spec_ref[kc].astype(F32)
+        spec = spec_buf[kc].astype(F32)
         filt_re, filt_im = spec[:, :LANES], spec[:, LANES:]
         parts = [re * filt_re - im * filt_im, re * filt_im + im * filt_re]
-        section[kc] = dot_back(jnp.concatenate(parts, axis=1).astype(BF16), inner_ref[kc])
+        section[kc] = dot_back(jnp.concatenate(parts, axis=1).astype(BF16), inner_buf[kc])
     for row in range(0, BLOCKS, 16):
         turn_re, turn_im = turn_ref[0, row : row + 16, :], turn_ref[1, row : row + 16, :]
         for j in range(2):
@@ -361,13 +408,16 @@
         "conv",
         shape((BLOCKS, BODY, LANES), BF16),
         [
-            pltpu.VMEM(((BLOCKS + 1) * MESSAGE, LANES), F32),
+            pltpu.VMEM((BLOCKS * 2 * WIDTH, LANES), F32),
             pltpu.VMEM((TILES, 2 * BLOCKS, 2 * LANES), F32),
             pltpu.VMEM((TILES, 2 * BLOCKS, 2 * LANES), BF16),
             pltpu.VMEM((TILES, 2 * BLOCKS, 2 * LANES), BF16),
             pltpu.VMEM((2, 2, BLOCKS, LANES), F32),
+            pltpu.VMEM((TILES, 2 * LANES, 2 * LANES), BF16),
+            pltpu.VMEM((TILES, 2 * BLOCKS, 2 * LANES), BF16),
+            pltpu.SemaphoreType.DMA((2, TILES)),
         ],
-        [VMEM] * 6,
+        [VMEM, HBM, VMEM, VMEM, VMEM, HBM],
         VMEM,
         10**9,
         8 * 1024 * 1024,
@@ -376,13 +426,11 @@
 
 
 def final_body(returned_ref, query_ref, direct_ref, out_ref, rows, out_buf, sems):
-    per_group = ROWS * TILES // GROUPS
     copies = []
     for step in range(STEPS):
         at = slice(step * ROWS, (step + 1) * ROWS)
-        for g in range(GROUPS):
-            message = returned_ref[:, step * GROUPS + g].astype(F32)
-            rows[g * per_group : (g + 1) * per_group, :] = message.reshape(per_group, LANES)
+        message = returned_ref[step * ROWS // 2 : (step + 1) * ROWS // 2].astype(F32)
+        rows[...] = message.reshape(ROWS * TILES, LANES)
         for c in range(TILES):
             lanes = slice(c * LANES, (c + 1) * LANES)
             long_result = rows[pl.ds(c, ROWS, stride=TILES), :]
@@ -416,19 +464,19 @@
 
 
 def exchange(messages):
-    return lax.all_to_all(messages, AXES, split_axis=0, concat_axis=0, tiled=True)
+    return lax.all_to_all(messages, OWNERS, split_axis=0, concat_axis=0, tiled=True)
 
 
 def shards(consts, q, k, v, short_taps, long_filter, skip_gain):
     consts = {name: jnp.asarray(table) for name, table in consts.items()}
     skip = skip_gain[None]
-    messages = gate(q, k, v, short_taps, skip)
+    messages = gate(q, k, v, short_taps, skip).reshape(BLOCKS, WIDTH, 2, LANES)
     messages, q, k, v, long_filter = lax.optimization_barrier((messages, q, k, v, long_filter))
-    arrived = exchange(messages.reshape(BLOCKS, MESSAGE, LANES))
-    filt = long_filter.reshape(2, BLOCKS * TILES, LANES)
+    arrived = exchange(messages).reshape(BLOCKS * 2 * WIDTH, LANES)
+    filt = long_filter.reshape(2, BLOCKS * TILES, LANES).swapaxes(0, 1)
+    filt = filt.reshape(2 * BLOCKS * TILES, LANES)
     spec, query, direct_term = beside(filt, consts, q, k, v, short_taps, skip)
-    results = conv(arrived, spec, consts)
-    returned = exchange(results).reshape(SEQ, CH, BODY, LANES)
+    returned = exchange(conv(arrived, spec, consts))
     return final(returned, query, direct_term)
 
 

time: 55.4 us -> 54.5 us (0.984)
  local copies, waits for them, and re-layouts: 8.14 us -> 0.03 us
  Pallas kernels: 10.9 us -> 16.7 us
  waiting for transfers between devices: 6.62 us -> 8.18 us
    unnamed x31 -> x10, local copies, waits for them, and re-layouts: 8.14 us -> 0.03 us
    pallas_call x2, Pallas kernels: 7.08 us -> 10.7 us  [the longest x1 6.34 us: beside(): call(beside_body, 'beside', (shape(spec, BF16), shape((CHANNELS, TOKENS),...]
    pallas_call x1, Pallas kernels: 2.77 us -> 4.92 us  [conv(): call(conv_body, 'conv', shape((BLOCKS, BODY, LANES), BF16), [pltpu.VMEM((...]
    all_to_all x1, waiting for transfers between devices: 6.62 us -> 8.18 us  [exchange(): lax.all_to_all(messages, OWNERS, split_axis=0, concat_axis=0, tiled=True)]
  transfers between devices with their start and end apart: 1 -> 1, of which waited for: 1 -> 1; matrix products, arithmetic and copies ran while one was open for 2% -> 0% of each run, Pallas kernels for 5% -> 12%
where the time goes in v3:
time: 54.5 us; the launch traced here: 54.2 us
  blocking collectives  17.7 us (32%)
  Pallas kernels  16.7 us (31%)
  starting transfers between devices  11.5 us (21%)
  waiting for transfers between devices  8.18 us (15%)
    all_to_all x1, blocking collectives, exchange(): lax.all_to_all(messages, OWNERS, split_axis=0, concat_axis=0, tiled=True)  17.7 us
    all_to_all x1, starting transfers between devices, exchange(): lax.all_to_all(messages, OWNERS, split_axis=0, concat_axis=0, tiled=True)  11.5 us
    all_to_all x1, waiting for transfers between devices, exchange(): lax.all_to_all(messages, OWNERS, split_axis=0, concat_axis=0, tiled=True)  8.18 us
    pallas_call x1, Pallas kernels, beside(): call(beside_body, 'beside', (shape(spec, BF16), shape((CHANNELS, TOKENS),...  6.34 us
    pallas_call x1, Pallas kernels, conv(): call(conv_body, 'conv', shape((BLOCKS, BODY, LANES), BF16), [pltpu.VMEM((...  4.92 us
    pallas_call x1, Pallas kernels, gate(): call(gate_body, 'gate', shape((CHANNELS * WIDTH, LANES), BF16), [pltpu.VM...  4.4 us
  transfers between devices with their start and end apart: 1, of which 1 were waited for; matrix products, arithmetic and copies ran while one was open for 0% of the time, Pallas kernels for 12%

profile of v3, /device:TPU:1, one launch (start us, length us, event | category | flops | bytes accessed | tf_op | source)
XLA Modules:
  0.0 54.2 jit_solution(16481194274289103245)
XLA Ops:
  0.0 4.4 %gate.1 = bf16[2304,128]{1,0:T(8,128)(2,1)} custom-call(bf16[256,1024]{1,0:T(8,128)(2,1)} %q_ref.2, bf16[256,1024]{1,0:T(8,128)(2,1)} %k_ref.2, bf16[256,1024]{1,0:T(8,128)(2,1)} %v_ref.2, f32[3,3,256]{2,1,0:T(4,128)} %taps_ref.3, f32[1,256]{1,0:T(1,128)} %bitcast.11), custom_call_target="tpu_custom_call" | custom-call | flops 10000000 | bytes 2097152 | tf_op jit(solution)/shard_map/gate/pallas_call | solution.py:169
  4.4 11.5 %all-to-all-start = ((bf16[128,9,2,128]{3,2,1,0:T(2,128)(2,1)}), bf16[128,9,2,128]{3,2,1,0:T(2,128)(2,1)S(1)}, u32[]{:S(2)}, u32[]{:S(2)}) async-start(bf16[128,9,2,128]{3,2,1,0:T(2,128)(2,1)} %bitcast.9), calls=%async_computation | async-start | bytes 1179648 | tf_op jit(solution)/shard_map/all_to_all | solution.py:467
  15.9 0.0 copy-start
  15.9 0.0 copy-start.3
  15.9 0.0 copy-start.4
  16.0 6.3 %beside.1 = (bf16[8,256,256]{2,1,0:T(8,128)(2,1)}, f32[256,1024]{1,0:T(8,128)}, f32[256,1024]{1,0:T(8,128)}) custom-call(bf16[2048,128]{1,0:T(8,128)(2,1)} %bitcast.10, bf16[8,256,128]{2,1,0:T(8,128)(2,1)} %constant.8.clone.outer_ref, f32[2,128,128]{2,1,0:T(8,128)} %constant.10.clone.turn_ref, bf16[8,256,256]{2,1,0:T(8,128)(2,1)} %constant.11.clone.inner_ref, ...), custom_call_target="tpu_custom_call" | custom-call | flops 1000000000 | bytes 8388608 | tf_op jit(solution)/shard_map/beside/pallas_call | solution.py:300
  22.3 8.2 %all-to-all-done = bf16[128,9,2,128]{3,2,1,0:T(2,128)(2,1)S(1)} async-done(((bf16[128,9,2,128]{3,2,1,0:T(2,128)(2,1)}), bf16[128,9,2,128]{3,2,1,0:T(2,128)(2,1)S(1)}, u32[]{:S(2)}, u32[]{:S(2)}) %all-to-all-start) | async-done | bytes 589856 | tf_op jit(solution)/shard_map/all_to_all | solution.py:467
  30.5 0.0 copy-done
  30.5 0.0 copy-done.3
  30.5 0.0 copy-done.4
  30.5 0.0 copy-start.2
  30.5 4.9 %conv.1 = bf16[128,16,128]{2,1,0:T(8,128)(2,1)S(1)} custom-call(bf16[2304,128]{1,0:T(8,128)(2,1)S(1)} %bitcast.8, bf16[8,256,256]{2,1,0:T(8,128)(2,1)} %get-tuple-element.18.spec_ref, bf16[8,256,128]{2,1,0:T(8,128)(2,1)S(1)} %copy-done, bf16[8,128,256]{2,1,0:T(8,128)(2,1)S(1)} %copy-done.3, f32[2,128,128]{2,1,0:T(8,128)S(1)} %copy-done.4, ...), custom_call_target="tpu_custom_call" | custom-call | flops 1000000000 | bytes 8388608 | tf_op jit(solution)/shard_map/conv/pallas_call | solution.py:406
  35.4 0.0 copy-start.1
  35.4 17.7 %all_to_all.10.returned_ref = bf16[128,16,128]{2,1,0:T(8,128)(2,1)S(1)} all-to-all(bf16[128,16,128]{2,1,0:T(8,128)(2,1)S(1)} %conv.1), channel_id=1, replica_groups=mesh['seq'=8,'ch'=16] {'ch','seq'}, dimensions={0} | all-to-all | bytes 1048576 | tf_op jit(solution)/shard_map/all_to_all | solution.py:467
  53.2 0.0 copy-done.2
  53.2 0.0 copy-done.1
  53.2 1.1 %final.1 = bf16[256,1024]{1,0:T(8,128)(2,1)} custom-call(bf16[128,16,128]{2,1,0:T(8,128)(2,1)S(1)} %all_to_all.10.returned_ref, f32[256,1024]{1,0:T(8,128)S(1)} %copy-done.1, f32[256,1024]{1,0:T(8,128)S(1)} %copy-done.2), custom_call_target="tpu_custom_call" | custom-call | flops 1000000 | bytes 2097152 | tf_op jit(solution)/shard_map/final/pallas_call | solution.py:449
Async XLA Ops:
  4.4 26.1 %all-to-all-start = ((bf16[128,9,2,128]{3,2,1,0:T(2,128)(2,1)}), bf16[128,9,2,128]{3,2,1,0:T(2,128)(2,1)S(1)}, u32[]{:S(2)}, u32[]{:S(2)}) async-start(bf16[128,9,2,128]{3,2,1,0:T(2,128)(2,1)} %bitcast.9), calls=%async_computation | async-start | bytes 1179648 | tf_op jit(solution)/shard_map/all_to_all | solution.py:467
  15.9 14.6 %copy-start = (bf16[8,256,128]{2,1,0:T(8,128)(2,1)S(1)}, bf16[8,256,128]{2,1,0:T(8,128)(2,1)}, u32[]{:S(2)}) copy-start(bf16[8,256,128]{2,1,0:T(8,128)(2,1)} %constant.8.clone.outer_ref) | copy-start | bytes 1572868
  15.9 14.6 %copy-start.3 = (bf16[8,128,256]{2,1,0:T(8,128)(2,1)S(1)}, bf16[8,128,256]{2,1,0:T(8,128)(2,1)}, u32[]{:S(2)}) copy-start(bf16[8,128,256]{2,1,0:T(8,128)(2,1)} %constant.9.clone.outer_back_ref) | copy-start | bytes 1572868
  15.9 14.5 %copy-start.4 = (f32[2,128,128]{2,1,0:T(8,128)S(1)}, f32[2,128,128]{2,1,0:T(8,128)}, u32[]{:S(2)}) copy-start(f32[2,128,128]{2,1,0:T(8,128)} %constant.10.clone.turn_ref) | copy-start | bytes 393220
  30.5 22.7 %copy-start.2 = (f32[256,1024]{1,0:T(8,128)S(1)}, f32[256,1024]{1,0:T(8,128)}, u32[]{:S(2)}) copy-start(f32[256,1024]{1,0:T(8,128)} %get-tuple-element.20.direct_ref) | copy-start | bytes 3145732
  35.4 17.7 %copy-start.1 = (f32[256,1024]{1,0:T(8,128)S(1)}, f32[256,1024]{1,0:T(8,128)}, u32[]{:S(2)}) copy-start(f32[256,1024]{1,0:T(8,128)} %get-tuple-element.19.query_ref) | copy-start | bytes 3145732

commit v4 on v3

--- a/solution.py
+++ b/solution.py
@@ -22,7 +22,7 @@
 CH = 16
 BODY = 2 * TILES
 WIDTH = TILES + 1
-GATE_LIMIT, BESIDE_LIMIT, CONV_LIMIT, FINAL_LIMIT = 60, 60, 51, 16
+GATE_LIMIT, BESIDE_LIMIT, CONV_LIMIT, FINAL_LIMIT = 60, 60, 16, 16
 ROWS = 64
 STEPS = CHANNELS // ROWS
 AXES = ("seq", "ch")
@@ -51,7 +51,6 @@
     narrow = ml_dtypes.bfloat16
     return dict(
         outer=outer.astype(narrow),
-        outer_back=outer.swapaxes(1, 2).astype(narrow),
         turn=turn.astype(np.float32),
         inner=inner.astype(narrow),
     )
@@ -331,20 +330,22 @@
     )(filt, *(consts[name] for name in names), q, k, v, taps, skip)
 
 
+def touch_body(spec_ref, *refs):
+    out_ref = refs[-1]
+    out_ref[...] = spec_ref[0, :16, :LANES].astype(F32)
+
+
+def touch(spec, consts):
+    return call(
+        touch_body, "touch", shape((16, LANES), F32), [], [VMEM] * 4, VMEM, 10**4, 10**6, CONV_LIMIT
+    )(spec, *(consts[name] for name in ('outer', 'turn', 'inner')))
+
+
 def conv_body(
-    arrived_ref, spec_ref, outer_ref, outer_back_ref, turn_ref, inner_ref, out_ref,
-    rows, section, turned, back, edges, inner_buf, spec_buf, sems
+    arrived_ref, spec_ref, outer_ref, turn_ref, inner_ref, touched_ref, out_ref,
+    rows, section, turned, back, edges
 ):
-    copies = [
-        [
-            pltpu.make_async_copy(ref.at[kc], buf.at[kc], sems.at[i, kc])
-            for i, (ref, buf) in enumerate(((inner_ref, inner_buf), (spec_ref, spec_buf)))
-        ]
-        for kc in range(TILES)
-    ]
-    for pair in copies:
-        for copy in pair:
-            copy.start()
+    del touched_ref
     rows[...] = arrived_ref[...].astype(F32)
 
     def arrived(j, c):
@@ -368,14 +369,12 @@
         signals.append(jnp.concatenate(halves, axis=1).astype(BF16))
     forward(signals, outer_ref, turn_ref, section, turned)
     for kc in range(TILES):
-        for copy in copies[kc]:
-            copy.wait()
-        spectrum = dot(turned[kc], inner_buf[kc])
+        spectrum = dot(turned[kc], inner_ref[kc])
         re, im = spectrum[:, :LANES], spectrum[:, LANES:]
-        spec = spec_buf[kc].astype(F32)
+        spec = spec_ref[kc].astype(F32)
         filt_re, filt_im = spec[:, :LANES], spec[:, LANES:]
         parts = [re * filt_re - im * filt_im, re * filt_im + im * filt_re]
-        section[kc] = dot_back(jnp.concatenate(parts, axis=1).astype(BF16), inner_buf[kc])
+        section[kc] = dot_back(jnp.concatenate(parts, axis=1).astype(BF16), inner_ref[kc])
     for row in range(0, BLOCKS, 16):
         turn_re, turn_im = turn_ref[0, row : row + 16, :], turn_ref[1, row : row + 16, :]
         for j in range(2):
@@ -391,7 +390,9 @@
                 back[c, row : row + 16, half] = re[c].astype(BF16)
                 back[c, BLOCKS + row : BLOCKS + row + 16, half] = im[c].astype(BF16)
     for c in range(TILES):
-        result = dot(outer_back_ref[c], back[c])
+        result = lax.dot_general(
+            outer_ref[c], back[c], (((0,), (0,)), ((), ())), preferred_element_type=F32
+        )
         for j in range(2):
             half = result[:, j * LANES : (j + 1) * LANES]
             if c == 0:
@@ -401,8 +402,8 @@
     out_ref[...] = rows[: BLOCKS * BODY, :].reshape(BLOCKS, BODY, LANES).astype(BF16)
 
 
-def conv(arrived, spec, consts):
-    names = ("outer", "outer_back", "turn", "inner")
+def conv(arrived, spec, consts, touched):
+    names = ("outer", "turn", "inner")
     return call(
         conv_body,
         "conv",
@@ -413,16 +414,13 @@
             pltpu.VMEM((TILES, 2 * BLOCKS, 2 * LANES), BF16),
             pltpu.VMEM((TILES, 2 * BLOCKS, 2 * LANES), BF16),
             pltpu.VMEM((2, 2, BLOCKS, LANES), F32),
-            pltpu.VMEM((TILES, 2 * LANES, 2 * LANES), BF16),
-            pltpu.VMEM((TILES, 2 * BLOCKS, 2 * LANES), BF16),
-            pltpu.SemaphoreType.DMA((2, TILES)),
         ],
-        [VMEM, HBM, VMEM, VMEM, VMEM, HBM],
+        [VMEM] * 6,
         VMEM,
         10**9,
         8 * 1024 * 1024,
         CONV_LIMIT,
-    )(arrived, spec, *(consts[name] for name in names))
+    )(arrived, spec, *(consts[name] for name in names), touched)
 
 
 def final_body(returned_ref, query_ref, direct_ref, out_ref, rows, out_buf, sems):
@@ -476,7 +474,7 @@
     filt = long_filter.reshape(2, BLOCKS * TILES, LANES).swapaxes(0, 1)
     filt = filt.reshape(2 * BLOCKS * TILES, LANES)
     spec, query, direct_term = beside(filt, consts, q, k, v, short_taps, skip)
-    returned = exchange(conv(arrived, spec, consts))
+    returned = exchange(conv(arrived, spec, consts, touch(spec, consts)))
     return final(returned, query, direct_term)
 
 

time: 54.5 us -> 52.4 us (0.961)
  Pallas kernels: 16.7 us -> 14.6 us
  waiting for transfers between devices: 8.18 us -> 6.89 us
  local copies, waits for them, and re-layouts: 0.03 us -> 1.25 us
    pallas_call x1, Pallas kernels: 4.92 us -> 2.75 us  [conv(): call(conv_body, 'conv', shape((BLOCKS, BODY, LANES), BF16), [pltpu.VMEM((...]
    all_to_all x1, waiting for transfers between devices: 8.18 us -> 6.89 us  [exchange(): lax.all_to_all(messages, OWNERS, split_axis=0, concat_axis=0, tiled=True)]
    unnamed x10 -> x14, local copies, waits for them, and re-layouts: 0.03 us -> 1.25 us
where the time goes in v4:
time: 52.4 us; the launch traced here: 52.1 us
  blocking collectives  17.8 us (34%)
  Pallas kernels  14.6 us (28%)
  starting transfers between devices  11.5 us (22%)
  waiting for transfers between devices  6.89 us (13%)
  local copies, waits for them, and re-layouts  1.25 us (2%)
    all_to_all x1, blocking collectives, exchange(): lax.all_to_all(messages, OWNERS, split_axis=0, concat_axis=0, tiled=True)  17.8 us
    all_to_all x1, starting transfers between devices, exchange(): lax.all_to_all(messages, OWNERS, split_axis=0, concat_axis=0, tiled=True)  11.5 us
    all_to_all x1, waiting for transfers between devices, exchange(): lax.all_to_all(messages, OWNERS, split_axis=0, concat_axis=0, tiled=True)  6.89 us
    pallas_call x1, Pallas kernels, beside(): call(beside_body, 'beside', (shape(spec, BF16), shape((CHANNELS, TOKENS),...  6.37 us
    pallas_call x1, Pallas kernels, gate(): call(gate_body, 'gate', shape((CHANNELS * WIDTH, LANES), BF16), [pltpu.VM...  4.39 us
    pallas_call x1, Pallas kernels, conv(): call(conv_body, 'conv', shape((BLOCKS, BODY, LANES), BF16), [pltpu.VMEM((...  2.75 us
    unnamed x14, local copies, waits for them, and re-layouts  1.25 us
    pallas_call x1, Pallas kernels, final(): call(final_body, 'final', shape((CHANNELS, TOKENS), BF16), [pltpu.VMEM((R...  1.06 us
  transfers between devices with their start and end apart: 1, of which 1 were waited for; matrix products, arithmetic and copies ran while one was open for 0% of the time, Pallas kernels for 12%

profile of v4, /device:TPU:1, one launch (start us, length us, event | category | flops | bytes accessed | tf_op | source)
XLA Modules:
  0.0 52.1 jit_solution(15642816772873829779)
XLA Ops:
  0.0 4.4 %gate.1 = bf16[2304,128]{1,0:T(8,128)(2,1)} custom-call(bf16[256,1024]{1,0:T(8,128)(2,1)} %q_ref.2, bf16[256,1024]{1,0:T(8,128)(2,1)} %k_ref.2, bf16[256,1024]{1,0:T(8,128)(2,1)} %v_ref.2, f32[3,3,256]{2,1,0:T(4,128)} %taps_ref.3, f32[1,256]{1,0:T(1,128)} %bitcast.11), custom_call_target="tpu_custom_call" | custom-call | flops 10000000 | bytes 2097152 | tf_op jit(solution)/shard_map/gate/pallas_call | solution.py:168
  4.4 11.5 %all-to-all-start = ((bf16[128,9,2,128]{3,2,1,0:T(2,128)(2,1)}), bf16[128,9,2,128]{3,2,1,0:T(2,128)(2,1)S(1)}, u32[]{:S(2)}, u32[]{:S(2)}) async-start(bf16[128,9,2,128]{3,2,1,0:T(2,128)(2,1)} %bitcast.9), calls=%async_computation | async-start | bytes 1179648 | tf_op jit(solution)/shard_map/all_to_all | solution.py:465
  15.9 0.0 copy-start
  15.9 0.0 copy-start.1
  15.9 0.0 copy-start.4
  16.0 6.4 %beside.1 = (bf16[8,256,256]{2,1,0:T(8,128)(2,1)}, f32[256,1024]{1,0:T(8,128)}, f32[256,1024]{1,0:T(8,128)}) custom-call(bf16[2048,128]{1,0:T(8,128)(2,1)} %bitcast.10, bf16[8,256,128]{2,1,0:T(8,128)(2,1)} %constant.6.clone.outer_ref.refs_0_, f32[2,128,128]{2,1,0:T(8,128)} %constant.7.clone.turn_ref.refs_1_, ...), custom_call_target="tpu_custom_call" | custom-call | flops 1000000000 | bytes 8388608 | tf_op jit(solution)/shard_map/beside/pallas_call | solution.py:299
  22.3 0.0 copy-done
  22.3 0.0 copy-done.1
  22.3 0.0 copy-done.4
  22.4 0.0 copy-start.2
  22.4 1.2 %copy-done.2 = bf16[8,256,256]{2,1,0:T(8,128)(2,1)S(1)} copy-done((bf16[8,256,256]{2,1,0:T(8,128)(2,1)S(1)}, bf16[8,256,256]{2,1,0:T(8,128)(2,1)}, u32[]{:S(2)}) %copy-start.2) | copy-done | bytes 1048600
  23.6 0.0 copy-start.3
  23.6 6.9 %all-to-all-done = bf16[128,9,2,128]{3,2,1,0:T(2,128)(2,1)S(1)} async-done(((bf16[128,9,2,128]{3,2,1,0:T(2,128)(2,1)}), bf16[128,9,2,128]{3,2,1,0:T(2,128)(2,1)S(1)}, u32[]{:S(2)}, u32[]{:S(2)}) %all-to-all-start) | async-done | bytes 589856 | tf_op jit(solution)/shard_map/all_to_all | solution.py:465
  30.5 0.0 copy-done.3
  30.5 0.0 copy-start.6
  30.5 2.8 %conv.1 = bf16[128,16,128]{2,1,0:T(8,128)(2,1)S(1)} custom-call(bf16[2304,128]{1,0:T(8,128)(2,1)S(1)} %bitcast.8, bf16[8,256,256]{2,1,0:T(8,128)(2,1)S(1)} %copy-done.3, bf16[8,256,128]{2,1,0:T(8,128)(2,1)S(1)} %copy-done.1, f32[2,128,128]{2,1,0:T(8,128)S(1)} %copy-done.4, bf16[8,256,256]{2,1,0:T(8,128)(2,1)S(1)} %copy-done, f32[16,128]{1,0:T(8,128)S(1)} %touch.1.touched_ref), custom_call_target="tpu_custom_call" | custom-call | flops 1000000000 | bytes 8388608 | tf_op jit(solution)/shard_map/conv/pallas_call | solution.py:407
  33.2 0.0 copy-start.5
  33.3 17.8 %all_to_all.10.returned_ref = bf16[128,16,128]{2,1,0:T(8,128)(2,1)S(1)} all-to-all(bf16[128,16,128]{2,1,0:T(8,128)(2,1)S(1)} %conv.1), channel_id=1, replica_groups=mesh['seq'=8,'ch'=16] {'ch','seq'}, dimensions={0} | all-to-all | bytes 1048576 | tf_op jit(solution)/shard_map/all_to_all | solution.py:465
  51.0 0.0 copy-done.6
  51.0 0.0 copy-done.5
  51.0 1.1 %final.1 = bf16[256,1024]{1,0:T(8,128)(2,1)} custom-call(bf16[128,16,128]{2,1,0:T(8,128)(2,1)S(1)} %all_to_all.10.returned_ref, f32[256,1024]{1,0:T(8,128)S(1)} %copy-done.5, f32[256,1024]{1,0:T(8,128)S(1)} %copy-done.6), custom_call_target="tpu_custom_call" | custom-call | flops 1000000 | bytes 2097152 | tf_op jit(solution)/shard_map/final/pallas_call | solution.py:447
  (1 shorter events, 0.0 us)
Async XLA Ops:
  4.4 26.1 %all-to-all-start = ((bf16[128,9,2,128]{3,2,1,0:T(2,128)(2,1)}), bf16[128,9,2,128]{3,2,1,0:T(2,128)(2,1)S(1)}, u32[]{:S(2)}, u32[]{:S(2)}) async-start(bf16[128,9,2,128]{3,2,1,0:T(2,128)(2,1)} %bitcast.9), calls=%async_computation | async-start | bytes 1179648 | tf_op jit(solution)/shard_map/all_to_all | solution.py:465
  15.9 6.4 %copy-start = (bf16[8,256,256]{2,1,0:T(8,128)(2,1)S(1)}, bf16[8,256,256]{2,1,0:T(8,128)(2,1)}, u32[]{:S(2)}) copy-start(bf16[8,256,256]{2,1,0:T(8,128)(2,1)} %constant.8.clone.inner_ref.refs_2_) | copy-start | bytes 3145732
  15.9 6.4 %copy-start.1 = (bf16[8,256,128]{2,1,0:T(8,128)(2,1)S(1)}, bf16[8,256,128]{2,1,0:T(8,128)(2,1)}, u32[]{:S(2)}) copy-start(bf16[8,256,128]{2,1,0:T(8,128)(2,1)} %constant.6.clone.outer_ref.refs_0_) | copy-start | bytes 1572868
  15.9 6.4 %copy-start.4 = (f32[2,128,128]{2,1,0:T(8,128)S(1)}, f32[2,128,128]{2,1,0:T(8,128)}, u32[]{:S(2)}) copy-start(f32[2,128,128]{2,1,0:T(8,128)} %constant.7.clone.turn_ref.refs_1_) | copy-start | bytes 393220
  22.4 1.2 %copy-start.2 = (bf16[8,256,256]{2,1,0:T(8,128)(2,1)S(1)}, bf16[8,256,256]{2,1,0:T(8,128)(2,1)}, u32[]{:S(2)}) copy-start(bf16[8,256,256]{2,1,0:T(8,128)(2,1)} %get-tuple-element.18.spec_ref) | copy-start | bytes 3145732
  23.6 6.9 %copy-start.3 = (bf16[8,256,256]{2,1,0:T(8,128)(2,1)S(1)}, bf16[8,256,256]{2,1,0:T(8,128)(2,1)}, u32[]{:S(2)}) copy-start(bf16[8,256,256]{2,1,0:T(8,128)(2,1)} %get-tuple-element.18.spec_ref) | copy-start | bytes 3145732
  30.5 20.6 %copy-start.6 = (f32[256,1024]{1,0:T(8,128)S(1)}, f32[256,1024]{1,0:T(8,128)}, u32[]{:S(2)}) copy-start(f32[256,1024]{1,0:T(8,128)} %get-tuple-element.20.direct_ref) | copy-start | bytes 3145732
  33.2 17.8 %copy-start.5 = (f32[256,1024]{1,0:T(8,128)S(1)}, f32[256,1024]{1,0:T(8,128)}, u32[]{:S(2)}) copy-start(f32[256,1024]{1,0:T(8,128)} %get-tuple-element.19.query_ref) | copy-start | bytes 3145732

commit v5 on v4

--- a/solution.py
+++ b/solution.py
@@ -22,9 +22,11 @@
 CH = 16
 BODY = 2 * TILES
 WIDTH = TILES + 1
-GATE_LIMIT, BESIDE_LIMIT, CONV_LIMIT, FINAL_LIMIT = 60, 60, 16, 16
+GATE_LIMIT, FILTER_LIMIT, DIRECT_LIMIT, CONV_LIMIT, FINAL_LIMIT = 60, 52, 60, 16, 16
 ROWS = 64
 STEPS = CHANNELS // ROWS
+DIRECT_ROWS = 128
+DIRECT_STEPS = CHANNELS // DIRECT_ROWS
 AXES = ("seq", "ch")
 OWNERS = ("ch", "seq")
 VMEM = pl.BlockSpec(memory_space=pltpu.VMEM)
@@ -99,13 +101,31 @@
     return [cols[:, 3 * stream + i : 3 * stream + i + 1] for i in range(3)]
 
 
+def moved(x):
+    src = lax.broadcasted_iota(jnp.int32, (2 * LANES, 2 * LANES), 0)
+    dst = lax.broadcasted_iota(jnp.int32, (2 * LANES, 2 * LANES), 1)
+    shift = (src - LANES == dst % LANES - 1 - dst // LANES).astype(BF16)
+    count = x.shape[0]
+    tiles = x.shape[1] // LANES
+    wide = jnp.concatenate([x[:, -LANES:], x], axis=1)
+    both = dot(
+        jnp.concatenate([wide[:, c * LANES : (c + 2) * LANES] for c in range(tiles)], axis=0), shift
+    )
+    both = [both[c * count : (c + 1) * count] for c in range(tiles)]
+    return tuple(
+        jnp.concatenate([tile[:, i * LANES : (i + 1) * LANES] for tile in both], axis=1)
+        for i in range(2)
+    )
+
+
 def causal(x, taps):
-    return taps[0] * x + taps[1] * pltpu.roll(x, 1, 1) + taps[2] * pltpu.roll(x, 2, 1)
+    back1, back2 = moved(x)
+    return taps[0] * x.astype(F32) + taps[1] * back1 + taps[2] * back2
 
 
 def with_edges(x, taps):
-    back1, back2 = pltpu.roll(x, 1, 1), pltpu.roll(x, 2, 1)
-    sums = taps[0] * x + taps[1] * back1 + taps[2] * back2
+    back1, back2 = moved(x)
+    sums = taps[0] * x.astype(F32) + taps[1] * back1 + taps[2] * back2
     lane = lax.broadcasted_iota(jnp.int32, (x.shape[0], LANES), 1)
     near = jnp.where(lane < 1, back1[:, :LANES], 0.0)
     far = jnp.where(lane < 2, back2[:, :LANES], 0.0)
@@ -115,7 +135,7 @@
 
 def gate_body(
     q_ref, k_ref, v_ref, taps_ref, skip_ref, out_ref,
-    taps_buf, skip_buf, q_buf, k_buf, v_buf, tap_rows, cols_buf, rows, small, sems
+    taps_buf, skip_buf, q_buf, k_buf, v_buf, tap_rows, rows, small, sems
 ):
     def small_copies():
         pairs = [(taps_ref, taps_buf), (skip_ref, skip_buf)]
@@ -124,44 +144,32 @@
         ]
         return [pltpu.make_async_copy(a, b, small.at[i]) for i, (a, b) in enumerate(pairs)]
 
-    copies = []
-    for step in range(STEPS):
-        at = pl.ds(step * ROWS, ROWS)
-        copies.append(
-            [
-                pltpu.make_async_copy(ref.at[at], buf.at[at], sems.at[i, step])
-                for i, (ref, buf) in enumerate(((k_ref, k_buf), (v_ref, v_buf)))
-            ]
-        )
-    first = small_copies()
-    for copy in first:
+    copies = small_copies() + [
+        pltpu.make_async_copy(k_ref, k_buf, sems.at[0]),
+        pltpu.make_async_copy(v_ref, v_buf, sems.at[1]),
+    ]
+    for copy in copies:
         copy.start()
-    for pair in copies:
-        for copy in pair:
-            copy.start()
-    for copy in first:
-        copy.wait()
-    cols_buf[...] = columns([taps_buf[0], taps_buf[1], taps_buf[2], skip_buf[...]], tap_rows)
-    for step in range(STEPS):
-        for copy in copies[step]:
-            copy.wait()
-        at = slice(step * ROWS, (step + 1) * ROWS)
-        cols = cols_buf[at, :]
-        query_taps, key_taps, value_taps = (taps_of(cols, stream) for stream in range(3))
-        key, key_own, key_onward = with_edges(k_buf[at, :].astype(F32), key_taps)
-        value, value_own, value_onward = with_edges(v_buf[at, :].astype(F32), value_taps)
-        query = jnp.concatenate([q_buf[0, at, :], q_buf[1, at, :]], axis=1).astype(F32)
-        _, query_own, query_onward = with_edges(query, query_taps)
-        gated = key * value
-        for c in range(TILES):
-            rows[pl.ds(c, ROWS, stride=WIDTH), :] = gated[:, c * LANES : (c + 1) * LANES]
-        lane = lanes_of(key_own)
-        own = jnp.where(lane < 2, key_own, pltpu.roll(query_own, 2, 1))
-        own_value = pltpu.roll(jnp.where(lane < 2, value_own, cols[:, 9:10]), 4, 1)
-        onward = key_onward + pltpu.roll(query_onward, 2, 1) + pltpu.roll(value_onward, 4, 1)
-        edge = jnp.where(lane < 8, own_value, pltpu.roll(onward, 8, 1))
-        rows[pl.ds(TILES, ROWS, stride=WIDTH), :] = jnp.where(lane < 4, own, edge)
-        out_ref[step * ROWS * WIDTH : (step + 1) * ROWS * WIDTH, :] = rows[...].astype(BF16)
+    for copy in copies[:2]:
+        copy.wait()
+    cols = columns([taps_buf[0], taps_buf[1], taps_buf[2], skip_buf[...]], tap_rows)
+    for copy in copies[2:]:
+        copy.wait()
+    query_taps, key_taps, value_taps = (taps_of(cols, stream) for stream in range(3))
+    key, key_own, key_onward = with_edges(k_buf[...], key_taps)
+    value, value_own, value_onward = with_edges(v_buf[...], value_taps)
+    query = jnp.concatenate([q_buf[0], q_buf[1]], axis=1)
+    _, query_own, query_onward = with_edges(query, query_taps)
+    gated = key * value
+    for c in range(TILES):
+        rows[pl.ds(c, CHANNELS, stride=WIDTH), :] = gated[:, c * LANES : (c + 1) * LANES]
+    lane = lanes_of(key_own)
+    own = jnp.where(lane < 2, key_own, pltpu.roll(query_own, 2, 1))
+    own_value = pltpu.roll(jnp.where(lane < 2, value_own, cols[:, 9:10]), 4, 1)
+    onward = key_onward + pltpu.roll(query_onward, 2, 1) + pltpu.roll(value_onward, 4, 1)
+    edge = jnp.where(lane < 8, own_value, pltpu.roll(onward, 8, 1))
+    rows[pl.ds(TILES, CHANNELS, stride=WIDTH), :] = jnp.where(lane < 4, own, edge)
+    out_ref[...] = rows[...].astype(BF16)
 
 
 def gate(q, k, v, taps, skip):
@@ -176,10 +184,9 @@
             pltpu.VMEM((CHANNELS, TOKENS), BF16),
             pltpu.VMEM((CHANNELS, TOKENS), BF16),
             pltpu.VMEM((LANES, CHANNELS), F32),
-            pltpu.VMEM((CHANNELS, LANES), F32),
-            pltpu.VMEM((ROWS * WIDTH, LANES), F32),
+            pltpu.VMEM((CHANNELS * WIDTH, LANES), F32),
             pltpu.SemaphoreType.DMA((4,)),
-            pltpu.SemaphoreType.DMA((2, STEPS)),
+            pltpu.SemaphoreType.DMA((2,)),
         ],
         [HBM] * 5,
         VMEM,
@@ -228,52 +235,11 @@
                 turned[kc, at, LANES:] = (re[kc] * turn_im + im[kc] * turn_re).astype(BF16)
 
 
-def beside_body(
-    filt_ref, outer_ref, turn_ref, inner_ref, q_ref, k_ref, v_ref, taps_ref, skip_ref,
-    spec_ref, query_ref, direct_ref,
-    filt_buf, outer_buf, turn_buf, inner_buf, streams, taps_buf, skip_buf, spec_buf, query_buf, direct_buf,
-    rows, section, turned, tap_rows, cols_buf, small, in_sems, table_sems, out_sems, spec_sems
+def filter_body(
+    filt_ref, outer_ref, turn_ref, inner_ref, spec_ref,
+    spec_buf, rows, section, turned, spec_sems
 ):
-    first = [
-        pltpu.make_async_copy(taps_ref, taps_buf, small.at[0]),
-        pltpu.make_async_copy(skip_ref, skip_buf, small.at[1]),
-    ]
-    places = [pl.ds(step * ROWS, ROWS) for step in range(STEPS)]
-    copies = [
-        [
-            pltpu.make_async_copy(ref.at[place], streams.at[i, place], in_sems.at[i, step])
-            for i, ref in enumerate((q_ref, k_ref, v_ref))
-        ]
-        for step, place in enumerate(places)
-    ]
-    pairs = ((filt_ref, filt_buf), (outer_ref, outer_buf), (turn_ref, turn_buf), (inner_ref, inner_buf))
-    tables_in = [
-        pltpu.make_async_copy(a, b, table_sems.at[i]) for i, (a, b) in enumerate(pairs)
-    ]
-    for copy in first + [copy for group in copies for copy in group] + tables_in:
-        copy.start()
-    for copy in first:
-        copy.wait()
-    out_copies = []
-    cols_buf[...] = columns([taps_buf[0], taps_buf[1], taps_buf[2], skip_buf[...]], tap_rows)
-    for step in range(STEPS):
-        for copy in copies[step]:
-            copy.wait()
-        at = slice(step * ROWS, (step + 1) * ROWS)
-        cols = cols_buf[at, :]
-        query, key, value = (
-            causal(streams[i, at, :].astype(F32), taps_of(cols, i)) for i in range(3)
-        )
-        query_buf[at, :] = query
-        direct_buf[at, :] = cols[:, 9:10] * (key * value).astype(BF16).astype(F32)
-        for i, (buf, ref) in enumerate(((query_buf, query_ref), (direct_buf, direct_ref))):
-            out_copies.append(
-                pltpu.make_async_copy(buf.at[places[step]], ref.at[places[step]], out_sems.at[i, step])
-            )
-            out_copies[-1].start()
-    for copy in tables_in:
-        copy.wait()
-    rows[...] = filt_buf[...].astype(F32)
+    rows[...] = filt_ref[...].astype(F32)
     signals = []
     for c in range(TILES):
         halves = []
@@ -284,68 +250,106 @@
             ]
             halves.append(jnp.concatenate(parts, axis=0))
         signals.append(jnp.concatenate(halves, axis=1).astype(BF16))
-    forward(signals, outer_buf, turn_buf, section, turned)
+    forward(signals, outer_ref, turn_ref, section, turned)
+    out_copies = []
     for kc in range(TILES):
-        spec_buf[kc] = (dot(turned[kc], inner_buf[kc]) * (1.0 / LENGTH)).astype(BF16)
+        spec_buf[kc] = (dot(turned[kc], inner_ref[kc]) * (1.0 / LENGTH)).astype(BF16)
         out_copies.append(pltpu.make_async_copy(spec_buf.at[kc], spec_ref.at[kc], spec_sems.at[kc]))
         out_copies[-1].start()
     for copy in out_copies:
         copy.wait()
 
 
-def beside(filt, consts, q, k, v, taps, skip):
+def filter_spectra(filt, consts):
     names = ("outer", "turn", "inner")
     spec = (TILES, 2 * BLOCKS, 2 * LANES)
     return call(
-        beside_body,
-        "beside",
-        (shape(spec, BF16), shape((CHANNELS, TOKENS), F32), shape((CHANNELS, TOKENS), F32)),
-        [
-            pltpu.VMEM((2 * BLOCKS * TILES, LANES), BF16),
-            pltpu.VMEM((TILES, 2 * BLOCKS, LANES), BF16),
-            pltpu.VMEM((2, BLOCKS, LANES), F32),
-            pltpu.VMEM((TILES, 2 * LANES, 2 * LANES), BF16),
+        filter_body,
+        "filter_spectra",
+        shape(spec, BF16),
+        [
+            pltpu.VMEM(spec, BF16),
+            pltpu.VMEM((2 * BLOCKS * TILES, LANES), F32),
+            pltpu.VMEM(spec, F32),
+            pltpu.VMEM(spec, BF16),
+            pltpu.SemaphoreType.DMA((TILES,)),
+        ],
+        [VMEM] * 4,
+        HBM,
+        10**9,
+        4 * 1024 * 1024,
+        FILTER_LIMIT,
+    )(filt, *(consts[name] for name in names))
+
+
+def direct_body(
+    q_ref, k_ref, v_ref, taps_ref, skip_ref, query_ref, direct_ref,
+    streams, taps_buf, skip_buf, query_buf, direct_buf, tap_rows, cols_buf, small, in_sems, out_sems
+):
+    first = [
+        pltpu.make_async_copy(taps_ref, taps_buf, small.at[0]),
+        pltpu.make_async_copy(skip_ref, skip_buf, small.at[1]),
+    ]
+    places = [pl.ds(step * DIRECT_ROWS, DIRECT_ROWS) for step in range(DIRECT_STEPS)]
+    copies = [
+        [
+            pltpu.make_async_copy(ref.at[place], streams.at[i, place], in_sems.at[i, step])
+            for i, ref in enumerate((q_ref, k_ref, v_ref))
+        ]
+        for step, place in enumerate(places)
+    ]
+    for copy in first + [copy for group in copies for copy in group]:
+        copy.start()
+    for copy in first:
+        copy.wait()
+    out_copies = []
+    cols_buf[...] = columns([taps_buf[0], taps_buf[1], taps_buf[2], skip_buf[...]], tap_rows)
+    for step in range(DIRECT_STEPS):
+        for copy in copies[step]:
+            copy.wait()
+        at = slice(step * DIRECT_ROWS, (step + 1) * DIRECT_ROWS)
+        cols = cols_buf[at, :]
+        query, key, value = (causal(streams[i, at, :], taps_of(cols, i)) for i in range(3))
+        query_buf[at, :] = query
+        direct_buf[at, :] = cols[:, 9:10] * (key * value).astype(BF16).astype(F32)
+        for i, (buf, ref) in enumerate(((query_buf, query_ref), (direct_buf, direct_ref))):
+            out_copies.append(
+                pltpu.make_async_copy(buf.at[places[step]], ref.at[places[step]], out_sems.at[i, step])
+            )
+            out_copies[-1].start()
+    for copy in out_copies:
+        copy.wait()
+
+
+def direct(q, k, v, taps, skip):
+    return call(
+        direct_body,
+        "direct",
+        (shape((CHANNELS, TOKENS), F32), shape((CHANNELS, TOKENS), F32)),
+        [
             pltpu.VMEM((3, CHANNELS, TOKENS), BF16),
             pltpu.VMEM((3, 3, CHANNELS), F32),
             pltpu.VMEM((1, CHANNELS), F32),
-            pltpu.VMEM(spec, BF16),
             pltpu.VMEM((CHANNELS, TOKENS), F32),
             pltpu.VMEM((CHANNELS, TOKENS), F32),
-            pltpu.VMEM((2 * BLOCKS * TILES, LANES), F32),
-            pltpu.VMEM(spec, F32),
-            pltpu.VMEM(spec, BF16),
             pltpu.VMEM((LANES, CHANNELS), F32),
             pltpu.VMEM((CHANNELS, LANES), F32),
             pltpu.SemaphoreType.DMA((2,)),
-            pltpu.SemaphoreType.DMA((3, STEPS)),
-            pltpu.SemaphoreType.DMA((4,)),
-            pltpu.SemaphoreType.DMA((2, STEPS)),
-            pltpu.SemaphoreType.DMA((TILES,)),
+            pltpu.SemaphoreType.DMA((3, DIRECT_STEPS)),
+            pltpu.SemaphoreType.DMA((2, DIRECT_STEPS)),
         ],
-        [HBM] * 9,
-        (HBM,) * 3,
+        [HBM] * 5,
+        (HBM,) * 2,
         10**9,
-        8 * 1024 * 1024,
-        BESIDE_LIMIT,
-    )(filt, *(consts[name] for name in names), q, k, v, taps, skip)
-
-
-def touch_body(spec_ref, *refs):
-    out_ref = refs[-1]
-    out_ref[...] = spec_ref[0, :16, :LANES].astype(F32)
-
-
-def touch(spec, consts):
-    return call(
-        touch_body, "touch", shape((16, LANES), F32), [], [VMEM] * 4, VMEM, 10**4, 10**6, CONV_LIMIT
-    )(spec, *(consts[name] for name in ('outer', 'turn', 'inner')))
+        4 * 1024 * 1024,
+        DIRECT_LIMIT,
+    )(q, k, v, taps, skip)
 
 
 def conv_body(
-    arrived_ref, spec_ref, outer_ref, turn_ref, inner_ref, touched_ref, out_ref,
+    arrived_ref, spec_ref, outer_ref, turn_ref, inner_ref, out_ref,
     rows, section, turned, back, edges
 ):
-    del touched_ref
     rows[...] = arrived_ref[...].astype(F32)
 
     def arrived(j, c):
@@ -402,7 +406,7 @@
     out_ref[...] = rows[: BLOCKS * BODY, :].reshape(BLOCKS, BODY, LANES).astype(BF16)
 
 
-def conv(arrived, spec, consts, touched):
+def conv(arrived, spec, consts):
     names = ("outer", "turn", "inner")
     return call(
         conv_body,
@@ -415,12 +419,12 @@
             pltpu.VMEM((TILES, 2 * BLOCKS, 2 * LANES), BF16),
             pltpu.VMEM((2, 2, BLOCKS, LANES), F32),
         ],
-        [VMEM] * 6,
+        [VMEM] * 5,
         VMEM,
         10**9,
         8 * 1024 * 1024,
         CONV_LIMIT,
-    )(arrived, spec, *(consts[name] for name in names), touched)
+    )(arrived, spec, *(consts[name] for name in names))
 
 
 def final_body(returned_ref, query_ref, direct_ref, out_ref, rows, out_buf, sems):
@@ -473,8 +477,11 @@
     arrived = exchange(messages).reshape(BLOCKS * 2 * WIDTH, LANES)
     filt = long_filter.reshape(2, BLOCKS * TILES, LANES).swapaxes(0, 1)
     filt = filt.reshape(2 * BLOCKS * TILES, LANES)
-    spec, query, direct_term = beside(filt, consts, q, k, v, short_taps, skip)
-    returned = exchange(conv(arrived, spec, consts, touch(spec, consts)))
+    spec = filter_spectra(filt, consts)
+    spec, q, k, v = lax.optimization_barrier((spec, q, k, v))
+    query, direct_term = direct(q, k, v, short_taps, skip)
+    spec, query, direct_term = lax.optimization_barrier((spec, query, direct_term))
+    returned = exchange(conv(arrived, spec, consts))
     return final(returned, query, direct_term)
 
 

time: 52.4 us -> 51.2 us (0.977)
  local copies, waits for them, and re-layouts: 1.25 us -> 0.04 us
    unnamed x14, local copies, waits for them, and re-layouts: 1.25 us -> 0.04 us
    pallas_call x2, Pallas kernels: 6.37 us -> 7.48 us  [the longest x1 3.77 us: direct(): call(direct_body, 'direct', (shape((CHANNELS, TOKENS), F32), shape((CHANN...]
    pallas_call x1, Pallas kernels: 4.39 us -> 3.3 us  [gate(): call(gate_body, 'gate', shape((CHANNELS * WIDTH, LANES), BF16), [pltpu.VM...]
  transfers between devices with their start and end apart: 1 -> 1, of which waited for: 1 -> 1; matrix products, arithmetic and copies ran while one was open for 0% -> 0% of each run, Pallas kernels for 12% -> 15%
where the time goes in v5:
time: 51.2 us; the launch traced here: 51 us
  blocking collectives  17.7 us (35%)
  Pallas kernels  14.6 us (29%)
  starting transfers between devices  11.5 us (22%)
  waiting for transfers between devices  7.01 us (14%)
    all_to_all x1, blocking collectives, exchange(): lax.all_to_all(messages, OWNERS, split_axis=0, concat_axis=0, tiled=True)  17.7 us
    all_to_all x1, starting transfers between devices, exchange(): lax.all_to_all(messages, OWNERS, split_axis=0, concat_axis=0, tiled=True)  11.5 us
    all_to_all x1, waiting for transfers between devices, exchange(): lax.all_to_all(messages, OWNERS, split_axis=0, concat_axis=0, tiled=True)  7.01 us
    pallas_call x1, Pallas kernels, direct(): call(direct_body, 'direct', (shape((CHANNELS, TOKENS), F32), shape((CHANN...  3.77 us
    pallas_call x1, Pallas kernels, filter_spectra(): call(filter_body, 'filter_spectra', shape(spec, BF16), [pltpu.VMEM(spec,...  3.71 us
    pallas_call x1, Pallas kernels, gate(): call(gate_body, 'gate', shape((CHANNELS * WIDTH, LANES), BF16), [pltpu.VM...  3.3 us
    pallas_call x1, Pallas kernels, conv(): call(conv_body, 'conv', shape((BLOCKS, BODY, LANES), BF16), [pltpu.VMEM((...  2.75 us
    pallas_call x1, Pallas kernels, final(): call(final_body, 'final', shape((CHANNELS, TOKENS), BF16), [pltpu.VMEM((R...  1.06 us
  transfers between devices with their start and end apart: 1, of which 1 were waited for; matrix products, arithmetic and copies ran while one was open for 0% of the time, Pallas kernels for 15%

profile of v5, /device:TPU:1, one launch (start us, length us, event | category | flops | bytes accessed | tf_op | source)
XLA Modules:
  0.0 51.0 jit_solution(3967694645738274246)
XLA Ops:
  0.0 3.3 %gate.1 = bf16[2304,128]{1,0:T(8,128)(2,1)} custom-call(bf16[256,1024]{1,0:T(8,128)(2,1)} %q_ref.2, bf16[256,1024]{1,0:T(8,128)(2,1)} %k_ref.2, bf16[256,1024]{1,0:T(8,128)(2,1)} %v_ref.2, f32[3,3,256]{2,1,0:T(4,128)} %taps_ref.3, f32[1,256]{1,0:T(1,128)} %bitcast.11), custom_call_target="tpu_custom_call" | custom-call | flops 10000000 | bytes 2097152 | tf_op jit(solution)/shard_map/gate/pallas_call | solution.py:176
  3.3 0.0 copy-start.4
  3.3 0.0 copy-start.5
  3.3 0.0 copy-start.6
  3.3 11.5 %all-to-all-start = ((bf16[128,9,2,128]{3,2,1,0:T(2,128)(2,1)}), bf16[128,9,2,128]{3,2,1,0:T(2,128)(2,1)S(1)}, u32[]{:S(2)}, u32[]{:S(2)}) async-start(bf16[128,9,2,128]{3,2,1,0:T(2,128)(2,1)} %bitcast.10), calls=%async_computation | async-start | bytes 1179648 | tf_op jit(solution)/shard_map/all_to_all | solution.py:469
  14.9 0.0 copy-done.4
  14.9 0.0 copy-done.5
  14.9 0.0 copy-done.6
  14.9 3.7 %filter_spectra.1.spec_ref = bf16[8,256,256]{2,1,0:T(8,128)(2,1)} custom-call(bf16[2048,128]{1,0:T(8,128)(2,1)S(1)} %bitcast.9, bf16[8,256,128]{2,1,0:T(8,128)(2,1)S(1)} %copy-done.4, f32[2,128,128]{2,1,0:T(8,128)S(1)} %copy-done.5, bf16[8,256,256]{2,1,0:T(8,128)(2,1)} %constant.8.clone.inner_ref), custom_call_target="tpu_custom_call" | custom-call | flops 1000000000 | bytes 4194304 | tf_op jit(solution)/shard_map/filter_spectra/pallas_call | solution.py:266
  18.6 0.0 copy-start.2
  18.6 0.0 copy-start.3
  18.6 3.8 %direct.1 = (f32[256,1024]{1,0:T(8,128)}, f32[256,1024]{1,0:T(8,128)}) custom-call(bf16[256,1024]{1,0:T(8,128)(2,1)} %q_ref.2, bf16[256,1024]{1,0:T(8,128)(2,1)} %k_ref.2, bf16[256,1024]{1,0:T(8,128)(2,1)} %v_ref.2, f32[3,3,256]{2,1,0:T(4,128)} %taps_ref.3, f32[1,256]{1,0:T(1,128)} %bitcast.12), custom_call_target="tpu_custom_call" | custom-call | flops 1000000000 | bytes 4194304 | tf_op jit(solution)/shard_map/direct/pallas_call | solution.py:325
  22.4 7.0 %all-to-all-done = bf16[128,9,2,128]{3,2,1,0:T(2,128)(2,1)S(1)} async-done(((bf16[128,9,2,128]{3,2,1,0:T(2,128)(2,1)}), bf16[128,9,2,128]{3,2,1,0:T(2,128)(2,1)S(1)}, u32[]{:S(2)}, u32[]{:S(2)}) %all-to-all-start) | async-done | bytes 589856 | tf_op jit(solution)/shard_map/all_to_all | solution.py:469
  29.4 0.0 copy-done.2
  29.4 0.0 copy-done.3
  29.4 0.0 copy-start.1
  29.4 2.8 %conv.1 = bf16[128,16,128]{2,1,0:T(8,128)(2,1)S(1)} custom-call(bf16[2304,128]{1,0:T(8,128)(2,1)S(1)} %bitcast.8, bf16[8,256,256]{2,1,0:T(8,128)(2,1)S(1)} %copy-done.3, bf16[8,256,128]{2,1,0:T(8,128)(2,1)S(1)} %copy-done.4, f32[2,128,128]{2,1,0:T(8,128)S(1)} %copy-done.5, bf16[8,256,256]{2,1,0:T(8,128)(2,1)S(1)} %copy-done.2), custom_call_target="tpu_custom_call" | custom-call | flops 1000000000 | bytes 8388608 | tf_op jit(solution)/shard_map/conv/pallas_call | solution.py:411
  32.2 0.0 copy-start
  32.2 17.7 %all_to_all.10.returned_ref = bf16[128,16,128]{2,1,0:T(8,128)(2,1)S(1)} all-to-all(bf16[128,16,128]{2,1,0:T(8,128)(2,1)S(1)} %conv.1), channel_id=1, replica_groups=mesh['seq'=8,'ch'=16] {'ch','seq'}, dimensions={0} | all-to-all | bytes 1048576 | tf_op jit(solution)/shard_map/all_to_all | solution.py:469
  49.9 0.0 copy-done.1
  49.9 0.0 copy-done
  49.9 1.1 %final.1 = bf16[256,1024]{1,0:T(8,128)(2,1)} custom-call(bf16[128,16,128]{2,1,0:T(8,128)(2,1)S(1)} %all_to_all.10.returned_ref, f32[256,1024]{1,0:T(8,128)S(1)} %copy-done, f32[256,1024]{1,0:T(8,128)S(1)} %copy-done.1), custom_call_target="tpu_custom_call" | custom-call | flops 1000000 | bytes 2097152 | tf_op jit(solution)/shard_map/final/pallas_call | solution.py:451
Async XLA Ops:
  3.3 11.5 %copy-start.4 = (bf16[8,256,128]{2,1,0:T(8,128)(2,1)S(1)}, bf16[8,256,128]{2,1,0:T(8,128)(2,1)}, u32[]{:S(2)}) copy-start(bf16[8,256,128]{2,1,0:T(8,128)(2,1)} %constant.6.clone.outer_ref) | copy-start | bytes 1572868
  3.3 11.5 %copy-start.5 = (f32[2,128,128]{2,1,0:T(8,128)S(1)}, f32[2,128,128]{2,1,0:T(8,128)}, u32[]{:S(2)}) copy-start(f32[2,128,128]{2,1,0:T(8,128)} %constant.7.clone.turn_ref) | copy-start | bytes 393220
  3.3 11.5 %copy-start.6 = (bf16[1,1,2,131072]{3,2,1,0:T(2,128)(2,1)S(1)}, bf16[1,1,2,131072]{3,2,1,0:T(2,128)(2,1)}, u32[]{:S(2)}) copy-start(bf16[1,1,2,131072]{3,2,1,0:T(2,128)(2,1)} %param.13) | copy-start | bytes 1572868
  3.3 26.1 %all-to-all-start = ((bf16[128,9,2,128]{3,2,1,0:T(2,128)(2,1)}), bf16[128,9,2,128]{3,2,1,0:T(2,128)(2,1)S(1)}, u32[]{:S(2)}, u32[]{:S(2)}) async-start(bf16[128,9,2,128]{3,2,1,0:T(2,128)(2,1)} %bitcast.10), calls=%async_computation | async-start | bytes 1179648 | tf_op jit(solution)/shard_map/all_to_all | solution.py:469
  18.6 10.8 %copy-start.2 = (bf16[8,256,256]{2,1,0:T(8,128)(2,1)S(1)}, bf16[8,256,256]{2,1,0:T(8,128)(2,1)}, u32[]{:S(2)}) copy-start(bf16[8,256,256]{2,1,0:T(8,128)(2,1)} %constant.8.clone.inner_ref) | copy-start | bytes 3145732
  18.6 10.8 %copy-start.3 = (bf16[8,256,256]{2,1,0:T(8,128)(2,1)S(1)}, bf16[8,256,256]{2,1,0:T(8,128)(2,1)}, u32[]{:S(2)}) copy-start(bf16[8,256,256]{2,1,0:T(8,128)(2,1)} %filter_spectra.1.spec_ref) | copy-start | bytes 3145732
  29.4 20.5 %copy-start.1 = (f32[256,1024]{1,0:T(8,128)S(1)}, f32[256,1024]{1,0:T(8,128)}, u32[]{:S(2)}) copy-start(f32[256,1024]{1,0:T(8,128)} %get-tuple-element.32.direct_ref) | copy-start | bytes 3145732
  32.2 17.7 %copy-start = (f32[256,1024]{1,0:T(8,128)S(1)}, f32[256,1024]{1,0:T(8,128)}, u32[]{:S(2)}) copy-start(f32[256,1024]{1,0:T(8,128)} %get-tuple-element.31.query_ref) | copy-start | bytes 3145732

commit v6 on v5

--- a/solution.py
+++ b/solution.py
@@ -15,6 +15,7 @@
 LANES = 128
 TOKENS = 1024
 TILES = TOKENS // LANES
+HALF = TILES // 2
 BLOCKS = 128
 LENGTH = BLOCKS * TOKENS
 CHANNELS = 256
@@ -22,7 +23,7 @@
 CH = 16
 BODY = 2 * TILES
 WIDTH = TILES + 1
-GATE_LIMIT, FILTER_LIMIT, DIRECT_LIMIT, CONV_LIMIT, FINAL_LIMIT = 60, 52, 60, 16, 16
+GATE_LIMIT, FILTER_LIMIT, DIRECT_LIMIT, CONV_LIMIT, FINAL_LIMIT = 60, 60, 60, 16, 16
 ROWS = 64
 STEPS = CHANNELS // ROWS
 DIRECT_ROWS = 128
@@ -47,9 +48,7 @@
     k2 = np.arange(LANES)[None, None, :]
     phase = (lane * (TILES * k2 + tile) % TOKENS) * (step / TOKENS)
     cos, sin = np.cos(phase), np.sin(phase)
-    inner = np.concatenate(
-        [np.concatenate([cos, -sin], axis=2), np.concatenate([sin, cos], axis=2)], axis=1
-    )
+    inner = np.concatenate([cos, -sin], axis=2)
     narrow = ml_dtypes.bfloat16
     return dict(
         outer=outer.astype(narrow),
@@ -196,43 +195,57 @@
     )(q, k, v, taps, skip)
 
 
-def eight_points(re, im):
+def sums_and_differences(outer_ref, c):
+    near, far = outer_ref[c], outer_ref[c + HALF]
+    return jnp.concatenate(
+        [jnp.concatenate([near, far], axis=1), jnp.concatenate([near, -far], axis=1)], axis=0
+    )
+
+
+def complex_table(inner_ref, kc):
+    real = inner_ref[kc]
+    imag = jnp.concatenate([-real[:, LANES:], real[:, :LANES]], axis=1)
+    return jnp.concatenate([real, imag], axis=0)
+
+
+def four_points(re, im):
+    sum_re = [re[i] + re[i + 2] for i in range(2)]
+    sum_im = [im[i] + im[i + 2] for i in range(2)]
+    dif_re = [re[i] - re[i + 2] for i in range(2)]
+    dif_im = [im[i] - im[i + 2] for i in range(2)]
+    out_re = [sum_re[0] + sum_re[1], dif_re[0] + dif_im[1], sum_re[0] - sum_re[1], dif_re[0] - dif_im[1]]
+    out_im = [sum_im[0] + sum_im[1], dif_im[0] - dif_re[1], sum_im[0] - sum_im[1], dif_im[0] + dif_re[1]]
+    return out_re, out_im
+
+
+def eighths(re, im):
     half = math.sqrt(0.5)
-    out_re, out_im = [None] * 8, [None] * 8
-
-    def four_points(re, im, first):
-        sum_re = [re[i] + re[i + 2] for i in range(2)]
-        sum_im = [im[i] + im[i + 2] for i in range(2)]
-        dif_re = [re[i] - re[i + 2] for i in range(2)]
-        dif_im = [im[i] - im[i + 2] for i in range(2)]
-        out_re[first], out_im[first] = sum_re[0] + sum_re[1], sum_im[0] + sum_im[1]
-        out_re[first + 4], out_im[first + 4] = sum_re[0] - sum_re[1], sum_im[0] - sum_im[1]
-        out_re[first + 2], out_im[first + 2] = dif_re[0] + dif_im[1], dif_im[0] - dif_re[1]
-        out_re[first + 6], out_im[first + 6] = dif_re[0] - dif_im[1], dif_im[0] + dif_re[1]
-
-    four_points([re[i] + re[i + 4] for i in range(4)], [im[i] + im[i + 4] for i in range(4)], 0)
-    re = [re[i] - re[i + 4] for i in range(4)]
-    im = [im[i] - im[i + 4] for i in range(4)]
-    turned_re = [re[0], (re[1] + im[1]) * half, im[2], (im[3] - re[3]) * half]
-    turned_im = [im[0], (im[1] - re[1]) * half, -re[2], (re[3] + im[3]) * -half]
-    four_points(turned_re, turned_im, 1)
+    out_re = [re[0], (re[1] + im[1]) * half, im[2], (im[3] - re[3]) * half]
+    out_im = [im[0], (im[1] - re[1]) * half, -re[2], (re[3] + im[3]) * -half]
     return out_re, out_im
 
 
 def forward(signals, outer_ref, turn_ref, section, turned):
-    for c in range(TILES):
-        section[c] = dot(outer_ref[c], signals[c])
+    for c in range(HALF):
+        section[c] = dot(
+            sums_and_differences(outer_ref, c),
+            jnp.concatenate([signals[c], signals[c + HALF]], axis=0),
+        )
     for row in range(0, BLOCKS, 16):
         turn_re, turn_im = turn_ref[0, row : row + 16, :], turn_ref[1, row : row + 16, :]
         for j in range(2):
             half = slice(j * LANES, (j + 1) * LANES)
-            re = [section[c, row : row + 16, half] for c in range(TILES)]
-            im = [section[c, BLOCKS + row : BLOCKS + row + 16, half] for c in range(TILES)]
-            re, im = eight_points(re, im)
+            parts = [
+                [section[c, m * BLOCKS + row : m * BLOCKS + row + 16, half] for c in range(HALF)]
+                for m in range(4)
+            ]
+            even = four_points(parts[0], parts[1])
+            odd = four_points(*eighths(parts[2], parts[3]))
             at = slice(j * BLOCKS + row, j * BLOCKS + row + 16)
             for kc in range(TILES):
-                turned[kc, at, :LANES] = (re[kc] * turn_re - im[kc] * turn_im).astype(BF16)
-                turned[kc, at, LANES:] = (re[kc] * turn_im + im[kc] * turn_re).astype(BF16)
+                re, im = (part[kc // 2] for part in (odd if kc % 2 else even))
+                turned[kc, at, :LANES] = (re * turn_re - im * turn_im).astype(BF16)
+                turned[kc, at, LANES:] = (re * turn_im + im * turn_re).astype(BF16)
 
 
 def filter_body(
@@ -253,7 +266,7 @@
     forward(signals, outer_ref, turn_ref, section, turned)
     out_copies = []
     for kc in range(TILES):
-        spec_buf[kc] = (dot(turned[kc], inner_ref[kc]) * (1.0 / LENGTH)).astype(BF16)
+        spec_buf[kc] = (dot(turned[kc], complex_table(inner_ref, kc)) * (1.0 / LENGTH)).astype(BF16)
         out_copies.append(pltpu.make_async_copy(spec_buf.at[kc], spec_ref.at[kc], spec_sems.at[kc]))
         out_copies[-1].start()
     for copy in out_copies:
@@ -270,7 +283,7 @@
         [
             pltpu.VMEM(spec, BF16),
             pltpu.VMEM((2 * BLOCKS * TILES, LANES), F32),
-            pltpu.VMEM(spec, F32),
+            pltpu.VMEM((HALF, 4 * BLOCKS, 2 * LANES), F32),
             pltpu.VMEM(spec, BF16),
             pltpu.SemaphoreType.DMA((TILES,)),
         ],
@@ -348,7 +361,7 @@
 
 def conv_body(
     arrived_ref, spec_ref, outer_ref, turn_ref, inner_ref, out_ref,
-    rows, section, turned, back, edges
+    rows, section, turned, product, back, edges
 ):
     rows[...] = arrived_ref[...].astype(F32)
 
@@ -373,36 +386,43 @@
         signals.append(jnp.concatenate(halves, axis=1).astype(BF16))
     forward(signals, outer_ref, turn_ref, section, turned)
     for kc in range(TILES):
-        spectrum = dot(turned[kc], inner_ref[kc])
+        table = complex_table(inner_ref, kc)
+        spectrum = dot(turned[kc], table)
         re, im = spectrum[:, :LANES], spectrum[:, LANES:]
         spec = spec_ref[kc].astype(F32)
         filt_re, filt_im = spec[:, :LANES], spec[:, LANES:]
         parts = [re * filt_re - im * filt_im, re * filt_im + im * filt_re]
-        section[kc] = dot_back(jnp.concatenate(parts, axis=1).astype(BF16), inner_ref[kc])
+        product[kc] = dot_back(jnp.concatenate(parts, axis=1).astype(BF16), table)
     for row in range(0, BLOCKS, 16):
         turn_re, turn_im = turn_ref[0, row : row + 16, :], turn_ref[1, row : row + 16, :]
         for j in range(2):
             at = slice(j * BLOCKS + row, j * BLOCKS + row + 16)
             re, im = [], []
             for kc in range(TILES):
-                part_re, part_im = section[kc, at, :LANES], section[kc, at, LANES:]
+                part_re, part_im = product[kc, at, :LANES], product[kc, at, LANES:]
                 re.append(part_re * turn_re + part_im * turn_im)
                 im.append(part_im * turn_re - part_re * turn_im)
-            im, re = eight_points(im, re)
+            even_im, even_re = four_points(im[0::2], re[0::2])
+            odd_im, odd_re = eighths(*four_points(im[1::2], re[1::2]))
             half = slice(j * LANES, (j + 1) * LANES)
-            for c in range(TILES):
-                back[c, row : row + 16, half] = re[c].astype(BF16)
-                back[c, BLOCKS + row : BLOCKS + row + 16, half] = im[c].astype(BF16)
-    for c in range(TILES):
+            for m, part in enumerate((even_re, even_im, odd_re, odd_im)):
+                for c in range(HALF):
+                    back[c, m * BLOCKS + row : m * BLOCKS + row + 16, half] = part[c].astype(BF16)
+    for c in range(HALF):
         result = lax.dot_general(
-            outer_ref[c], back[c], (((0,), (0,)), ((), ())), preferred_element_type=F32
+            sums_and_differences(outer_ref, c),
+            back[c],
+            (((0,), (0,)), ((), ())),
+            preferred_element_type=F32,
         )
-        for j in range(2):
-            half = result[:, j * LANES : (j + 1) * LANES]
-            if c == 0:
-                start = edges[0, j] * (half.astype(BF16).astype(F32) + edges[1, j])
-                half = jnp.where(lanes_of(half) < 2, start, half)
-            rows[pl.ds(j * TILES + c, BLOCKS, stride=BODY), :] = half
+        for tile in (c, c + HALF):
+            for j in range(2):
+                first = BLOCKS if tile >= HALF else 0
+                half = result[first : first + BLOCKS, j * LANES : (j + 1) * LANES]
+                if tile == 0:
+                    start = edges[0, j] * (half.astype(BF16).astype(F32) + edges[1, j])
+                    half = jnp.where(lanes_of(half) < 2, start, half)
+                rows[pl.ds(j * TILES + tile, BLOCKS, stride=BODY), :] = half
     out_ref[...] = rows[: BLOCKS * BODY, :].reshape(BLOCKS, BODY, LANES).astype(BF16)
 
 
@@ -414,9 +434,10 @@
         shape((BLOCKS, BODY, LANES), BF16),
         [
             pltpu.VMEM((BLOCKS * 2 * WIDTH, LANES), F32),
+            pltpu.VMEM((HALF, 4 * BLOCKS, 2 * LANES), F32),
+            pltpu.VMEM((TILES, 2 * BLOCKS, 2 * LANES), BF16),
             pltpu.VMEM((TILES, 2 * BLOCKS, 2 * LANES), F32),
-            pltpu.VMEM((TILES, 2 * BLOCKS, 2 * LANES), BF16),
-            pltpu.VMEM((TILES, 2 * BLOCKS, 2 * LANES), BF16),
+            pltpu.VMEM((HALF, 4 * BLOCKS, 2 * LANES), BF16),
             pltpu.VMEM((2, 2, BLOCKS, LANES), F32),
         ],
         [VMEM] * 5,

time: 51.2 us -> 51.1 us (level)
  no operation moved by 1% of the time
where the time goes in v6:
time: 51.1 us; the launch traced here: 50.8 us
  blocking collectives  17.7 us (35%)
  Pallas kernels  14.6 us (29%)
  starting transfers between devices  11.5 us (23%)
  waiting for transfers between devices  6.87 us (13%)
    all_to_all x1, blocking collectives, exchange(): lax.all_to_all(messages, OWNERS, split_axis=0, concat_axis=0, tiled=True)  17.7 us
    all_to_all x1, starting transfers between devices, exchange(): lax.all_to_all(messages, OWNERS, split_axis=0, concat_axis=0, tiled=True)  11.5 us
    all_to_all x1, waiting for transfers between devices, exchange(): lax.all_to_all(messages, OWNERS, split_axis=0, concat_axis=0, tiled=True)  6.87 us
    pallas_call x1, Pallas kernels, filter_spectra(): call(filter_body, 'filter_spectra', shape(spec, BF16), [pltpu.VMEM(spec,...  3.87 us
    pallas_call x1, Pallas kernels, direct(): call(direct_body, 'direct', (shape((CHANNELS, TOKENS), F32), shape((CHANN...  3.76 us
    pallas_call x1, Pallas kernels, gate(): call(gate_body, 'gate', shape((CHANNELS * WIDTH, LANES), BF16), [pltpu.VM...  3.31 us
    pallas_call x1, Pallas kernels, conv(): call(conv_body, 'conv', shape((BLOCKS, BODY, LANES), BF16), [pltpu.VMEM((...  2.61 us
    pallas_call x1, Pallas kernels, final(): call(final_body, 'final', shape((CHANNELS, TOKENS), BF16), [pltpu.VMEM((R...  1.06 us
  transfers between devices with their start and end apart: 1, of which 1 were waited for; matrix products, arithmetic and copies ran while one was open for 0% of the time, Pallas kernels for 15%

profile of v6, /device:TPU:1, one launch (start us, length us, event | category | flops | bytes accessed | tf_op | source)
XLA Modules:
  0.0 50.8 jit_solution(1686678018183410268)
XLA Ops:
  0.0 3.3 %gate.1 = bf16[2304,128]{1,0:T(8,128)(2,1)} custom-call(bf16[256,1024]{1,0:T(8,128)(2,1)} %q_ref.2, bf16[256,1024]{1,0:T(8,128)(2,1)} %k_ref.2, bf16[256,1024]{1,0:T(8,128)(2,1)} %v_ref.2, f32[3,3,256]{2,1,0:T(4,128)} %taps_ref.3, f32[1,256]{1,0:T(1,128)} %bitcast.10), custom_call_target="tpu_custom_call" | custom-call | flops 10000000 | bytes 2097152 | tf_op jit(solution)/shard_map/gate/pallas_call | solution.py:175
  3.3 11.5 %all-to-all-start = ((bf16[128,9,2,128]{3,2,1,0:T(2,128)(2,1)}), bf16[128,9,2,128]{3,2,1,0:T(2,128)(2,1)S(1)}, u32[]{:S(2)}, u32[]{:S(2)}) async-start(bf16[128,9,2,128]{3,2,1,0:T(2,128)(2,1)} %bitcast.9), calls=%async_computation | async-start | bytes 1179648 | tf_op jit(solution)/shard_map/all_to_all | solution.py:490
  14.8 3.9 %filter_spectra.1.spec_ref = bf16[8,256,256]{2,1,0:T(8,128)(2,1)} custom-call(bf16[2048,128]{1,0:T(8,128)(2,1)} %bitcast.12, bf16[8,256,128]{2,1,0:T(8,128)(2,1)} %constant.6.clone.outer_ref, f32[2,128,128]{2,1,0:T(8,128)} %constant.7.clone.turn_ref, bf16[8,128,256]{2,1,0:T(8,128)(2,1)} %constant.8.clone.inner_ref), custom_call_target="tpu_custom_call" | custom-call | flops 1000000000 | bytes 4194304 | tf_op jit(solution)/shard_map/filter_spectra/pallas_call | solution.py:279
  18.7 0.0 copy-start.2
  18.7 0.0 copy-start.3
  18.7 0.0 copy-start.4
  18.7 0.0 copy-start.5
  18.8 3.8 %direct.1 = (f32[256,1024]{1,0:T(8,128)}, f32[256,1024]{1,0:T(8,128)}) custom-call(bf16[256,1024]{1,0:T(8,128)(2,1)} %q_ref.2, bf16[256,1024]{1,0:T(8,128)(2,1)} %k_ref.2, bf16[256,1024]{1,0:T(8,128)(2,1)} %v_ref.2, f32[3,3,256]{2,1,0:T(4,128)} %taps_ref.3, f32[1,256]{1,0:T(1,128)} %bitcast.11), custom_call_target="tpu_custom_call" | custom-call | flops 1000000000 | bytes 4194304 | tf_op jit(solution)/shard_map/direct/pallas_call | solution.py:338
  22.5 6.9 %all-to-all-done = bf16[128,9,2,128]{3,2,1,0:T(2,128)(2,1)S(1)} async-done(((bf16[128,9,2,128]{3,2,1,0:T(2,128)(2,1)}), bf16[128,9,2,128]{3,2,1,0:T(2,128)(2,1)S(1)}, u32[]{:S(2)}, u32[]{:S(2)}) %all-to-all-start) | async-done | bytes 589856 | tf_op jit(solution)/shard_map/all_to_all | solution.py:490
  29.4 0.0 copy-done.2
  29.4 0.0 copy-done.3
  29.4 0.0 copy-done.4
  29.4 0.0 copy-done.5
  29.4 0.0 copy-start.1
  29.4 2.6 %conv.1 = bf16[128,16,128]{2,1,0:T(8,128)(2,1)S(1)} custom-call(bf16[2304,128]{1,0:T(8,128)(2,1)S(1)} %bitcast.8, bf16[8,256,256]{2,1,0:T(8,128)(2,1)S(1)} %copy-done.5, bf16[8,256,128]{2,1,0:T(8,128)(2,1)S(1)} %copy-done.3, f32[2,128,128]{2,1,0:T(8,128)S(1)} %copy-done.4, bf16[8,128,256]{2,1,0:T(8,128)(2,1)S(1)} %copy-done.2), custom_call_target="tpu_custom_call" | custom-call | flops 1000000000 | bytes 8388608 | tf_op jit(solution)/shard_map/conv/pallas_call | solution.py:431
  32.0 0.0 copy-start
  32.0 17.7 %all_to_all.10.returned_ref = bf16[128,16,128]{2,1,0:T(8,128)(2,1)S(1)} all-to-all(bf16[128,16,128]{2,1,0:T(8,128)(2,1)S(1)} %conv.1), channel_id=1, replica_groups=mesh['seq'=8,'ch'=16] {'ch','seq'}, dimensions={0} | all-to-all | bytes 1048576 | tf_op jit(solution)/shard_map/all_to_all | solution.py:490
  49.8 0.0 copy-done.1
  49.8 0.0 copy-done
  49.8 1.1 %final.1 = bf16[256,1024]{1,0:T(8,128)(2,1)} custom-call(bf16[128,16,128]{2,1,0:T(8,128)(2,1)S(1)} %all_to_all.10.returned_ref, f32[256,1024]{1,0:T(8,128)S(1)} %copy-done, f32[256,1024]{1,0:T(8,128)S(1)} %copy-done.1), custom_call_target="tpu_custom_call" | custom-call | flops 1000000 | bytes 2097152 | tf_op jit(solution)/shard_map/final/pallas_call | solution.py:472
Async XLA Ops:
  3.3 26.1 %all-to-all-start = ((bf16[128,9,2,128]{3,2,1,0:T(2,128)(2,1)}), bf16[128,9,2,128]{3,2,1,0:T(2,128)(2,1)S(1)}, u32[]{:S(2)}, u32[]{:S(2)}) async-start(bf16[128,9,2,128]{3,2,1,0:T(2,128)(2,1)} %bitcast.9), calls=%async_computation | async-start | bytes 1179648 | tf_op jit(solution)/shard_map/all_to_all | solution.py:490
  18.7 10.7 %copy-start.2 = (bf16[8,128,256]{2,1,0:T(8,128)(2,1)S(1)}, bf16[8,128,256]{2,1,0:T(8,128)(2,1)}, u32[]{:S(2)}) copy-start(bf16[8,128,256]{2,1,0:T(8,128)(2,1)} %constant.8.clone.inner_ref) | copy-start | bytes 1572868
  18.7 10.7 %copy-start.3 = (bf16[8,256,128]{2,1,0:T(8,128)(2,1)S(1)}, bf16[8,256,128]{2,1,0:T(8,128)(2,1)}, u32[]{:S(2)}) copy-start(bf16[8,256,128]{2,1,0:T(8,128)(2,1)} %constant.6.clone.outer_ref) | copy-start | bytes 1572868
  18.7 10.7 %copy-start.4 = (f32[2,128,128]{2,1,0:T(8,128)S(1)}, f32[2,128,128]{2,1,0:T(8,128)}, u32[]{:S(2)}) copy-start(f32[2,128,128]{2,1,0:T(8,128)} %constant.7.clone.turn_ref) | copy-start | bytes 393220
  18.7 10.7 %copy-start.5 = (bf16[8,256,256]{2,1,0:T(8,128)(2,1)S(1)}, bf16[8,256,256]{2,1,0:T(8,128)(2,1)}, u32[]{:S(2)}) copy-start(bf16[8,256,256]{2,1,0:T(8,128)(2,1)} %filter_spectra.1.spec_ref) | copy-start | bytes 3145732
  29.4 20.4 %copy-start.1 = (f32[256,1024]{1,0:T(8,128)S(1)}, f32[256,1024]{1,0:T(8,128)}, u32[]{:S(2)}) copy-start(f32[256,1024]{1,0:T(8,128)} %get-tuple-element.32.direct_ref) | copy-start | bytes 3145732
  32.0 17.7 %copy-start = (f32[256,1024]{1,0:T(8,128)S(1)}, f32[256,1024]{1,0:T(8,128)}, u32[]{:S(2)}) copy-start(f32[256,1024]{1,0:T(8,128)} %get-tuple-element.31.query_ref) | copy-start | bytes 3145732

commit v7 on v6

--- a/solution.py
+++ b/solution.py
@@ -29,7 +29,8 @@
 DIRECT_ROWS = 128
 DIRECT_STEPS = CHANNELS // DIRECT_ROWS
 AXES = ("seq", "ch")
-OWNERS = ("ch", "seq")
+ORDER = (0, 8, 4, 12, 2, 10, 6, 14, 1, 9, 5, 13, 3, 11, 7, 15)
+PLACE = tuple(ORDER.index(g) for g in range(CH))
 VMEM = pl.BlockSpec(memory_space=pltpu.VMEM)
 HBM = pl.BlockSpec(memory_space=pltpu.HBM)
 
@@ -38,7 +39,7 @@
     step = 2.0 * math.pi
     tile = np.arange(TILES)[:, None, None]
     k1 = np.arange(BLOCKS)[None, :, None]
-    block = np.arange(BLOCKS).reshape(SEQ, CH).T.reshape(1, 1, BLOCKS)
+    block = np.arange(BLOCKS).reshape(SEQ, CH).T[list(ORDER)].reshape(1, 1, BLOCKS)
     phase = ((TILES * block + tile) * (4 * k1 + 1) % (4 * TOKENS)) * (step / (4 * TOKENS))
     outer = np.concatenate([np.cos(phase), -np.sin(phase)], axis=1)
     lane = np.arange(LANES)[None, :]
@@ -130,6 +131,11 @@
     far = jnp.where(lane < 2, back2[:, :LANES], 0.0)
     onward = taps[1] * near + taps[2] * far
     return sums, sums[:, :LANES] - onward, onward
+
+
+def ordered(x):
+    size = CHANNELS // CH
+    return jnp.concatenate([x[g * size : (g + 1) * size] for g in ORDER], axis=0)
 
 
 def gate_body(
@@ -161,13 +167,13 @@
     _, query_own, query_onward = with_edges(query, query_taps)
     gated = key * value
     for c in range(TILES):
-        rows[pl.ds(c, CHANNELS, stride=WIDTH), :] = gated[:, c * LANES : (c + 1) * LANES]
+        rows[pl.ds(c, CHANNELS, stride=WIDTH), :] = ordered(gated[:, c * LANES : (c + 1) * LANES])
     lane = lanes_of(key_own)
     own = jnp.where(lane < 2, key_own, pltpu.roll(query_own, 2, 1))
     own_value = pltpu.roll(jnp.where(lane < 2, value_own, cols[:, 9:10]), 4, 1)
     onward = key_onward + pltpu.roll(query_onward, 2, 1) + pltpu.roll(value_onward, 4, 1)
     edge = jnp.where(lane < 8, own_value, pltpu.roll(onward, 8, 1))
-    rows[pl.ds(TILES, CHANNELS, stride=WIDTH), :] = jnp.where(lane < 4, own, edge)
+    rows[pl.ds(TILES, CHANNELS, stride=WIDTH), :] = ordered(jnp.where(lane < 4, own, edge))
     out_ref[...] = rows[...].astype(BF16)
 
 
@@ -259,7 +265,7 @@
         for j in range(2):
             parts = [
                 rows[pl.ds(2 * (g * TILES + c) + j, SEQ, stride=2 * TILES * CH), :]
-                for g in range(CH)
+                for g in ORDER
             ]
             halves.append(jnp.concatenate(parts, axis=0))
         signals.append(jnp.concatenate(halves, axis=1).astype(BF16))
@@ -374,10 +380,12 @@
         if c == 0:
             for j in range(2):
                 edge = arrived(j, TILES)
-                last = edge[BLOCKS - SEQ :]
-                step = lax.broadcasted_iota(jnp.int32, last.shape, 0)
-                last = jnp.where(step == 0, 0.0, pltpu.roll(last, 1, 0))
-                before = jnp.concatenate([last, edge[: BLOCKS - SEQ]], axis=0)
+                pieces = [edge[n * SEQ : (n + 1) * SEQ] for n in range(CH)]
+                step = lax.broadcasted_iota(jnp.int32, pieces[0].shape, 0)
+                last = jnp.where(step == 0, 0.0, pltpu.roll(pieces[PLACE[CH - 1]], 1, 0))
+                before = jnp.concatenate(
+                    [pieces[PLACE[g - 1]] if g else last for g in ORDER], axis=0
+                )
                 total = edge + pltpu.roll(before, LANES - 8, 1)
                 gated = (total * pltpu.roll(total, LANES - 4, 1)).astype(BF16).astype(F32)
                 edges[0, j] = pltpu.roll(total, LANES - 2, 1)
@@ -452,7 +460,10 @@
     copies = []
     for step in range(STEPS):
         at = slice(step * ROWS, (step + 1) * ROWS)
-        message = returned_ref[step * ROWS // 2 : (step + 1) * ROWS // 2].astype(F32)
+        groups = range(step * ROWS // (2 * SEQ), (step + 1) * ROWS // (2 * SEQ))
+        message = jnp.concatenate(
+            [returned_ref[PLACE[g] * SEQ : (PLACE[g] + 1) * SEQ] for g in groups], axis=0
+        ).astype(F32)
         rows[...] = message.reshape(ROWS * TILES, LANES)
         for c in range(TILES):
             lanes = slice(c * LANES, (c + 1) * LANES)
@@ -487,7 +498,10 @@
 
 
 def exchange(messages):
-    return lax.all_to_all(messages, OWNERS, split_axis=0, concat_axis=0, tiled=True)
+    group = [s * CH + g for g in ORDER for s in range(SEQ)]
+    return lax.all_to_all(
+        messages, AXES, split_axis=0, concat_axis=0, axis_index_groups=[group], tiled=True
+    )
 
 
 def shards(consts, q, k, v, short_taps, long_filter, skip_gain):

time: 51.1 us -> 50.3 us (0.984)
  waiting for transfers between devices: 6.87 us -> 5.69 us
    all_to_all x1, waiting for transfers between devices: 6.87 us -> 5.69 us  [exchange(): lax.all_to_all(messages, AXES, split_axis=0, concat_axis=0, axis_index_gr...]
where the time goes in v7:
time: 50.3 us; the launch traced here: 50.1 us
  blocking collectives  18.1 us (36%)
  Pallas kernels  14.7 us (29%)
  starting transfers between devices  11.5 us (23%)
  waiting for transfers between devices  5.69 us (11%)
    all_to_all x1, blocking collectives, exchange(): lax.all_to_all(messages, AXES, split_axis=0, concat_axis=0, axis_index_gr...  18.1 us
    all_to_all x1, starting transfers between devices, exchange(): lax.all_to_all(messages, AXES, split_axis=0, concat_axis=0, axis_index_gr...  11.5 us
    all_to_all x1, waiting for transfers between devices, exchange(): lax.all_to_all(messages, AXES, split_axis=0, concat_axis=0, axis_index_gr...  5.69 us
    pallas_call x1, Pallas kernels, filter_spectra(): call(filter_body, 'filter_spectra', shape(spec, BF16), [pltpu.VMEM(spec,...  3.94 us
    pallas_call x1, Pallas kernels, direct(): call(direct_body, 'direct', (shape((CHANNELS, TOKENS), F32), shape((CHANN...  3.76 us
    pallas_call x1, Pallas kernels, gate(): call(gate_body, 'gate', shape((CHANNELS * WIDTH, LANES), BF16), [pltpu.VM...  3.31 us
    pallas_call x1, Pallas kernels, conv(): call(conv_body, 'conv', shape((BLOCKS, BODY, LANES), BF16), [pltpu.VMEM((...  2.65 us
    pallas_call x1, Pallas kernels, final(): call(final_body, 'final', shape((CHANNELS, TOKENS), BF16), [pltpu.VMEM((R...  1.06 us
  transfers between devices with their start and end apart: 1, of which 1 were waited for; matrix products, arithmetic and copies ran while one was open for 0% of the time, Pallas kernels for 15%

profile of v7, /device:TPU:1, one launch (start us, length us, event | category | flops | bytes accessed | tf_op | source)
XLA Modules:
  0.0 50.1 jit_solution(9910483280942762778)
XLA Ops:
  0.0 3.3 %gate.1 = bf16[2304,128]{1,0:T(8,128)(2,1)} custom-call(bf16[256,1024]{1,0:T(8,128)(2,1)} %q_ref.2, bf16[256,1024]{1,0:T(8,128)(2,1)} %k_ref.2, bf16[256,1024]{1,0:T(8,128)(2,1)} %v_ref.2, f32[3,3,256]{2,1,0:T(4,128)} %taps_ref.3, f32[1,256]{1,0:T(1,128)} %bitcast.10), custom_call_target="tpu_custom_call" | custom-call | flops 10000000 | bytes 2097152 | tf_op jit(solution)/shard_map/gate/pallas_call | solution.py:181
  3.3 11.5 %all-to-all-start = ((bf16[128,9,2,128]{3,2,1,0:T(2,128)(2,1)}), bf16[128,9,2,128]{3,2,1,0:T(2,128)(2,1)S(1)}, u32[]{:S(2)}, u32[]{:S(2)}) async-start(bf16[128,9,2,128]{3,2,1,0:T(2,128)(2,1)} %bitcast.9), calls=%async_computation | async-start | bytes 1179648 | tf_op jit(solution)/shard_map/all_to_all | solution.py:502
  14.8 3.9 %filter_spectra.1.spec_ref = bf16[8,256,256]{2,1,0:T(8,128)(2,1)} custom-call(bf16[2048,128]{1,0:T(8,128)(2,1)} %bitcast.12, bf16[8,256,128]{2,1,0:T(8,128)(2,1)} %constant.6.clone.outer_ref, f32[2,128,128]{2,1,0:T(8,128)} %constant.7.clone.turn_ref, bf16[8,128,256]{2,1,0:T(8,128)(2,1)} %constant.8.clone.inner_ref), custom_call_target="tpu_custom_call" | custom-call | flops 1000000000 | bytes 4194304 | tf_op jit(solution)/shard_map/filter_spectra/pallas_call | solution.py:285
  18.8 0.0 copy-start.2
  18.8 0.0 copy-start.3
  18.8 0.0 copy-start.4
  18.8 0.0 copy-start.5
  18.8 3.8 %direct.1 = (f32[256,1024]{1,0:T(8,128)}, f32[256,1024]{1,0:T(8,128)}) custom-call(bf16[256,1024]{1,0:T(8,128)(2,1)} %q_ref.2, bf16[256,1024]{1,0:T(8,128)(2,1)} %k_ref.2, bf16[256,1024]{1,0:T(8,128)(2,1)} %v_ref.2, f32[3,3,256]{2,1,0:T(4,128)} %taps_ref.3, f32[1,256]{1,0:T(1,128)} %bitcast.11), custom_call_target="tpu_custom_call" | custom-call | flops 1000000000 | bytes 4194304 | tf_op jit(solution)/shard_map/direct/pallas_call | solution.py:344
  22.6 5.7 %all-to-all-done = bf16[128,9,2,128]{3,2,1,0:T(2,128)(2,1)S(1)} async-done(((bf16[128,9,2,128]{3,2,1,0:T(2,128)(2,1)}), bf16[128,9,2,128]{3,2,1,0:T(2,128)(2,1)S(1)}, u32[]{:S(2)}, u32[]{:S(2)}) %all-to-all-start) | async-done | bytes 589856 | tf_op jit(solution)/shard_map/all_to_all | solution.py:502
  28.3 0.0 copy-done.2
  28.3 0.0 copy-done.3
  28.3 0.0 copy-done.4
  28.3 0.0 copy-done.5
  28.3 0.0 copy-start.1
  28.3 2.6 %conv.1 = bf16[128,16,128]{2,1,0:T(8,128)(2,1)S(1)} custom-call(bf16[2304,128]{1,0:T(8,128)(2,1)S(1)} %bitcast.8, bf16[8,256,256]{2,1,0:T(8,128)(2,1)S(1)} %copy-done.5, bf16[8,256,128]{2,1,0:T(8,128)(2,1)S(1)} %copy-done.3, f32[2,128,128]{2,1,0:T(8,128)S(1)} %copy-done.4, bf16[8,128,256]{2,1,0:T(8,128)(2,1)S(1)} %copy-done.2), custom_call_target="tpu_custom_call" | custom-call | flops 1000000000 | bytes 8388608 | tf_op jit(solution)/shard_map/conv/pallas_call | solution.py:439
  31.0 0.0 copy-start
  31.0 18.1 %all_to_all.10.returned_ref = bf16[128,16,128]{2,1,0:T(8,128)(2,1)S(1)} all-to-all(bf16[128,16,128]{2,1,0:T(8,128)(2,1)S(1)} %conv.1), channel_id=1, replica_groups={{0,16,32,48,64,80,96,112,8,24,40,56,72,88,104,120,4,20,36,52,68,84,100,..., dimensions={0} | all-to-all | bytes 1048576 | tf_op jit(solution)/shard_map/all_to_all | solution.py:502
  49.0 0.0 copy-done.1
  49.0 0.0 copy-done
  49.0 1.1 %final.1 = bf16[256,1024]{1,0:T(8,128)(2,1)} custom-call(bf16[128,16,128]{2,1,0:T(8,128)(2,1)S(1)} %all_to_all.10.returned_ref, f32[256,1024]{1,0:T(8,128)S(1)} %copy-done, f32[256,1024]{1,0:T(8,128)S(1)} %copy-done.1), custom_call_target="tpu_custom_call" | custom-call | flops 1000000 | bytes 2097152 | tf_op jit(solution)/shard_map/final/pallas_call | solution.py:483
Async XLA Ops:
  3.3 25.0 %all-to-all-start = ((bf16[128,9,2,128]{3,2,1,0:T(2,128)(2,1)}), bf16[128,9,2,128]{3,2,1,0:T(2,128)(2,1)S(1)}, u32[]{:S(2)}, u32[]{:S(2)}) async-start(bf16[128,9,2,128]{3,2,1,0:T(2,128)(2,1)} %bitcast.9), calls=%async_computation | async-start | bytes 1179648 | tf_op jit(solution)/shard_map/all_to_all | solution.py:502
  18.8 9.5 %copy-start.2 = (bf16[8,128,256]{2,1,0:T(8,128)(2,1)S(1)}, bf16[8,128,256]{2,1,0:T(8,128)(2,1)}, u32[]{:S(2)}) copy-start(bf16[8,128,256]{2,1,0:T(8,128)(2,1)} %constant.8.clone.inner_ref) | copy-start | bytes 1572868
  18.8 9.5 %copy-start.3 = (bf16[8,256,128]{2,1,0:T(8,128)(2,1)S(1)}, bf16[8,256,128]{2,1,0:T(8,128)(2,1)}, u32[]{:S(2)}) copy-start(bf16[8,256,128]{2,1,0:T(8,128)(2,1)} %constant.6.clone.outer_ref) | copy-start | bytes 1572868
  18.8 9.5 %copy-start.4 = (f32[2,128,128]{2,1,0:T(8,128)S(1)}, f32[2,128,128]{2,1,0:T(8,128)}, u32[]{:S(2)}) copy-start(f32[2,128,128]{2,1,0:T(8,128)} %constant.7.clone.turn_ref) | copy-start | bytes 393220
  18.8 9.5 %copy-start.5 = (bf16[8,256,256]{2,1,0:T(8,128)(2,1)S(1)}, bf16[8,256,256]{2,1,0:T(8,128)(2,1)}, u32[]{:S(2)}) copy-start(bf16[8,256,256]{2,1,0:T(8,128)(2,1)} %filter_spectra.1.spec_ref) | copy-start | bytes 3145732
  28.3 20.7 %copy-start.1 = (f32[256,1024]{1,0:T(8,128)S(1)}, f32[256,1024]{1,0:T(8,128)}, u32[]{:S(2)}) copy-start(f32[256,1024]{1,0:T(8,128)} %get-tuple-element.32.direct_ref) | copy-start | bytes 3145732
  31.0 18.1 %copy-start = (f32[256,1024]{1,0:T(8,128)S(1)}, f32[256,1024]{1,0:T(8,128)}, u32[]{:S(2)}) copy-start(f32[256,1024]{1,0:T(8,128)} %get-tuple-element.31.query_ref) | copy-start | bytes 3145732

commit v8 on v7

--- a/solution.py
+++ b/solution.py
@@ -29,7 +29,7 @@
 DIRECT_ROWS = 128
 DIRECT_STEPS = CHANNELS // DIRECT_ROWS
 AXES = ("seq", "ch")
-ORDER = (0, 8, 4, 12, 2, 10, 6, 14, 1, 9, 5, 13, 3, 11, 7, 15)
+ORDER = (9, 1, 13, 5, 11, 3, 15, 7, 8, 0, 12, 4, 10, 2, 14, 6)
 PLACE = tuple(ORDER.index(g) for g in range(CH))
 VMEM = pl.BlockSpec(memory_space=pltpu.VMEM)
 HBM = pl.BlockSpec(memory_space=pltpu.HBM)
@@ -149,10 +149,12 @@
         ]
         return [pltpu.make_async_copy(a, b, small.at[i]) for i, (a, b) in enumerate(pairs)]
 
-    copies = small_copies() + [
+    first, last = small_copies()[:2], small_copies()[2:]
+    copies = first + [
         pltpu.make_async_copy(k_ref, k_buf, sems.at[0]),
         pltpu.make_async_copy(v_ref, v_buf, sems.at[1]),
     ]
+    copies += last
     for copy in copies:
         copy.start()
     for copy in copies[:2]:

time: 50.3 us -> 49.7 us (0.988)
  transfers between devices with their start and end apart: 1 -> 1, of which waited for: 1 -> 1; matrix products, arithmetic and copies ran while one was open for 0% -> 0% of each run, Pallas kernels for 15% -> 16%
where the time goes in v8:
time: 49.7 us; the launch traced here: 49.5 us
  blocking collectives  17.6 us (35%)
  Pallas kernels  14.6 us (29%)
  starting transfers between devices  11.5 us (23%)
  waiting for transfers between devices  5.54 us (11%)
    all_to_all x1, blocking collectives, exchange(): lax.all_to_all(messages, AXES, split_axis=0, concat_axis=0, axis_index_gr...  17.6 us
    all_to_all x1, starting transfers between devices, exchange(): lax.all_to_all(messages, AXES, split_axis=0, concat_axis=0, axis_index_gr...  11.5 us
    all_to_all x1, waiting for transfers between devices, exchange(): lax.all_to_all(messages, AXES, split_axis=0, concat_axis=0, axis_index_gr...  5.54 us
    pallas_call x1, Pallas kernels, filter_spectra(): call(filter_body, 'filter_spectra', shape(spec, BF16), [pltpu.VMEM(spec,...  3.92 us
    pallas_call x1, Pallas kernels, direct(): call(direct_body, 'direct', (shape((CHANNELS, TOKENS), F32), shape((CHANN...  3.76 us
    pallas_call x1, Pallas kernels, gate(): call(gate_body, 'gate', shape((CHANNELS * WIDTH, LANES), BF16), [pltpu.VM...  3.27 us
    pallas_call x1, Pallas kernels, conv(): call(conv_body, 'conv', shape((BLOCKS, BODY, LANES), BF16), [pltpu.VMEM((...  2.62 us
    pallas_call x1, Pallas kernels, final(): call(final_body, 'final', shape((CHANNELS, TOKENS), BF16), [pltpu.VMEM((R...  1.06 us
  transfers between devices with their start and end apart: 1, of which 1 were waited for; matrix products, arithmetic and copies ran while one was open for 0% of the time, Pallas kernels for 16%

profile of v8, /device:TPU:1, one launch (start us, length us, event | category | flops | bytes accessed | tf_op | source)
XLA Modules:
  0.0 49.5 jit_solution(6210676015792204427)
XLA Ops:
  0.0 3.3 %gate.1 = bf16[2304,128]{1,0:T(8,128)(2,1)} custom-call(bf16[256,1024]{1,0:T(8,128)(2,1)} %q_ref.2, bf16[256,1024]{1,0:T(8,128)(2,1)} %k_ref.2, bf16[256,1024]{1,0:T(8,128)(2,1)} %v_ref.2, f32[3,3,256]{2,1,0:T(4,128)} %taps_ref.3, f32[1,256]{1,0:T(1,128)} %bitcast.10), custom_call_target="tpu_custom_call" | custom-call | flops 10000000 | bytes 2097152 | tf_op jit(solution)/shard_map/gate/pallas_call | solution.py:183
  3.3 11.5 %all-to-all-start = ((bf16[128,9,2,128]{3,2,1,0:T(2,128)(2,1)}), bf16[128,9,2,128]{3,2,1,0:T(2,128)(2,1)S(1)}, u32[]{:S(2)}, u32[]{:S(2)}) async-start(bf16[128,9,2,128]{3,2,1,0:T(2,128)(2,1)} %bitcast.9), calls=%async_computation | async-start | bytes 1179648 | tf_op jit(solution)/shard_map/all_to_all | solution.py:504
  14.8 3.9 %filter_spectra.1.spec_ref = bf16[8,256,256]{2,1,0:T(8,128)(2,1)} custom-call(bf16[2048,128]{1,0:T(8,128)(2,1)} %bitcast.12, bf16[8,256,128]{2,1,0:T(8,128)(2,1)} %constant.6.clone.outer_ref, f32[2,128,128]{2,1,0:T(8,128)} %constant.7.clone.turn_ref, bf16[8,128,256]{2,1,0:T(8,128)(2,1)} %constant.8.clone.inner_ref), custom_call_target="tpu_custom_call" | custom-call | flops 1000000000 | bytes 4194304 | tf_op jit(solution)/shard_map/filter_spectra/pallas_call | solution.py:287
  18.7 0.0 copy-start.2
  18.7 0.0 copy-start.3
  18.7 0.0 copy-start.4
  18.8 0.0 copy-start.5
  18.8 3.8 %direct.1 = (f32[256,1024]{1,0:T(8,128)}, f32[256,1024]{1,0:T(8,128)}) custom-call(bf16[256,1024]{1,0:T(8,128)(2,1)} %q_ref.2, bf16[256,1024]{1,0:T(8,128)(2,1)} %k_ref.2, bf16[256,1024]{1,0:T(8,128)(2,1)} %v_ref.2, f32[3,3,256]{2,1,0:T(4,128)} %taps_ref.3, f32[1,256]{1,0:T(1,128)} %bitcast.11), custom_call_target="tpu_custom_call" | custom-call | flops 1000000000 | bytes 4194304 | tf_op jit(solution)/shard_map/direct/pallas_call | solution.py:346
  22.5 5.5 %all-to-all-done = bf16[128,9,2,128]{3,2,1,0:T(2,128)(2,1)S(1)} async-done(((bf16[128,9,2,128]{3,2,1,0:T(2,128)(2,1)}), bf16[128,9,2,128]{3,2,1,0:T(2,128)(2,1)S(1)}, u32[]{:S(2)}, u32[]{:S(2)}) %all-to-all-start) | async-done | bytes 589856 | tf_op jit(solution)/shard_map/all_to_all | solution.py:504
  28.1 0.0 copy-done.2
  28.1 0.0 copy-done.3
  28.1 0.0 copy-done.4
  28.1 0.0 copy-done.5
  28.1 0.0 copy-start.1
  28.1 2.6 %conv.1 = bf16[128,16,128]{2,1,0:T(8,128)(2,1)S(1)} custom-call(bf16[2304,128]{1,0:T(8,128)(2,1)S(1)} %bitcast.8, bf16[8,256,256]{2,1,0:T(8,128)(2,1)S(1)} %copy-done.5, bf16[8,256,128]{2,1,0:T(8,128)(2,1)S(1)} %copy-done.3, f32[2,128,128]{2,1,0:T(8,128)S(1)} %copy-done.4, bf16[8,128,256]{2,1,0:T(8,128)(2,1)S(1)} %copy-done.2), custom_call_target="tpu_custom_call" | custom-call | flops 1000000000 | bytes 8388608 | tf_op jit(solution)/shard_map/conv/pallas_call | solution.py:441
  30.7 0.0 copy-start
  30.7 17.6 %all_to_all.10.returned_ref = bf16[128,16,128]{2,1,0:T(8,128)(2,1)S(1)} all-to-all(bf16[128,16,128]{2,1,0:T(8,128)(2,1)S(1)} %conv.1), channel_id=1, replica_groups={{9,25,41,57,73,89,105,121,1,17,33,49,65,81,97,113,13,29,45,61,77,93,109..., dimensions={0} | all-to-all | bytes 1048576 | tf_op jit(solution)/shard_map/all_to_all | solution.py:504
  48.4 0.0 copy-done.1
  48.4 0.0 copy-done
  48.4 1.1 %final.1 = bf16[256,1024]{1,0:T(8,128)(2,1)} custom-call(bf16[128,16,128]{2,1,0:T(8,128)(2,1)S(1)} %all_to_all.10.returned_ref, f32[256,1024]{1,0:T(8,128)S(1)} %copy-done, f32[256,1024]{1,0:T(8,128)S(1)} %copy-done.1), custom_call_target="tpu_custom_call" | custom-call | flops 1000000 | bytes 2097152 | tf_op jit(solution)/shard_map/final/pallas_call | solution.py:485
Async XLA Ops:
  3.3 24.8 %all-to-all-start = ((bf16[128,9,2,128]{3,2,1,0:T(2,128)(2,1)}), bf16[128,9,2,128]{3,2,1,0:T(2,128)(2,1)S(1)}, u32[]{:S(2)}, u32[]{:S(2)}) async-start(bf16[128,9,2,128]{3,2,1,0:T(2,128)(2,1)} %bitcast.9), calls=%async_computation | async-start | bytes 1179648 | tf_op jit(solution)/shard_map/all_to_all | solution.py:504
  18.7 9.4 %copy-start.2 = (bf16[8,128,256]{2,1,0:T(8,128)(2,1)S(1)}, bf16[8,128,256]{2,1,0:T(8,128)(2,1)}, u32[]{:S(2)}) copy-start(bf16[8,128,256]{2,1,0:T(8,128)(2,1)} %constant.8.clone.inner_ref) | copy-start | bytes 1572868
  18.7 9.4 %copy-start.3 = (bf16[8,256,128]{2,1,0:T(8,128)(2,1)S(1)}, bf16[8,256,128]{2,1,0:T(8,128)(2,1)}, u32[]{:S(2)}) copy-start(bf16[8,256,128]{2,1,0:T(8,128)(2,1)} %constant.6.clone.outer_ref) | copy-start | bytes 1572868
  18.7 9.3 %copy-start.4 = (f32[2,128,128]{2,1,0:T(8,128)S(1)}, f32[2,128,128]{2,1,0:T(8,128)}, u32[]{:S(2)}) copy-start(f32[2,128,128]{2,1,0:T(8,128)} %constant.7.clone.turn_ref) | copy-start | bytes 393220
  18.8 9.3 %copy-start.5 = (bf16[8,256,256]{2,1,0:T(8,128)(2,1)S(1)}, bf16[8,256,256]{2,1,0:T(8,128)(2,1)}, u32[]{:S(2)}) copy-start(bf16[8,256,256]{2,1,0:T(8,128)(2,1)} %filter_spectra.1.spec_ref) | copy-start | bytes 3145732
  28.1 20.3 %copy-start.1 = (f32[256,1024]{1,0:T(8,128)S(1)}, f32[256,1024]{1,0:T(8,128)}, u32[]{:S(2)}) copy-start(f32[256,1024]{1,0:T(8,128)} %get-tuple-element.32.direct_ref) | copy-start | bytes 3145732
  30.7 17.7 %copy-start = (f32[256,1024]{1,0:T(8,128)S(1)}, f32[256,1024]{1,0:T(8,128)}, u32[]{:S(2)}) copy-start(f32[256,1024]{1,0:T(8,128)} %get-tuple-element.31.query_ref) | copy-start | bytes 3145732

commit v9 on v8

--- a/solution.py
+++ b/solution.py
@@ -151,8 +151,9 @@
 
     first, last = small_copies()[:2], small_copies()[2:]
     copies = first + [
-        pltpu.make_async_copy(k_ref, k_buf, sems.at[0]),
-        pltpu.make_async_copy(v_ref, v_buf, sems.at[1]),
+        pltpu.make_async_copy(ref.at[pl.ds(p * 128, 128)], buf.at[pl.ds(p * 128, 128)], sems.at[i, p])
+        for i, (ref, buf) in enumerate(((k_ref, k_buf), (v_ref, v_buf)))
+        for p in range(2)
     ]
     copies += last
     for copy in copies:
@@ -193,7 +194,7 @@
             pltpu.VMEM((LANES, CHANNELS), F32),
             pltpu.VMEM((CHANNELS * WIDTH, LANES), F32),
             pltpu.SemaphoreType.DMA((4,)),
-            pltpu.SemaphoreType.DMA((2,)),
+            pltpu.SemaphoreType.DMA((2, 2)),
         ],
         [HBM] * 5,
         VMEM,

time: 49.7 us -> 49.7 us (level)
  no operation moved by 1% of the time
where the time goes in v9:
time: 49.7 us; the launch traced here: 49.4 us
  blocking collectives  17.6 us (35%)
  Pallas kernels  14.7 us (30%)
  starting transfers between devices  11.5 us (23%)
  waiting for transfers between devices  5.54 us (11%)
    all_to_all x1, blocking collectives, exchange(): lax.all_to_all(messages, AXES, split_axis=0, concat_axis=0, axis_index_gr...  17.6 us
    all_to_all x1, starting transfers between devices, exchange(): lax.all_to_all(messages, AXES, split_axis=0, concat_axis=0, axis_index_gr...  11.5 us
    all_to_all x1, waiting for transfers between devices, exchange(): lax.all_to_all(messages, AXES, split_axis=0, concat_axis=0, axis_index_gr...  5.54 us
    pallas_call x1, Pallas kernels, filter_spectra(): call(filter_body, 'filter_spectra', shape(spec, BF16), [pltpu.VMEM(spec,...  3.92 us
    pallas_call x1, Pallas kernels, direct(): call(direct_body, 'direct', (shape((CHANNELS, TOKENS), F32), shape((CHANN...  3.76 us
    pallas_call x1, Pallas kernels, gate(): call(gate_body, 'gate', shape((CHANNELS * WIDTH, LANES), BF16), [pltpu.VM...  3.27 us
    pallas_call x1, Pallas kernels, conv(): call(conv_body, 'conv', shape((BLOCKS, BODY, LANES), BF16), [pltpu.VMEM((...  2.63 us
    pallas_call x1, Pallas kernels, final(): call(final_body, 'final', shape((CHANNELS, TOKENS), BF16), [pltpu.VMEM((R...  1.06 us
  transfers between devices with their start and end apart: 1, of which 1 were waited for; matrix products, arithmetic and copies ran while one was open for 0% of the time, Pallas kernels for 16%

profile of v9, /device:TPU:1, one launch (start us, length us, event | category | flops | bytes accessed | tf_op | source)
XLA Modules:
  0.0 49.4 jit_solution(16879394309305095532)
XLA Ops:
  0.0 3.3 %gate.1 = bf16[2304,128]{1,0:T(8,128)(2,1)} custom-call(bf16[256,1024]{1,0:T(8,128)(2,1)} %q_ref.2, bf16[256,1024]{1,0:T(8,128)(2,1)} %k_ref.2, bf16[256,1024]{1,0:T(8,128)(2,1)} %v_ref.2, f32[3,3,256]{2,1,0:T(4,128)} %taps_ref.3, f32[1,256]{1,0:T(1,128)} %bitcast.10), custom_call_target="tpu_custom_call" | custom-call | flops 10000000 | bytes 2097152 | tf_op jit(solution)/shard_map/gate/pallas_call | solution.py:184
  3.3 11.5 %all-to-all-start = ((bf16[128,9,2,128]{3,2,1,0:T(2,128)(2,1)}), bf16[128,9,2,128]{3,2,1,0:T(2,128)(2,1)S(1)}, u32[]{:S(2)}, u32[]{:S(2)}) async-start(bf16[128,9,2,128]{3,2,1,0:T(2,128)(2,1)} %bitcast.9), calls=%async_computation | async-start | bytes 1179648 | tf_op jit(solution)/shard_map/all_to_all | solution.py:505
  14.8 3.9 %filter_spectra.1.spec_ref = bf16[8,256,256]{2,1,0:T(8,128)(2,1)} custom-call(bf16[2048,128]{1,0:T(8,128)(2,1)} %bitcast.12, bf16[8,256,128]{2,1,0:T(8,128)(2,1)} %constant.6.clone.outer_ref, f32[2,128,128]{2,1,0:T(8,128)} %constant.7.clone.turn_ref, bf16[8,128,256]{2,1,0:T(8,128)(2,1)} %constant.8.clone.inner_ref), custom_call_target="tpu_custom_call" | custom-call | flops 1000000000 | bytes 4194304 | tf_op jit(solution)/shard_map/filter_spectra/pallas_call | solution.py:288
  18.7 0.0 copy-start.2
  18.7 0.0 copy-start.3
  18.7 0.0 copy-start.4
  18.8 0.0 copy-start.5
  18.8 3.8 %direct.1 = (f32[256,1024]{1,0:T(8,128)}, f32[256,1024]{1,0:T(8,128)}) custom-call(bf16[256,1024]{1,0:T(8,128)(2,1)} %q_ref.2, bf16[256,1024]{1,0:T(8,128)(2,1)} %k_ref.2, bf16[256,1024]{1,0:T(8,128)(2,1)} %v_ref.2, f32[3,3,256]{2,1,0:T(4,128)} %taps_ref.3, f32[1,256]{1,0:T(1,128)} %bitcast.11), custom_call_target="tpu_custom_call" | custom-call | flops 1000000000 | bytes 4194304 | tf_op jit(solution)/shard_map/direct/pallas_call | solution.py:347
  22.5 5.5 %all-to-all-done = bf16[128,9,2,128]{3,2,1,0:T(2,128)(2,1)S(1)} async-done(((bf16[128,9,2,128]{3,2,1,0:T(2,128)(2,1)}), bf16[128,9,2,128]{3,2,1,0:T(2,128)(2,1)S(1)}, u32[]{:S(2)}, u32[]{:S(2)}) %all-to-all-start) | async-done | bytes 589856 | tf_op jit(solution)/shard_map/all_to_all | solution.py:505
  28.1 0.0 copy-done.2
  28.1 0.0 copy-done.3
  28.1 0.0 copy-done.4
  28.1 0.0 copy-done.5
  28.1 0.0 copy-start.1
  28.1 2.6 %conv.1 = bf16[128,16,128]{2,1,0:T(8,128)(2,1)S(1)} custom-call(bf16[2304,128]{1,0:T(8,128)(2,1)S(1)} %bitcast.8, bf16[8,256,256]{2,1,0:T(8,128)(2,1)S(1)} %copy-done.5, bf16[8,256,128]{2,1,0:T(8,128)(2,1)S(1)} %copy-done.3, f32[2,128,128]{2,1,0:T(8,128)S(1)} %copy-done.4, bf16[8,128,256]{2,1,0:T(8,128)(2,1)S(1)} %copy-done.2), custom_call_target="tpu_custom_call" | custom-call | flops 1000000000 | bytes 8388608 | tf_op jit(solution)/shard_map/conv/pallas_call | solution.py:442
  30.7 0.0 copy-start
  30.8 17.6 %all_to_all.10.returned_ref = bf16[128,16,128]{2,1,0:T(8,128)(2,1)S(1)} all-to-all(bf16[128,16,128]{2,1,0:T(8,128)(2,1)S(1)} %conv.1), channel_id=1, replica_groups={{9,25,41,57,73,89,105,121,1,17,33,49,65,81,97,113,13,29,45,61,77,93,109..., dimensions={0} | all-to-all | bytes 1048576 | tf_op jit(solution)/shard_map/all_to_all | solution.py:505
  48.4 0.0 copy-done.1
  48.4 0.0 copy-done
  48.4 1.1 %final.1 = bf16[256,1024]{1,0:T(8,128)(2,1)} custom-call(bf16[128,16,128]{2,1,0:T(8,128)(2,1)S(1)} %all_to_all.10.returned_ref, f32[256,1024]{1,0:T(8,128)S(1)} %copy-done, f32[256,1024]{1,0:T(8,128)S(1)} %copy-done.1), custom_call_target="tpu_custom_call" | custom-call | flops 1000000 | bytes 2097152 | tf_op jit(solution)/shard_map/final/pallas_call | solution.py:486
Async XLA Ops:
  3.3 24.8 %all-to-all-start = ((bf16[128,9,2,128]{3,2,1,0:T(2,128)(2,1)}), bf16[128,9,2,128]{3,2,1,0:T(2,128)(2,1)S(1)}, u32[]{:S(2)}, u32[]{:S(2)}) async-start(bf16[128,9,2,128]{3,2,1,0:T(2,128)(2,1)} %bitcast.9), calls=%async_computation | async-start | bytes 1179648 | tf_op jit(solution)/shard_map/all_to_all | solution.py:505
  18.7 9.4 %copy-start.2 = (bf16[8,128,256]{2,1,0:T(8,128)(2,1)S(1)}, bf16[8,128,256]{2,1,0:T(8,128)(2,1)}, u32[]{:S(2)}) copy-start(bf16[8,128,256]{2,1,0:T(8,128)(2,1)} %constant.8.clone.inner_ref) | copy-start | bytes 1572868
  18.7 9.4 %copy-start.3 = (bf16[8,256,128]{2,1,0:T(8,128)(2,1)S(1)}, bf16[8,256,128]{2,1,0:T(8,128)(2,1)}, u32[]{:S(2)}) copy-start(bf16[8,256,128]{2,1,0:T(8,128)(2,1)} %constant.6.clone.outer_ref) | copy-start | bytes 1572868
  18.7 9.3 %copy-start.4 = (f32[2,128,128]{2,1,0:T(8,128)S(1)}, f32[2,128,128]{2,1,0:T(8,128)}, u32[]{:S(2)}) copy-start(f32[2,128,128]{2,1,0:T(8,128)} %constant.7.clone.turn_ref) | copy-start | bytes 393220
  18.8 9.3 %copy-start.5 = (bf16[8,256,256]{2,1,0:T(8,128)(2,1)S(1)}, bf16[8,256,256]{2,1,0:T(8,128)(2,1)}, u32[]{:S(2)}) copy-start(bf16[8,256,256]{2,1,0:T(8,128)(2,1)} %filter_spectra.1.spec_ref) | copy-start | bytes 3145732
  28.1 20.3 %copy-start.1 = (f32[256,1024]{1,0:T(8,128)S(1)}, f32[256,1024]{1,0:T(8,128)}, u32[]{:S(2)}) copy-start(f32[256,1024]{1,0:T(8,128)} %get-tuple-element.32.direct_ref) | copy-start | bytes 3145732
  30.7 17.6 %copy-start = (f32[256,1024]{1,0:T(8,128)S(1)}, f32[256,1024]{1,0:T(8,128)}, u32[]{:S(2)}) copy-start(f32[256,1024]{1,0:T(8,128)} %get-tuple-element.31.query_ref) | copy-start | bytes 3145732
